TPU v7x, 32 devices: a whole 2x2x4 slice. The times are simulated.
32 devices in a mesh: rep: 8 (over z, y), grp: 4 (over x, core).
Axes of the slice: x: 2, y: 2, z: 4, core: 2. Of those that a mesh axis runs over, the one named last changes fastest.
Arguments:
- tokens: bfloat16 [16, 580, 1024], P('rep', 'grp'), may hold values from -6 to 6
- cotangent: bfloat16 [16, 580, 1024], P('rep', 'grp'), may hold values from -6 to 6
- image_valid: int32 [16], P('rep'), may hold values 0 or 1
- token_valid: int32 [16, 580], P('rep'), may hold values from 0 to 1, as said below
- norm1_gain: bfloat16 [2, 1024], P(None, 'grp'), may hold values from 0.5 to 1.5
- norm1_bias: bfloat16 [2, 1024], P(None, 'grp'), may hold values from -2 to 2
- w_qkv: bfloat16 [2, 1024, 3072], P(None, 'grp'), may hold values from -0.1875 to 0.1875
- b_qv: bfloat16 [2, 2048], P(None, 'grp'), may hold values from -2 to 2
- w_out: bfloat16 [2, 1024, 1024], P(None, 'grp'), may hold values from -0.5 to 0.5
- b_out: bfloat16 [2, 1024], P(None, 'grp'), may hold values from -2 to 2
- norm2_gain: bfloat16 [2, 1024], P(None, 'grp'), may hold values from 0.5 to 1.5
- norm2_bias: bfloat16 [2, 1024], P(None, 'grp'), may hold values from -2 to 2
- w_up: bfloat16 [2, 1024, 4096], P(None, 'grp'), may hold values from -0.1875 to 0.1875
- b_up: bfloat16 [2, 4096], P(None, 'grp'), may hold values from -2 to 2
- w_down: bfloat16 [2, 4096, 1024], P(None, 'grp'), may hold values from -0.09375 to 0.09375
- b_down: bfloat16 [2, 1024], P(None, 'grp'), may hold values from -2 to 2
Outputs:
- activations: bfloat16 [16, 580, 1024], P('rep', 'grp')
- grad_tokens: bfloat16 [16, 580, 1024], P('rep', 'grp')
- grad_norm1_gain: float32 [2, 1024], P(None, 'grp')
- grad_norm1_bias: float32 [2, 1024], P(None, 'grp')
- grad_w_qkv: float32 [2, 1024, 3072], P(None, 'grp')
- grad_b_qv: float32 [2, 2048], P(None, 'grp')
- grad_w_out: float32 [2, 1024, 1024], P(None, 'grp')
- grad_b_out: float32 [2, 1024], P(None, 'grp')
- grad_norm2_gain: float32 [2, 1024], P(None, 'grp')
- grad_norm2_bias: float32 [2, 1024], P(None, 'grp')
- grad_w_up: float32 [2, 1024, 4096], P(None, 'grp')
- grad_b_up: float32 [2, 4096], P(None, 'grp')
- grad_w_down: float32 [2, 4096, 1024], P(None, 'grp')
- grad_b_down: float32 [2, 1024], P(None, 'grp')
Inputs may be any that keep to these rules, and one draw needn't show every extreme that they name: `token_valid`: each row is 1 on a prefix of 508 slots or more and 0 after it.
All inputs are finite; a program needn't handle non-finite values. No bound on the sum of `image_valid` on one device may be relied on, other than what follows from the above.
Results may differ from a plain program's by a relative error of at most 0.017.
Values may be sent and summed in bfloat16 or wider, within the bound.
A program may use at most 320 MiB of HBM per device.

v0:
```python
import jax
import jax.numpy as jnp
from jax import lax
from jax.sharding import PartitionSpec as P

HEAD = 64
LAYERS = 2
MICRO = 2


def normalize(values, gain_vec, shift_vec):
    centre = jnp.mean(values, axis=-1, keepdims=True)
    spread = jnp.mean(jnp.square(values - centre), axis=-1, keepdims=True)
    return (values - centre) * lax.rsqrt(spread + 1e-06) * gain_vec + shift_vec


def exact_gelu(v):
    return jax.nn.gelu(v, approximate=False)


def attention_scores(query_heads, key_heads, key_mask):
    scores = jnp.einsum(
        "bqhd,bkhd->bhqk", query_heads, key_heads, preferred_element_type=jnp.float32
    ) * HEAD ** (-0.5)
    return jnp.where(key_mask[:, None, None, :], scores, -1000000000.0)


def layer_slice(stacked, layer_index):
    return tuple((w[layer_index] for w in stacked))


def forward_block(hidden, gathered, key_mask):
    (
        gain_one,
        shift_one,
        w_joined,
        b_joined,
        w_proj,
        b_proj,
        gain_two,
        shift_two,
        w_in,
        b_in,
        w_back,
        b_back,
    ) = gathered
    images_mb, row_count, model_width = hidden.shape
    head_count = model_width // HEAD
    flat_rows = hidden.reshape(images_mb * row_count, model_width)
    normed = normalize(
        flat_rows, gain_one.astype(jnp.float32), shift_one.astype(jnp.float32)
    ).astype(jnp.bfloat16)
    joined = jnp.dot(normed, w_joined, preferred_element_type=jnp.float32)
    queries = (joined[:, :model_width] + b_joined[:model_width].astype(jnp.float32)).astype(
        jnp.bfloat16
    )
    key_rows = joined[:, model_width : 2 * model_width].astype(jnp.bfloat16)
    values = (joined[:, 2 * model_width :] + b_joined[model_width:].astype(jnp.float32)).astype(
        jnp.bfloat16
    )
    all_keys, all_values = (
        lax.all_gather(
            key_rows.reshape(images_mb, row_count, model_width), "grp", axis=1, tiled=True
        ),
        lax.all_gather(
            values.reshape(images_mb, row_count, model_width), "grp", axis=1, tiled=True
        ),
    )
    query_heads = queries.reshape(images_mb, row_count, head_count, HEAD)
    key_heads = all_keys.reshape(images_mb, -1, head_count, HEAD)
    value_heads = all_values.reshape(images_mb, -1, head_count, HEAD)
    scores = attention_scores(query_heads, key_heads, key_mask)
    row_max = jnp.max(scores, axis=-1, keepdims=True)
    exp_terms = jnp.exp(scores - row_max)
    exp_total = jnp.sum(exp_terms, axis=-1, keepdims=True)
    softmax_out = exp_terms / exp_total
    log_total = row_max[..., 0] + jnp.log(exp_total[..., 0])
    attended = jnp.einsum(
        "bhqk,bkhd->bqhd",
        softmax_out.astype(jnp.bfloat16),
        value_heads,
        preferred_element_type=jnp.float32,
    )
    attended = attended.reshape(images_mb * row_count, model_width).astype(jnp.bfloat16)
    middle = flat_rows + (
        jnp.dot(attended, w_proj, preferred_element_type=jnp.float32) + b_proj.astype(jnp.float32)
    )
    normed_two = normalize(
        middle, gain_two.astype(jnp.float32), shift_two.astype(jnp.float32)
    ).astype(jnp.bfloat16)
    pre_active = jnp.dot(normed_two, w_in, preferred_element_type=jnp.float32) + b_in.astype(
        jnp.float32
    )
    active = exact_gelu(pre_active).astype(jnp.bfloat16)
    result = middle + (
        jnp.dot(active, w_back, preferred_element_type=jnp.float32) + b_back.astype(jnp.float32)
    )
    stored = (
        flat_rows,
        normed,
        query_heads,
        key_heads,
        value_heads,
        log_total,
        attended,
        middle,
        normed_two,
        pre_active,
        active,
    )
    return (result.reshape(images_mb, row_count, model_width), stored)


def backward_block(grad_flow, gathered, stored, key_mask):
    (
        gain_one,
        shift_one,
        w_joined,
        b_joined,
        w_proj,
        b_proj,
        gain_two,
        shift_two,
        w_in,
        b_in,
        w_back,
        b_back,
    ) = gathered
    (
        flat_rows,
        normed,
        query_heads,
        key_heads,
        value_heads,
        log_total,
        attended,
        middle,
        normed_two,
        pre_active,
        active,
    ) = stored
    images_mb, row_count, model_width = grad_flow.shape
    head_count = model_width // HEAD
    total_rows = images_mb * row_count
    flat_grad = grad_flow.reshape(total_rows, model_width)
    down_in = flat_grad.astype(jnp.bfloat16)
    grad_b_back = jnp.sum(down_in, axis=0, dtype=jnp.float32)
    grad_w_back = jnp.einsum("rf,rd->fd", active, down_in, preferred_element_type=jnp.float32)
    grad_active = jnp.einsum("rd,fd->rf", down_in, w_back, preferred_element_type=jnp.float32)
    unused_value, gelu_pull = jax.vjp(exact_gelu, pre_active)
    up_in = gelu_pull(grad_active)[0].astype(jnp.bfloat16)
    grad_b_in = jnp.sum(up_in, axis=0, dtype=jnp.float32)
    grad_w_in = jnp.einsum("rd,rf->df", normed_two, up_in, preferred_element_type=jnp.float32)
    grad_normed_two = jnp.einsum("rf,df->rd", up_in, w_in, preferred_element_type=jnp.float32)
    unused_norm, norm_pull = jax.vjp(
        normalize, middle, gain_two.astype(jnp.float32), shift_two.astype(jnp.float32)
    )
    grad_mid_norm, grad_gain_two, grad_shift_two = norm_pull(grad_normed_two)
    grad_middle = flat_grad + grad_mid_norm
    proj_in = grad_middle.astype(jnp.bfloat16)
    grad_b_proj = jnp.sum(proj_in, axis=0, dtype=jnp.float32)
    grad_w_proj = jnp.einsum("rd,re->de", attended, proj_in, preferred_element_type=jnp.float32)
    grad_attended = jnp.einsum("re,de->rd", proj_in, w_proj, preferred_element_type=jnp.float32)
    grad_attended = grad_attended.astype(jnp.bfloat16).reshape(
        images_mb, row_count, head_count, HEAD
    )
    scores = attention_scores(query_heads, key_heads, key_mask)
    softmax_out = jnp.exp(scores - log_total[..., None])
    grad_values_part = jnp.einsum(
        "bhqk,bqhd->bkhd",
        softmax_out.astype(jnp.bfloat16),
        grad_attended,
        preferred_element_type=jnp.float32,
    )
    grad_soft = jnp.einsum(
        "bqhd,bkhd->bhqk", grad_attended, value_heads, preferred_element_type=jnp.float32
    )
    grad_scores = softmax_out * (
        grad_soft - jnp.sum(grad_soft * softmax_out, axis=-1, keepdims=True)
    )
    score_in = grad_scores.astype(jnp.bfloat16)
    grad_queries = jnp.einsum(
        "bhqk,bkhd->bqhd", score_in, key_heads, preferred_element_type=jnp.float32
    ) * HEAD ** (-0.5)
    grad_keys_part = jnp.einsum(
        "bhqk,bqhd->bkhd", score_in, query_heads, preferred_element_type=jnp.float32
    ) * HEAD ** (-0.5)
    seq_slots = key_heads.shape[1]
    grad_key_rows, grad_value_rows = (
        lax.psum_scatter(
            grad_keys_part.reshape(images_mb, seq_slots, model_width).astype(jnp.bfloat16),
            "grp",
            scatter_dimension=1,
            tiled=True,
        ).astype(jnp.float32),
        lax.psum_scatter(
            grad_values_part.reshape(images_mb, seq_slots, model_width).astype(jnp.bfloat16),
            "grp",
            scatter_dimension=1,
            tiled=True,
        ).astype(jnp.float32),
    )
    query_in = grad_queries.reshape(total_rows, model_width).astype(jnp.bfloat16)
    key_in = grad_key_rows.reshape(total_rows, model_width).astype(jnp.bfloat16)
    value_in = grad_value_rows.reshape(total_rows, model_width).astype(jnp.bfloat16)
    joined_grad = jnp.concatenate([query_in, key_in, value_in], axis=1)
    grad_b_joined = jnp.concatenate(
        [jnp.sum(query_in, axis=0, dtype=jnp.float32), jnp.sum(value_in, axis=0, dtype=jnp.float32)]
    )
    grad_w_joined = jnp.einsum("rd,re->de", normed, joined_grad, preferred_element_type=jnp.float32)
    grad_normed = jnp.einsum("re,de->rd", joined_grad, w_joined, preferred_element_type=jnp.float32)
    unused_first, first_pull = jax.vjp(
        normalize, flat_rows, gain_one.astype(jnp.float32), shift_one.astype(jnp.float32)
    )
    grad_in_norm, grad_gain_one, grad_shift_one = first_pull(grad_normed)
    grad_input = grad_middle + grad_in_norm
    terms = (
        grad_gain_one,
        grad_shift_one,
        grad_w_joined,
        grad_b_joined,
        grad_w_proj,
        grad_b_proj,
        grad_gain_two,
        grad_shift_two,
        grad_w_in,
        grad_b_in,
        grad_w_back,
        grad_b_back,
    )
    return (grad_input.reshape(images_mb, row_count, model_width), terms)


def local(
    tokens,
    cotangent,
    image_valid,
    token_valid,
    norm1_gain,
    norm1_bias,
    w_qkv,
    b_qv,
    w_out,
    b_out,
    norm2_gain,
    norm2_bias,
    w_up,
    b_up,
    w_down,
    b_down,
):
    stacked = (
        norm1_gain,
        norm1_bias,
        w_qkv,
        b_qv,
        w_out,
        b_out,
        norm2_gain,
        norm2_bias,
        w_up,
        b_up,
        w_down,
        b_down,
    )
    row_count = tokens.shape[1]
    images_mb = tokens.shape[0] // MICRO
    first_row = lax.axis_index("grp") * row_count
    totals = [
        [jnp.zeros(w.shape[1:], jnp.float32) for w in stacked] for layer_index in range(LAYERS)
    ]
    outputs = []
    grads_in = []
    for micro_index in range(MICRO):
        picked = slice(micro_index * images_mb, (micro_index + 1) * images_mb)
        hidden = tokens[picked].astype(jnp.float32)
        flags = token_valid[picked]
        key_mask = flags > 0
        own_flags = lax.dynamic_slice_in_dim(flags, first_row, row_count, 1)
        row_weight = (image_valid[picked][:, None] * own_flags).astype(jnp.float32)
        grad_flow = cotangent[picked].astype(jnp.float32) * row_weight[:, :, None]
        saved = []
        for layer_index in range(LAYERS):
            pieces = layer_slice(stacked, layer_index)
            gathered = (
                lax.all_gather(pieces[0], "grp", axis=0, tiled=True),
                lax.all_gather(pieces[1], "grp", axis=0, tiled=True),
                lax.all_gather(pieces[2], "grp", axis=0, tiled=True),
                lax.all_gather(pieces[3], "grp", axis=0, tiled=True),
                lax.all_gather(pieces[4], "grp", axis=0, tiled=True),
                lax.all_gather(pieces[5], "grp", axis=0, tiled=True),
                lax.all_gather(pieces[6], "grp", axis=0, tiled=True),
                lax.all_gather(pieces[7], "grp", axis=0, tiled=True),
                lax.all_gather(pieces[8], "grp", axis=0, tiled=True),
                lax.all_gather(pieces[9], "grp", axis=0, tiled=True),
                lax.all_gather(pieces[10], "grp", axis=0, tiled=True),
                lax.all_gather(pieces[11], "grp", axis=0, tiled=True),
            )
            hidden, stored = forward_block(hidden, gathered, key_mask)
            saved.append((None, stored))
        outputs.append(hidden.astype(jnp.bfloat16))
        for layer_index in reversed(range(LAYERS)):
            gathered, stored = saved[layer_index]
            pieces = layer_slice(stacked, layer_index)
            gathered = (
                lax.all_gather(pieces[0], "grp", axis=0, tiled=True),
                lax.all_gather(pieces[1], "grp", axis=0, tiled=True),
                lax.all_gather(pieces[2], "grp", axis=0, tiled=True),
                lax.all_gather(pieces[3], "grp", axis=0, tiled=True),
                lax.all_gather(pieces[4], "grp", axis=0, tiled=True),
                lax.all_gather(pieces[5], "grp", axis=0, tiled=True),
                lax.all_gather(pieces[6], "grp", axis=0, tiled=True),
                lax.all_gather(pieces[7], "grp", axis=0, tiled=True),
                lax.all_gather(pieces[8], "grp", axis=0, tiled=True),
                lax.all_gather(pieces[9], "grp", axis=0, tiled=True),
                lax.all_gather(pieces[10], "grp", axis=0, tiled=True),
                lax.all_gather(pieces[11], "grp", axis=0, tiled=True),
            )
            grad_flow, terms = backward_block(grad_flow, gathered, stored, key_mask)
            shares = (
                lax.psum_scatter(
                    terms[0].astype(jnp.bfloat16), "grp", scatter_dimension=0, tiled=True
                ).astype(jnp.float32),
                lax.psum_scatter(
                    terms[1].astype(jnp.bfloat16), "grp", scatter_dimension=0, tiled=True
                ).astype(jnp.float32),
                lax.psum_scatter(
                    terms[2].astype(jnp.bfloat16), "grp", scatter_dimension=0, tiled=True
                ).astype(jnp.float32),
                lax.psum_scatter(
                    terms[3].astype(jnp.bfloat16), "grp", scatter_dimension=0, tiled=True
                ).astype(jnp.float32),
                lax.psum_scatter(
                    terms[4].astype(jnp.bfloat16), "grp", scatter_dimension=0, tiled=True
                ).astype(jnp.float32),
                lax.psum_scatter(
                    terms[5].astype(jnp.bfloat16), "grp", scatter_dimension=0, tiled=True
                ).astype(jnp.float32),
                lax.psum_scatter(
                    terms[6].astype(jnp.bfloat16), "grp", scatter_dimension=0, tiled=True
                ).astype(jnp.float32),
                lax.psum_scatter(
                    terms[7].astype(jnp.bfloat16), "grp", scatter_dimension=0, tiled=True
                ).astype(jnp.float32),
                lax.psum_scatter(
                    terms[8].astype(jnp.bfloat16), "grp", scatter_dimension=0, tiled=True
                ).astype(jnp.float32),
                lax.psum_scatter(
                    terms[9].astype(jnp.bfloat16), "grp", scatter_dimension=0, tiled=True
                ).astype(jnp.float32),
                lax.psum_scatter(
                    terms[10].astype(jnp.bfloat16), "grp", scatter_dimension=0, tiled=True
                ).astype(jnp.float32),
                lax.psum_scatter(
                    terms[11].astype(jnp.bfloat16), "grp", scatter_dimension=0, tiled=True
                ).astype(jnp.float32),
            )
            totals[layer_index] = [left + right for left, right in zip(totals[layer_index], shares)]
        grads_in.append(grad_flow.astype(jnp.bfloat16))
    merged = [
        jnp.stack([totals[layer_index][member] for layer_index in range(LAYERS)])
        for member in range(12)
    ]
    summed = (
        lax.psum(merged[0].astype(jnp.bfloat16), "rep").astype(jnp.float32),
        lax.psum(merged[1].astype(jnp.bfloat16), "rep").astype(jnp.float32),
        lax.psum(merged[2].astype(jnp.bfloat16), "rep").astype(jnp.float32),
        lax.psum(merged[3].astype(jnp.bfloat16), "rep").astype(jnp.float32),
        lax.psum(merged[4].astype(jnp.bfloat16), "rep").astype(jnp.float32),
        lax.psum(merged[5].astype(jnp.bfloat16), "rep").astype(jnp.float32),
        lax.psum(merged[6].astype(jnp.bfloat16), "rep").astype(jnp.float32),
        lax.psum(merged[7].astype(jnp.bfloat16), "rep").astype(jnp.float32),
        lax.psum(merged[8].astype(jnp.bfloat16), "rep").astype(jnp.float32),
        lax.psum(merged[9].astype(jnp.bfloat16), "rep").astype(jnp.float32),
        lax.psum(merged[10].astype(jnp.bfloat16), "rep").astype(jnp.float32),
        lax.psum(merged[11].astype(jnp.bfloat16), "rep").astype(jnp.float32),
    )
    return (jnp.concatenate(outputs, axis=0), jnp.concatenate(grads_in, axis=0)) + tuple(summed)


def solution(mesh):
    placed = (
        P("rep", "grp", None),
        P("rep", "grp", None),
        P("rep"),
        P("rep", None),
        P(None, "grp"),
        P(None, "grp"),
        P(None, "grp", None),
        P(None, "grp"),
        P(None, "grp", None),
        P(None, "grp"),
        P(None, "grp"),
        P(None, "grp"),
        P(None, "grp", None),
        P(None, "grp"),
        P(None, "grp", None),
        P(None, "grp"),
    )
    return jax.shard_map(
        local,
        mesh=mesh,
        in_specs=placed,
        out_specs=(
            P("rep", "grp", None),
            P("rep", "grp", None),
            P(None, "grp"),
            P(None, "grp"),
            P(None, "grp", None),
            P(None, "grp"),
            P(None, "grp", None),
            P(None, "grp"),
            P(None, "grp"),
            P(None, "grp"),
            P(None, "grp", None),
            P(None, "grp"),
            P(None, "grp", None),
            P(None, "grp"),
        ),
        check_vma=False,
    )
```

profile of v0, /device:TPU:0, one launch (start us, length us, event | category | flops | bytes accessed | tf_op | source)
XLA Modules:
  0.0 2372.0 jit_solution(806412783918876329)
XLA Ops:
  11.2 6.0 all-gather
  24.0 36.4 %all-gather.57.cloned.1.call-done = bf16[1,1024,3072]{2,1,0:T(8,128)(2,1)} async-done(((bf16[1,256,3072]{2,1,0:T(8,128)(2,1)}), bf16[1,1024,3072]{2,1,0:T(8,128)(2,1)}) %all-gather.57.cloned.1.call-update) | async-done | bytes 6291472 | tf_op jit(solution)/shard_map/all_gather | solution.py:288
  186.3 40.6 %all-gather.61.cloned.1.call-done = bf16[1,1024,4096]{2,1,0:T(8,128)(2,1)} async-done(((bf16[1,256,4096]{2,1,0:T(8,128)(2,1)}), bf16[1,1024,4096]{2,1,0:T(8,128)(2,1)}) %all-gather.61.cloned.1.call-update) | async-done | bytes 8388624 | tf_op jit(solution)/shard_map/all_gather | solution.py:294
  226.9 10.5 multiply_convert_fusion.11
  237.4 49.9 %all-gather.63.cloned.1.call-done = bf16[1,4096,1024]{2,1,0:T(8,128)(2,1)} async-done(((bf16[1,1024,1024]{2,1,0:T(8,128)(2,1)}), bf16[1,4096,1024]{2,1,0:T(8,128)(2,1)}) %all-gather.63.cloned.1.call-update) | async-done | bytes 8388624 | tf_op jit(solution)/shard_map/all_gather | solution.py:296
  292.9 42.4 %all-gather.65.cloned.1.call-done = bf16[1,1024,3072]{2,1,0:T(8,128)(2,1)} async-done(((bf16[1,256,3072]{2,1,0:T(8,128)(2,1)}), bf16[1,1024,3072]{2,1,0:T(8,128)(2,1)}) %all-gather.65.cloned.1.call-update) | async-done | bytes 6291472 | tf_op jit(solution)/shard_map/all_gather | solution.py:288
  341.5 10.5 multiply_convert_fusion.9
  433.7 9.0 all-gather.67.cloned.1.call-done
  452.8 50.2 %all-gather.69.cloned.1.call-done = bf16[1,1024,4096]{2,1,0:T(8,128)(2,1)} async-done(((bf16[1,256,4096]{2,1,0:T(8,128)(2,1)}), bf16[1,1024,4096]{2,1,0:T(8,128)(2,1)}) %all-gather.69.cloned.1.call-update) | async-done | bytes 8388624 | tf_op jit(solution)/shard_map/all_gather | solution.py:294
  503.0 10.8 multiply_convert_fusion.10
  513.8 8.4 multiply_convert_fusion.8
  522.2 40.5 %all-gather.71.cloned.1.call-done = bf16[1,4096,1024]{2,1,0:T(8,128)(2,1)} async-done(((bf16[1,1024,1024]{2,1,0:T(8,128)(2,1)}), bf16[1,4096,1024]{2,1,0:T(8,128)(2,1)}) %all-gather.71.cloned.1.call-update) | async-done | bytes 8388624 | tf_op jit(solution)/shard_map/all_gather | solution.py:296
  562.8 11.6 fusion.348
  578.2 9.3 fusion.349
  598.2 8.2 multiply_reduce_fusion.3
  638.5 95.4 %all-reduce.56.cloned.1.call-done = (bf16[1,580,1024]{1,2,0:T(8,128)(2,1)}, bf16[1,580,1024]{1,2,0:T(8,128)(2,1)}, bf16[1,580,1024]{1,2,0:T(8,128)(2,1)}, bf16[1,580,1024]{1,2,0:T(8,128)(2,1)}) async-done(((bf16[1,580,1024]{1,2,0:T(8,128)(2,1)}, bf16[1,580,1024]{1,2,0:T(8,128)(2,1)}, bf16[1,580,1024]{1,2,0:T(8,128)(2,1)}, bf16[1,580,1024]{1,2,0:T(8,128)(2,1)}), (bf16[1,580,1024]{1,2,0:T(8,128)(2,1)}, ...) | async-done | bytes 4751376
  747.0 6.2 multiply_reduce_fusion.9
  754.9 9.0 fusion.350
  767.0 9.2 fusion.351
  787.0 8.2 multiply_reduce_fusion.2
  804.8 6.0 fusion.145
  845.3 5.8 convolution_convert_fusion.1
  852.5 5.8 convolution_convert_fusion
  859.8 5.9 convolution_convert_fusion.5
  867.2 5.9 convolution_convert_fusion.4
  878.5 45.1 %all-reduce.54.cloned.1.call-done = (bf16[1,580,1024]{1,2,0:T(8,128)(2,1)}, bf16[1,580,1024]{1,2,0:T(8,128)(2,1)}, bf16[1,580,1024]{1,2,0:T(8,128)(2,1)}, bf16[1,580,1024]{1,2,0:T(8,128)(2,1)}) async-done(((bf16[1,580,1024]{1,2,0:T(8,128)(2,1)}, bf16[1,580,1024]{1,2,0:T(8,128)(2,1)}, bf16[1,580,1024]{1,2,0:T(8,128)(2,1)}, bf16[1,580,1024]{1,2,0:T(8,128)(2,1)}), (bf16[1,580,1024]{1,2,0:T(8,128)(2,1)}, ...) | async-done | bytes 4751376
  926.8 5.8 convolution_convert_fusion.11
  947.2 5.8 convolution_convert_fusion.7
  954.5 5.8 convolution_convert_fusion.6
  977.2 15.0 reduce-scatter.39.cloned.1.call-done
  1005.7 20.6 reduce-scatter.33.cloned.1.call-done
  1026.3 34.1 %reduce-scatter.35.cloned.1.call-done = bf16[256,1024]{1,0:T(8,128)(2,1)} async-done(((bf16[1024,1024]{1,0:T(8,128)(2,1)}), bf16[256,1024]{1,0:T(8,128)(2,1)}) %reduce-scatter.35.cloned.1.call-update) | async-done | bytes 524304 | tf_op jit(solution)/shard_map/reduce_scatter | solution.py:333
  1063.9 57.4 %reduce-scatter.29.cloned.1.call-done = bf16[256,3072]{1,0:T(8,128)(2,1)} async-done(((bf16[1024,3072]{1,0:T(8,128)(2,1)}), bf16[256,3072]{1,0:T(8,128)(2,1)}) %reduce-scatter.29.cloned.1.call-update) | async-done | bytes 1572880 | tf_op jit(solution)/shard_map/reduce_scatter | solution.py:327
  1121.4 61.5 %reduce-scatter.31.cloned.1.call-done = bf16[256,3072]{1,0:T(8,128)(2,1)} async-done(((bf16[1024,3072]{1,0:T(8,128)(2,1)}), bf16[256,3072]{1,0:T(8,128)(2,1)}) %reduce-scatter.31.cloned.1.call-update) | async-done | bytes 1572880 | tf_op jit(solution)/shard_map/reduce_scatter | solution.py:327
  1186.5 70.7 %reduce-scatter.53.cloned.1.call-done = bf16[1024,1024]{1,0:T(8,128)(2,1)} async-done(((bf16[4096,1024]{1,0:T(8,128)(2,1)}), bf16[1024,1024]{1,0:T(8,128)(2,1)}) %reduce-scatter.53.cloned.1.call-update) | async-done | bytes 2097168 | tf_op jit(solution)/shard_map/reduce_scatter | solution.py:351
  1257.2 74.4 %reduce-scatter.55.cloned.1.call-done = bf16[1024,1024]{1,0:T(8,128)(2,1)} async-done(((bf16[4096,1024]{1,0:T(8,128)(2,1)}), bf16[1024,1024]{1,0:T(8,128)(2,1)}) %reduce-scatter.55.cloned.1.call-update) | async-done | bytes 2097168 | tf_op jit(solution)/shard_map/reduce_scatter | solution.py:351
  1334.7 71.6 %reduce-scatter.45.cloned.1.call-done = bf16[256,4096]{1,0:T(8,128)(2,1)} async-done(((bf16[1024,4096]{1,0:T(8,128)(2,1)}), bf16[256,4096]{1,0:T(8,128)(2,1)}) %reduce-scatter.45.cloned.1.call-update) | async-done | bytes 2097168 | tf_op jit(solution)/shard_map/reduce_scatter | solution.py:345
  1406.3 75.1 %reduce-scatter.47.cloned.1.call-done = bf16[256,4096]{1,0:T(8,128)(2,1)} async-done(((bf16[1024,4096]{1,0:T(8,128)(2,1)}), bf16[256,4096]{1,0:T(8,128)(2,1)}) %reduce-scatter.47.cloned.1.call-update) | async-done | bytes 2097168 | tf_op jit(solution)/shard_map/reduce_scatter | solution.py:345
  1485.7 56.6 %reduce-scatter.25.cloned.1.call-done = bf16[256,3072]{1,0:T(8,128)(2,1)} async-done(((bf16[1024,3072]{1,0:T(8,128)(2,1)}), bf16[256,3072]{1,0:T(8,128)(2,1)}) %reduce-scatter.25.cloned.1.call-update) | async-done | bytes 1572880 | tf_op jit(solution)/shard_map/reduce_scatter | solution.py:327
  1542.3 60.9 %reduce-scatter.27.cloned.1.call-done = bf16[256,3072]{1,0:T(8,128)(2,1)} async-done(((bf16[1024,3072]{1,0:T(8,128)(2,1)}), bf16[256,3072]{1,0:T(8,128)(2,1)}) %reduce-scatter.27.cloned.1.call-update) | async-done | bytes 1572880 | tf_op jit(solution)/shard_map/reduce_scatter | solution.py:327
  1607.8 69.8 %reduce-scatter.41.cloned.1.call-done = bf16[256,4096]{1,0:T(8,128)(2,1)} async-done(((bf16[1024,4096]{1,0:T(8,128)(2,1)}), bf16[256,4096]{1,0:T(8,128)(2,1)}) %reduce-scatter.41.cloned.1.call-update) | async-done | bytes 2097168 | tf_op jit(solution)/shard_map/reduce_scatter | solution.py:345
  1677.6 74.5 %reduce-scatter.43.cloned.1.call-done = bf16[256,4096]{1,0:T(8,128)(2,1)} async-done(((bf16[1024,4096]{1,0:T(8,128)(2,1)}), bf16[256,4096]{1,0:T(8,128)(2,1)}) %reduce-scatter.43.cloned.1.call-update) | async-done | bytes 2097168 | tf_op jit(solution)/shard_map/reduce_scatter | solution.py:345
  1757.7 68.7 %reduce-scatter.49.cloned.1.call-done = bf16[1024,1024]{1,0:T(8,128)(2,1)} async-done(((bf16[4096,1024]{1,0:T(8,128)(2,1)}), bf16[1024,1024]{1,0:T(8,128)(2,1)}) %reduce-scatter.49.cloned.1.call-update) | async-done | bytes 2097168 | tf_op jit(solution)/shard_map/reduce_scatter | solution.py:351
  1826.3 74.5 %reduce-scatter.51.cloned.1.call-done = bf16[1024,1024]{1,0:T(8,128)(2,1)} async-done(((bf16[4096,1024]{1,0:T(8,128)(2,1)}), bf16[1024,1024]{1,0:T(8,128)(2,1)}) %reduce-scatter.51.cloned.1.call-update) | async-done | bytes 2097168 | tf_op jit(solution)/shard_map/reduce_scatter | solution.py:351
  1927.4 13.5 all-reduce.52.cloned.1.call-done
  1952.9 39.6 %all-reduce.40 = (bf16[2,256]{1,0:T(2,128)(2,1)S(1)}, bf16[2,256]{1,0:T(2,128)(2,1)S(1)}, bf16[2,512]{1,0:T(2,128)(2,1)S(1)}, bf16[2,256]{1,0:T(2,128)(2,1)S(1)}...) all-reduce(bf16[2,256]{1,0:T(2,128)(2,1)S(1)} %pad_maximum_fusion.2, ...), channel_id=1, replica_groups=mesh['rep'=8,'grp'=4] {'rep'}, use_global_device_ids=true, to_apply=%region_68.69 | all-reduce | flops 6144 | bytes 24576 | tf_op jit(solution)/shard_map/psum | solution.py:365
  1997.2 351.4 %all-reduce.50.cloned.1.call-done = (bf16[2,256,3072]{2,1,0:T(8,128)(2,1)}, bf16[2,256,1024]{2,1,0:T(8,128)(2,1)}, bf16[2,256,4096]{2,1,0:T(8,128)(2,1)}, bf16[2,1024,1024]{2,1,0:T(8,128)(2,1)}) async-done(((bf16[2,256,3072]{2,1,0:T(8,128)(2,1)}, bf16[2,256,1024]{2,1,0:T(8,128)(2,1)}, bf16[2,256,4096]{2,1,0:T(8,128)(2,1)}, bf16[2,1024,1024]{2,1,0:T(8,128)(2,1)}), (bf16[2,256,3072]{2,1,0:T(8,128)(2,1)}, ...) | async-done | bytes 12582928 | tf_op jit(solution)/shard_map/psum | solution.py:367
  2348.6 6.8 convert_element_type.1174
  (845 shorter events, 491.0 us)
Async XLA Ops:
  7.2 53.1 %all-gather.57.cloned.1.call-start = ((), (), s32[]{:S(2)}) async-start(), calls=%async_computation.32 | async-start | bytes 7864320 | tf_op jit(solution)/shard_map/all_gather | solution.py:288
  11.1 123.2 %all-gather.75.cloned.1.call-start = ((), (), s32[]{:S(2)}) async-start(), calls=%async_computation.41 | async-start | bytes 1556480 | tf_op jit(solution)/shard_map/all_gather | solution.py:62
  23.7 152.0 %copy-start.31 = (bf16[1,145,1024]{2,1,0:T(8,128)(2,1)}, bf16[1,145,1024]{2,1,0:T(8,128)(2,1)S(1)}, u32[]{:S(2)}) copy-start(bf16[1,145,1024]{2,1,0:T(8,128)(2,1)S(1)} %get-tuple-element.299) | copy-start | bytes 890884
  23.7 161.5 %copy-start.27 = (bf16[1,145,1024]{2,1,0:T(8,128)(2,1)}, bf16[1,145,1024]{2,1,0:T(8,128)(2,1)S(1)}, u32[]{:S(2)}) copy-start(bf16[1,145,1024]{2,1,0:T(8,128)(2,1)S(1)} %get-tuple-element.161) | copy-start | bytes 890884
  65.2 77.6 %all-gather.73.cloned.1.call-start = ((), (), s32[]{:S(2)}) async-start(), calls=%async_computation.40 | async-start | bytes 1556480 | tf_op jit(solution)/shard_map/all_gather | solution.py:65
  77.2 74.0 %all-gather.83.cloned.1.call-start = ((), (), s32[]{:S(2)}) async-start(), calls=%async_computation.45 | async-start | bytes 1556480 | tf_op jit(solution)/shard_map/all_gather | solution.py:62
  79.1 79.8 %all-gather.81.cloned.1.call-start = ((), (), s32[]{:S(2)}) async-start(), calls=%async_computation.44 | async-start | bytes 1556480 | tf_op jit(solution)/shard_map/all_gather | solution.py:65
  79.7 96.0 %all-gather.59.cloned.1.call-start = ((), (), s32[]{:S(2)}) async-start(), calls=%async_computation.33 | async-start | bytes 2621440 | tf_op jit(solution)/shard_map/all_gather | solution.py:290
  82.0 144.9 %all-gather.61.cloned.1.call-start = ((), (), s32[]{:S(2)}) async-start(), calls=%async_computation.34 | async-start | bytes 10485760 | tf_op jit(solution)/shard_map/all_gather | solution.py:294
  86.8 200.5 %all-gather.63.cloned.1.call-start = ((), (), s32[]{:S(2)}) async-start(), calls=%async_computation.35 | async-start | bytes 10485760 | tf_op jit(solution)/shard_map/all_gather | solution.py:296
  91.6 243.7 %all-gather.65.cloned.1.call-start = ((), (), s32[]{:S(2)}) async-start(), calls=%async_computation.36 | async-start | bytes 7864320 | tf_op jit(solution)/shard_map/all_gather | solution.py:288
  92.4 298.8 %all-gather.79.cloned.1.call-start = ((), (), s32[]{:S(2)}) async-start(), calls=%async_computation.43 | async-start | bytes 1556480 | tf_op jit(solution)/shard_map/all_gather | solution.py:62
  102.6 238.8 %copy-start.138 = (f32[1,1024]{1,0:T(1,128)}, f32[1,1024]{1,0:T(1,128)S(1)}, u32[]{:S(2)}) copy-start(f32[1,1024]{1,0:T(1,128)S(1)} %convert_element_type.1197) | copy-start | bytes 12292
  107.7 233.7 %copy-start.146 = (f32[1,1024]{1,0:T(1,128)}, f32[1,1024]{1,0:T(1,128)S(1)}, u32[]{:S(2)}) copy-start(f32[1,1024]{1,0:T(1,128)S(1)} %convert_element_type.1198) | copy-start | bytes 12292
  123.6 234.2 %copy-start.140 = (f32[1,1024]{1,0:T(1,128)}, f32[1,1024]{1,0:T(1,128)S(1)}, u32[]{:S(2)}) copy-start(f32[1,1024]{1,0:T(1,128)S(1)} %convert_element_type.1201) | copy-start | bytes 12292
  128.6 229.1 %copy-start.148 = (f32[1,1024]{1,0:T(1,128)}, f32[1,1024]{1,0:T(1,128)S(1)}, u32[]{:S(2)}) copy-start(f32[1,1024]{1,0:T(1,128)S(1)} %convert_element_type.1202) | copy-start | bytes 12292
  186.0 166.0 %copy-start.12 = (f32[145,1024]{1,0:T(8,128)}, f32[145,1024]{1,0:T(8,128)S(1)}, u32[]{:S(2)}) copy-start(f32[145,1024]{1,0:T(8,128)S(1)} %get-tuple-element.245) | copy-start | bytes 1781764
  186.0 155.4 %copy-start.164 = (f32[145]{0:T(256)}, f32[145]{0:T(256)S(1)}, u32[]{:S(2)}) copy-start(f32[145]{0:T(256)S(1)} %broadcast_multiply_fusion.2) | copy-start | bytes 1744
  186.3 155.2 %copy-start.177 = (f32[145]{0:T(256)}, f32[145]{0:T(256)S(1)}, u32[]{:S(2)}) copy-start(f32[145]{0:T(256)S(1)} %fusion.289) | copy-start | bytes 1744
  341.4 57.5 %all-gather.77.cloned.1.call-start = ((), (), s32[]{:S(2)}) async-start(), calls=%async_computation.42 | async-start | bytes 1556480 | tf_op jit(solution)/shard_map/all_gather | solution.py:65
  360.6 47.0 %all-gather.87.cloned.1.call-start = ((), (), s32[]{:S(2)}) async-start(), calls=%async_computation.47 | async-start | bytes 1556480 | tf_op jit(solution)/shard_map/all_gather | solution.py:62
  361.4 57.2 %all-gather.85.cloned.1.call-start = ((), (), s32[]{:S(2)}) async-start(), calls=%async_computation.46 | async-start | bytes 1556480 | tf_op jit(solution)/shard_map/all_gather | solution.py:65
  362.2 80.5 %all-gather.67.cloned.1.call-start = ((), (), s32[]{:S(2)}) async-start(), calls=%async_computation.37 | async-start | bytes 2621440 | tf_op jit(solution)/shard_map/all_gather | solution.py:290
  362.8 140.2 %all-gather.69.cloned.1.call-start = ((), (), s32[]{:S(2)}) async-start(), calls=%async_computation.38 | async-start | bytes 10485760 | tf_op jit(solution)/shard_map/all_gather | solution.py:294
  363.4 199.4 %all-gather.71.cloned.1.call-start = ((), (), s32[]{:S(2)}) async-start(), calls=%async_computation.39 | async-start | bytes 10485760 | tf_op jit(solution)/shard_map/all_gather | solution.py:296
  364.0 369.9 %all-reduce.56.cloned.1.call-start = ((), (), s32[]{:S(2)}) async-start(), calls=%async_computation.51 | async-start | bytes 10485760
  379.4 134.4 %copy-start.150 = (f32[1,1024]{1,0:T(1,128)}, f32[1,1024]{1,0:T(1,128)S(1)}, u32[]{:S(2)}) copy-start(f32[1,1024]{1,0:T(1,128)S(1)} %convert_element_type.1205) | copy-start | bytes 12292
  445.2 146.6 %copy-start.18 = (f32[145,1024]{1,0:T(8,128)}, f32[145,1024]{1,0:T(8,128)S(1)}, u32[]{:S(2)}) copy-start(f32[145,1024]{1,0:T(8,128)S(1)} %get-tuple-element.267) | copy-start | bytes 1781764
  452.5 139.3 %copy-start.20 = (f32[145,1024]{1,0:T(8,128)}, f32[145,1024]{1,0:T(8,128)S(1)}, u32[]{:S(2)}) copy-start(f32[145,1024]{1,0:T(8,128)S(1)} %get-tuple-element.261) | copy-start | bytes 1781764
  630.6 293.0 %all-reduce.54.cloned.1.call-start = ((), (), s32[]{:S(2)}) async-start(), calls=%async_computation.50 | async-start | bytes 10485760
  820.2 157.0 %reduce-scatter.37.cloned.1.call-start = ((), (), s32[]{:S(2)}) async-start(), calls=%async_computation.22 | async-start | bytes 2621440 | tf_op jit(solution)/shard_map/reduce_scatter | solution.py:333
  823.4 168.9 %reduce-scatter.39.cloned.1.call-start = ((), (), s32[]{:S(2)}) async-start(), calls=%async_computation.23 | async-start | bytes 2621440 | tf_op jit(solution)/shard_map/reduce_scatter | solution.py:333
  826.6 199.6 %reduce-scatter.33.cloned.1.call-start = ((), (), s32[]{:S(2)}) async-start(), calls=%async_computation.20 | async-start | bytes 2621440 | tf_op jit(solution)/shard_map/reduce_scatter | solution.py:333
  828.8 231.6 %reduce-scatter.35.cloned.1.call-start = ((), (), s32[]{:S(2)}) async-start(), calls=%async_computation.21 | async-start | bytes 2621440 | tf_op jit(solution)/shard_map/reduce_scatter | solution.py:333
  832.0 289.3 %reduce-scatter.29.cloned.1.call-start = ((), (), s32[]{:S(2)}) async-start(), calls=%async_computation.18 | async-start | bytes 7864320 | tf_op jit(solution)/shard_map/reduce_scatter | solution.py:327
  837.9 345.0 %reduce-scatter.31.cloned.1.call-start = ((), (), s32[]{:S(2)}) async-start(), calls=%async_computation.19 | async-start | bytes 7864320 | tf_op jit(solution)/shard_map/reduce_scatter | solution.py:327
  844.0 413.2 %reduce-scatter.53.cloned.1.call-start = ((), (), s32[]{:S(2)}) async-start(), calls=%async_computation.30 | async-start | bytes 10485760 | tf_op jit(solution)/shard_map/reduce_scatter | solution.py:351
  851.1 480.4 %reduce-scatter.55.cloned.1.call-start = ((), (), s32[]{:S(2)}) async-start(), calls=%async_computation.31 | async-start | bytes 10485760 | tf_op jit(solution)/shard_map/reduce_scatter | solution.py:351
  858.3 548.0 %reduce-scatter.45.cloned.1.call-start = ((), (), s32[]{:S(2)}) async-start(), calls=%async_computation.26 | async-start | bytes 10485760 | tf_op jit(solution)/shard_map/reduce_scatter | solution.py:345
  865.7 615.6 %reduce-scatter.47.cloned.1.call-start = ((), (), s32[]{:S(2)}) async-start(), calls=%async_computation.27 | async-start | bytes 10485760 | tf_op jit(solution)/shard_map/reduce_scatter | solution.py:345
  873.2 669.1 %reduce-scatter.25.cloned.1.call-start = ((), (), s32[]{:S(2)}) async-start(), calls=%async_computation.16 | async-start | bytes 7864320 | tf_op jit(solution)/shard_map/reduce_scatter | solution.py:327
  932.7 670.6 %reduce-scatter.27.cloned.1.call-start = ((), (), s32[]{:S(2)}) async-start(), calls=%async_computation.17 | async-start | bytes 7864320 | tf_op jit(solution)/shard_map/reduce_scatter | solution.py:327
  945.7 731.9 %reduce-scatter.41.cloned.1.call-start = ((), (), s32[]{:S(2)}) async-start(), calls=%async_computation.24 | async-start | bytes 10485760 | tf_op jit(solution)/shard_map/reduce_scatter | solution.py:345
  953.0 799.1 %reduce-scatter.43.cloned.1.call-start = ((), (), s32[]{:S(2)}) async-start(), calls=%async_computation.25 | async-start | bytes 10485760 | tf_op jit(solution)/shard_map/reduce_scatter | solution.py:345
  960.3 866.0 %reduce-scatter.49.cloned.1.call-start = ((), (), s32[]{:S(2)}) async-start(), calls=%async_computation.28 | async-start | bytes 10485760 | tf_op jit(solution)/shard_map/reduce_scatter | solution.py:351
  967.5 933.3 %reduce-scatter.51.cloned.1.call-start = ((), (), s32[]{:S(2)}) async-start(), calls=%async_computation.29 | async-start | bytes 10485760 | tf_op jit(solution)/shard_map/reduce_scatter | solution.py:351
  975.0 965.9 %all-reduce.52.cloned.1.call-start = ((), (), s32[]{:S(2)}) async-start(), calls=%async_computation.49 | async-start | bytes 196608
  1005.4 1343.2 %all-reduce.50.cloned.1.call-start = ((), (), s32[]{:S(2)}) async-start(), calls=%async_computation.48 | async-start | bytes 25165824 | tf_op jit(solution)/shard_map/psum | solution.py:367
  (223 other events, 2405.8 us)
Sparse Core Ops, SparseCore 0:
  11.2 49.0 all-gather.56
  65.3 17.8 all-gather.74
  84.7 17.8 all-gather.72
  104.0 17.8 all-gather.82
  123.9 17.8 all-gather.80
  143.7 22.5 all-gather.58
  168.5 58.3 all-gather.60
  229.0 58.2 all-gather.62
  288.9 46.3 all-gather.64
  341.5 17.8 all-gather.78
  361.5 17.8 all-gather.76
  380.8 17.8 all-gather.86
  400.8 17.8 all-gather.84
  420.1 22.5 all-gather.66
  444.7 58.2 all-gather.68
  504.4 58.2 all-gather.70
  630.7 103.0 all-reduce.55
  820.3 103.2 all-reduce.53
  926.1 31.5 reduce-scatter.36
  960.8 31.3 reduce-scatter.38
  994.8 31.4 reduce-scatter.32
  1029.0 31.3 reduce-scatter.34
  1062.9 58.3 reduce-scatter.28
  1124.5 58.3 reduce-scatter.30
  1185.4 71.7 reduce-scatter.52
  1259.8 71.6 reduce-scatter.54
  1334.6 71.7 reduce-scatter.44
  1409.6 71.6 reduce-scatter.46
  1483.9 58.3 reduce-scatter.24
  1544.9 58.3 reduce-scatter.26
  1605.8 71.7 reduce-scatter.40
  1680.4 71.6 reduce-scatter.42
  1754.5 71.7 reduce-scatter.48
  1829.1 71.6 reduce-scatter.50
  1906.1 34.7 all-reduce.51
  1947.4 401.1 all-reduce.49
where the time goes:
time: 2380 us; the launch traced here: 2370 us
  waiting for transfers between devices  1670 us (70%)
  matrix products  317 us (13%)
  local copies, waits for them, and re-layouts  138 us (6%)
  blocking collectives  122 us (5%)
  other arithmetic  106 us (4%)
    psum x1, waiting for transfers between devices, local(): lax.psum(merged[2].astype(jnp.bfloat16), 'rep').astype(jnp.float32)  351 us
    reduce_scatter x4, waiting for transfers between devices, local(): lax.psum_scatter(terms[8].astype(jnp.bfloat16), 'grp', scatter_dimension=...  291 us
    reduce_scatter x4, waiting for transfers between devices, local(): lax.psum_scatter(terms[10].astype(jnp.bfloat16), 'grp', scatter_dimension...  288 us
    reduce_scatter x4, waiting for transfers between devices, local(): lax.psum_scatter(terms[2].astype(jnp.bfloat16), 'grp', scatter_dimension=...  236 us
    unnamed x39, waiting for transfers between devices  158 us
    all_gather x2, waiting for transfers between devices, local(): lax.all_gather(pieces[8], 'grp', axis=0, tiled=True)  90.8 us
    all_gather x2, waiting for transfers between devices, local(): lax.all_gather(pieces[10], 'grp', axis=0, tiled=True)  90.4 us
    all_gather x2, waiting for transfers between devices, local(): lax.all_gather(pieces[2], 'grp', axis=0, tiled=True)  78.7 us
  transfers between devices with their start and end apart: 36, of which 27 were waited for; matrix products, arithmetic and copies ran while one was open for 15% of the time, Pallas kernels for 0%

commit v1 on v0

v1 whole, which is shorter than its diff:
```python
import functools

import jax
import jax.numpy as jnp
from jax import lax
from jax.experimental import pallas as pl
from jax.experimental.pallas import tpu as pltpu
from jax.sharding import PartitionSpec as P

HEAD = 64
MESH = pl.DeviceIdType.MESH
F32 = jnp.float32
BF16 = jnp.bfloat16
VMEM_LIMIT = 62 * 2**20
G1, B1, BOUT, G2, B2, BDOWN = range(6)


def nn(a, b):
    return lax.dot_general(a, b, (((1,), (0,)), ((), ())), preferred_element_type=F32)


def nt(a, b):
    return lax.dot_general(a, b, (((1,), (1,)), ((), ())), preferred_element_type=F32)


def tn(a, b):
    return lax.dot_general(a, b, (((0,), (0,)), ((), ())), preferred_element_type=F32)


def cols(j, width):
    return pl.ds(pl.multiple_of(j * width, width), width)


def loop(count, body):
    def step(j, carry):
        body(j)
        return carry

    lax.fori_loop(0, count, step, 0)


def mates():
    rep, grp = lax.axis_index("rep"), lax.axis_index("grp")
    return (rep, grp + 1 - 2 * (grp % 2))


def greet():
    barrier = pltpu.get_barrier_semaphore()
    pl.semaphore_signal(barrier, inc=1, device_id=mates(), device_id_type=MESH)
    pl.semaphore_wait(barrier, 1)


def to_mate(src, dst, send, recv, slot):
    return pltpu.make_async_remote_copy(
        src_ref=src,
        dst_ref=dst,
        send_sem=send.at[slot],
        recv_sem=recv.at[slot],
        device_id=mates(),
        device_id_type=MESH,
    )


def norm_rows(v):
    mean = jnp.mean(v, axis=-1, keepdims=True)
    off = v - mean
    rstd = lax.rsqrt(jnp.mean(off * off, axis=-1, keepdims=True) + 1e-6)
    return off * rstd, rstd


def scores_t(k2, qa, mask):
    st = jnp.where(mask > 0, nt(k2, qa), -1e9)
    top = jnp.max(st, axis=0, keepdims=True)
    e = jnp.exp(st - top)
    return e * (1.0 / jnp.sum(e, axis=0, keepdims=True))


def half_lanes(v, a):
    lane = lax.broadcasted_iota(jnp.int32, v.shape, 1)
    return jnp.where((lane >= HEAD) == (a == 1), v, jnp.zeros_like(v))


def fwd_kernel(
    x_ref, vec_ref, bqkv_ref, bup_ref, mask_ref, wqkv_ref, wout_ref, wup_ref, wdown_ref,
    x2_ref, x3_ref, h1_ref, qkv_ref, a_ref, h2_ref, z_ref, gp_ref,
    put_ref, got_ref, send, recv,
):
    rows, d = x_ref.shape
    hc = a_ref.shape[1]
    f = z_ref.shape[1]
    own, sib = pl.ds(0, rows), pl.ds(rows, rows)
    step = 16
    greet()

    def norm_out(src_ref, dst_ref, gain, shift):
        for i in range(rows // step):
            r = pl.ds(i * step, step)
            hat, _ = norm_rows(src_ref[r, :])
            dst_ref[r, :] = (hat * vec_ref[gain:gain + 1, :] + vec_ref[shift:shift + 1, :]).astype(BF16)

    norm_out(x_ref, h1_ref, G1, B1)
    cp = to_mate(h1_ref.at[own], h1_ref.at[sib], send, recv, 0)
    cp.start()

    wide = 256

    def qkv_rows(r):
        def body(j):
            c = cols(j, wide)
            out = nn(h1_ref[r, :], wqkv_ref[:, c]) + bqkv_ref[0:1, c]
            qkv_ref[r, c] = (out * bqkv_ref[1:2, c]).astype(BF16)

        loop(3 * hc // wide, body)

    qkv_rows(own)
    cp.wait()
    qkv_rows(sib)

    mask = mask_ref[:, 0:1]

    def pair(p):
        q2 = qkv_ref[:, pl.ds(pl.multiple_of(p * 128, 128), 128)]
        k2 = qkv_ref[:, pl.ds(pl.multiple_of(hc + p * 128, 128), 128)]
        v2 = qkv_ref[:, pl.ds(pl.multiple_of(2 * hc + p * 128, 128), 128)]
        vt = v2.T
        parts = []
        for a in range(2):
            pt = scores_t(k2, half_lanes(q2, a), mask)
            parts.append(nn(vt[a * HEAD:(a + 1) * HEAD, :], pt.astype(BF16)))
        a_ref[:, pl.ds(pl.multiple_of(p * 128, 128), 128)] = jnp.concatenate(parts, axis=0).T.astype(BF16)

    loop(hc // 128, pair)

    def exchange(left_ref, w_ref, base_ref, bias, out_ref, slot):
        def theirs(j):
            c = cols(j, wide)
            put_ref[slot, :, c] = nn(left_ref[sib, :], w_ref[:, c]).astype(BF16)

        loop(d // wide, theirs)
        cp = to_mate(put_ref.at[slot], got_ref.at[slot], send, recv, 1 + slot)
        cp.start()

        def ours(j):
            c = cols(j, wide)
            out_ref[:, c] = nn(left_ref[own, :], w_ref[:, c]) + base_ref[:, c] + vec_ref[bias:bias + 1, c]

        loop(d // wide, ours)
        cp.wait()
        out_ref[...] += got_ref[slot].astype(F32)

    exchange(a_ref, wout_ref, x_ref, BOUT, x2_ref, 0)
    norm_out(x2_ref, h2_ref, G2, B2)
    cp = to_mate(h2_ref.at[own], h2_ref.at[sib], send, recv, 3)
    cp.start()

    def up_rows(r):
        def body(j):
            c = cols(j, wide)
            u = nn(h2_ref[r, :], wup_ref[:, c]) + bup_ref[0:1, c]
            phi = 0.5 + 0.5 * lax.erf(u * 0.7071067811865476)
            z_ref[r, c] = (u * phi).astype(BF16)
            gp_ref[r, c] = (phi + u * jnp.exp(u * u * -0.5) * 0.3989422804014327).astype(BF16)

        loop(f // wide, body)

    up_rows(own)
    cp.wait()
    up_rows(sib)
    exchange(z_ref, wdown_ref, x2_ref, BDOWN, x3_ref, 1)


def bwd_kernel(
    g3_ref, x_ref, x2_ref, h1_ref, qkv_ref, a_ref, h2_ref, z_ref, gp_ref,
    vec_ref, mask_ref, wqkv_ref, wout_ref, wup_ref, wdown_ref,
    g0_ref, gwqkv_ref, gwout_ref, gwup_ref, gwdown_ref, gvec_ref, gbqkv_ref, gbup_ref,
    dm_ref, du_ref, da_ref, dj_ref, dx2_ref, dh_ref, put_ref, got_ref, send, recv,
):
    rows, d = g3_ref.shape
    hc = a_ref.shape[1]
    f = z_ref.shape[1]
    own, sib = pl.ds(0, rows), pl.ds(rows, rows)
    step = 16
    wide = 256
    greet()

    def send_round(src_ref, sum_row, slot):
        total = jnp.zeros((8, d), F32)
        for i in range(rows // step):
            r = pl.ds(i * step, step)
            low = src_ref[r, :].astype(BF16)
            dm_ref[slot, r, :] = low
            low = low.astype(F32)
            total = total + low[0:8, :] + low[8:16, :]
        gvec_ref[sum_row:sum_row + 1, :] = jnp.sum(total, axis=0, keepdims=True)
        cp = to_mate(dm_ref.at[slot, own], dm_ref.at[slot, sib], send, recv, slot)
        cp.start()
        return cp

    def exchange(left_ref, w_ref, slot):
        def theirs(j):
            c = cols(j, wide)
            put_ref[slot, :, c] = nt(left_ref[sib, :], w_ref[c, :]).astype(BF16)

        loop(d // wide, theirs)
        cp = to_mate(put_ref.at[slot], got_ref.at[slot], send, recv, 2 + slot)
        cp.start()

        def ours(j):
            c = cols(j, wide)
            dh_ref[:, c] = nt(left_ref[own, :], w_ref[c, :])

        loop(d // wide, ours)
        return cp

    def norm_back(value_ref, base_ref, out_ref, gain, shift, slot):
        total_g = jnp.zeros((8, d), F32)
        total_b = jnp.zeros((8, d), F32)
        for i in range(rows // step):
            r = pl.ds(i * step, step)
            hat, rstd = norm_rows(value_ref[r, :])
            dh = dh_ref[r, :] + got_ref[slot, r, :].astype(F32)
            prod = dh * hat
            total_g = total_g + prod[0:8, :] + prod[8:16, :]
            total_b = total_b + dh[0:8, :] + dh[8:16, :]
            dhat = dh * vec_ref[gain:gain + 1, :]
            m1 = jnp.mean(dhat, axis=-1, keepdims=True)
            m2 = jnp.mean(dhat * hat, axis=-1, keepdims=True)
            out_ref[r, :] = base_ref[r, :] + rstd * (dhat - m1 - hat * m2)
        gvec_ref[gain:gain + 1, :] = jnp.sum(total_g, axis=0, keepdims=True)
        gvec_ref[shift:shift + 1, :] = jnp.sum(total_b, axis=0, keepdims=True)

    cp = send_round(g3_ref, BDOWN, 0)

    def dz_rows(r):
        def body(j):
            c = cols(j, wide)
            dz = nt(dm_ref[0, r, :], wdown_ref[c, :])
            du_ref[r, c] = (dz * gp_ref[r, c].astype(F32)).astype(BF16)

        loop(f // wide, body)

    dz_rows(own)
    cp.wait()
    dz_rows(sib)

    def grads_ff(j):
        c = cols(j, wide)
        gwdown_ref[c, :] = tn(z_ref[:, c], dm_ref[0]).astype(BF16)
        du = du_ref[:, c]
        gwup_ref[:, c] = tn(h2_ref[...], du).astype(BF16)
        gbup_ref[0:1, c] = jnp.sum(du.astype(F32), axis=0, keepdims=True)

    cp = exchange(du_ref, wup_ref, 0)
    loop(f // wide, grads_ff)
    cp.wait()
    norm_back(x2_ref, g3_ref, dx2_ref, G2, B2, 0)
    cp = send_round(dx2_ref, BOUT, 1)

    def da_rows(r):
        def body(j):
            c = cols(j, wide)
            da_ref[r, c] = nt(dm_ref[1, r, :], wout_ref[c, :]).astype(BF16)

        loop(hc // wide, body)

    da_rows(own)
    cp.wait()
    da_rows(sib)

    def grads_out(j):
        c = cols(j, wide)
        gwout_ref[c, :] = tn(a_ref[:, c], dm_ref[1]).astype(BF16)

    loop(hc // wide, grads_out)
    mask = mask_ref[:, 0:1]

    def pair(p):
        cq = pl.ds(pl.multiple_of(p * 128, 128), 128)
        ck = pl.ds(pl.multiple_of(hc + p * 128, 128), 128)
        cv = pl.ds(pl.multiple_of(2 * hc + p * 128, 128), 128)
        q2, k2, v2, da2 = qkv_ref[:, cq], qkv_ref[:, ck], qkv_ref[:, cv], da_ref[:, cq]
        kt = k2.T
        dk = dv = None
        parts = []
        for a in range(2):
            qa, daa = half_lanes(q2, a), half_lanes(da2, a)
            pt = scores_t(k2, qa, mask)
            dpt = nt(v2, daa)
            delta = jnp.sum(dpt * pt, axis=0, keepdims=True)
            dst = (pt * (dpt - delta)).astype(BF16)
            dva = nn(pt.astype(BF16), daa)
            dka = nn(dst, qa)
            parts.append(nn(kt[a * HEAD:(a + 1) * HEAD, :], dst))
            dk = dka if dk is None else dk + dka
            dv = dva if dv is None else dv + dva
        dq = (jnp.concatenate(parts, axis=0).T * HEAD ** -0.5).astype(BF16)
        dv = dv.astype(BF16)
        dj_ref[:, cq] = dq
        dj_ref[:, ck] = dk.astype(BF16)
        dj_ref[:, cv] = dv
        gbqkv_ref[0:1, cq] = jnp.sum(dq.astype(F32), axis=0, keepdims=True)
        gbqkv_ref[0:1, cv] = jnp.sum(dv.astype(F32), axis=0, keepdims=True)

    loop(hc // 128, pair)
    cp = exchange(dj_ref, wqkv_ref, 1)

    def grads_qkv(j):
        c = cols(j, wide)
        gwqkv_ref[:, c] = tn(h1_ref[...], dj_ref[:, c]).astype(BF16)

    loop(3 * hc // wide, grads_qkv)
    cp.wait()
    norm_back(x_ref, dx2_ref, g0_ref, G1, B1, 1)


VM = pl.BlockSpec(memory_space=pltpu.VMEM)


def run_fwd(x, vec, bqkv, bup, mask, wqkv, wout, wup, wdown):
    rows, d = x.shape
    hc, f = wout.shape[0], wdown.shape[0]
    both = 2 * rows
    shapes = [
        ((rows, d), F32), ((rows, d), F32), ((both, d), BF16), ((both, 3 * hc), BF16),
        ((both, hc), BF16), ((both, d), BF16), ((both, f), BF16), ((both, f), BF16),
    ]
    args = (x, vec, bqkv, bup, mask, wqkv, wout, wup, wdown)
    return pl.pallas_call(
        fwd_kernel,
        out_shape=[jax.ShapeDtypeStruct(s, t) for s, t in shapes],
        in_specs=[VM] * len(args),
        out_specs=[VM] * len(shapes),
        scratch_shapes=[
            pltpu.VMEM((2, rows, d), BF16), pltpu.VMEM((2, rows, d), BF16),
            pltpu.SemaphoreType.DMA((4,)), pltpu.SemaphoreType.DMA((4,)),
        ],
        compiler_params=pltpu.CompilerParams(
            collective_id=1, has_side_effects=True, vmem_limit_bytes=VMEM_LIMIT
        ),
        cost_estimate=pl.CostEstimate(flops=8 * 10**9, bytes_accessed=20 * 10**6, transcendentals=0),
        name="layer_fwd",
    )(*args)


def run_bwd(g3, saved, vec, mask, wqkv, wout, wup, wdown):
    rows, d = g3.shape
    hc, f = wout.shape[0], wdown.shape[0]
    both = 2 * rows
    shapes = [
        ((rows, d), F32), (wqkv.shape, BF16), (wout.shape, BF16), (wup.shape, BF16), (wdown.shape, BF16),
        ((8, d), F32), ((8, 3 * hc), F32), ((8, f), F32),
    ]
    args = (g3, *saved, vec, mask, wqkv, wout, wup, wdown)
    return pl.pallas_call(
        bwd_kernel,
        out_shape=[jax.ShapeDtypeStruct(s, t) for s, t in shapes],
        in_specs=[VM] * len(args),
        out_specs=[VM] * len(shapes),
        scratch_shapes=[
            pltpu.VMEM((2, both, d), BF16), pltpu.VMEM((both, f), BF16), pltpu.VMEM((both, hc), BF16),
            pltpu.VMEM((both, 3 * hc), BF16), pltpu.VMEM((rows, d), F32), pltpu.VMEM((rows, d), F32),
            pltpu.VMEM((2, rows, d), BF16), pltpu.VMEM((2, rows, d), BF16),
            pltpu.SemaphoreType.DMA((4,)), pltpu.SemaphoreType.DMA((4,)),
        ],
        compiler_params=pltpu.CompilerParams(
            collective_id=2, has_side_effects=True, vmem_limit_bytes=VMEM_LIMIT
        ),
        cost_estimate=pl.CostEstimate(flops=17 * 10**9, bytes_accessed=40 * 10**6, transcendentals=0),
        name="layer_bwd",
    )(*args)


def swap(value, bit):
    return lax.ppermute(value, "grp", [(i, i ^ bit) for i in range(4)])


def pick(value, index, axis):
    return lax.dynamic_index_in_dim(value, index, axis, keepdims=False)


def local(
    tokens, cotangent, image_valid, token_valid,
    norm1_gain, norm1_bias, w_qkv, b_qv, w_out, b_out, norm2_gain, norm2_bias, w_up, b_up, w_down, b_down,
):
    grp = lax.axis_index("grp")
    x, c = grp // 2, grp % 2
    layers, dq, d3 = w_qkv.shape
    d = d3 // 3
    hc = d // 2
    f = 2 * w_down.shape[1] * 1
    seq = tokens.shape[1]
    real = 2 * seq
    rows = -(-real // 16) * 16

    def mine(value):
        got = swap(pick(value, 1 - x, 0), 2)
        return jnp.concatenate([pick(value, x, 0), got], axis=0)

    def pad(value):
        return jnp.pad(value, [(0, rows - real)] + [(0, 0)] * (value.ndim - 1))

    flags = pick(token_valid, x, 0).reshape(2, 2, seq)
    own_flags = pad(jnp.concatenate([pick(pick(flags, x, 0), c, 0), pick(pick(flags, 1 - x, 0), c, 0)]))
    sib_flags = pad(jnp.concatenate([pick(pick(flags, x, 0), 1 - c, 0), pick(pick(flags, 1 - x, 0), 1 - c, 0)]))
    mask = jnp.broadcast_to(jnp.concatenate([own_flags, sib_flags])[:, None], (2 * rows, 128))
    weight = (own_flags * pick(image_valid, x, 0)).astype(F32)
    hidden = pad(mine(tokens)).astype(F32)
    flow = pad(mine(cotangent)).astype(F32) * weight[:, None]

    smalls = [norm1_gain, norm1_bias, b_out, norm2_gain, norm2_bias, b_down, b_qv, b_up]
    widths = [s.shape[1] for s in smalls]
    packed = lax.all_gather(jnp.concatenate(smalls, axis=1), "grp", axis=0)
    parts, at = [], 0
    for width in widths:
        parts.append(packed[:, :, at:at + width].transpose(1, 0, 2).reshape(layers, 4 * width).astype(F32))
        at += width
    vecs = jnp.stack(parts[:6] + [jnp.zeros_like(parts[0])] * 2, axis=1)

    def halves(value, axis):
        return pick(value, c, axis)

    bq = halves(parts[6][:, :d].reshape(layers, 2, 2, d // 4), 2).reshape(layers, hc)
    bv = halves(parts[6][:, d:].reshape(layers, 2, 2, d // 4), 2).reshape(layers, hc)
    bqkv = jnp.concatenate([bq, jnp.zeros_like(bq), bv], axis=1)
    scale = jnp.concatenate([jnp.full_like(bq, HEAD ** -0.5), jnp.ones((layers, 2 * hc), F32)], axis=1)
    bqkv = jnp.pad(jnp.stack([bqkv, scale], axis=1), ((0, 0), (0, 6), (0, 0)))
    bup = halves(parts[7].reshape(layers, 2, 2, -1), 2).reshape(layers, 1, -1)
    bup = jnp.pad(bup, ((0, 0), (0, 7), (0, 0)))

    def by_core(value, other):
        return jnp.where(c == 0, jnp.concatenate([value, other], axis=1), jnp.concatenate([other, value], axis=1))

    def by_chip(value):
        other = swap(value, 2)
        return jnp.where(x == 0, jnp.concatenate([value, other], axis=1), jnp.concatenate([other, value], axis=1))

    def columns(w, groups):
        w = w.reshape(layers, w.shape[1], groups, 2, 2, -1)
        keep = pick(w, c, 4).reshape(layers, w.shape[1], -1)
        give = pick(w, 1 - c, 4).reshape(layers, w.shape[1], -1)
        return by_chip(by_core(keep, swap(give, 1)))

    wqkv = columns(w_qkv, 3)
    wup = columns(w_up, 1)
    wout = by_chip(w_out)
    wdown = by_chip(w_down)

    saved = []
    for l in range(layers):
        x2, x3, *rest = run_fwd(hidden, vecs[l], bqkv[l], bup[l], mask, wqkv[l], wout[l], wup[l], wdown[l])
        saved.append((hidden, x2, *rest))
        hidden = x3

    def give_back(value):
        value = value[:real].astype(BF16).reshape(2, seq, d)
        got = swap(value[1], 2)
        return jnp.where(x == 0, jnp.stack([value[0], got]), jnp.stack([got, value[0]]))

    activations = give_back(hidden)
    grads = [None] * layers
    for l in reversed(range(layers)):
        flow, *grads[l] = run_bwd(flow, saved[l], vecs[l], mask, wqkv[l], wout[l], wup[l], wdown[l])
    grad_tokens = give_back(flow)

    def reduce_big(index):
        g = jnp.stack([grads[l][index] for l in range(layers)])
        n = g.shape[1] // 2
        keep = lax.dynamic_slice_in_dim(g, x * n, n, 1)
        give = lax.dynamic_slice_in_dim(g, (1 - x) * n, n, 1)
        total = (keep.astype(F32) + swap(give, 2).astype(F32)).astype(BF16)
        return lax.psum(total, "rep")

    def uncolumns(g, groups):
        n = g.shape[1] // 2
        keep = lax.dynamic_slice_in_dim(g, c * n, n, 1)
        give = lax.dynamic_slice_in_dim(g, (1 - c) * n, n, 1)
        got = swap(give, 1)
        keep = keep.reshape(layers, n, groups, 2, -1)
        got = got.reshape(layers, n, groups, 2, -1)
        return jnp.where(c == 0, jnp.stack([keep, got], axis=4), jnp.stack([got, keep], axis=4)).reshape(layers, n, -1).astype(F32)

    gqkv = uncolumns(reduce_big(0), 3)
    gout = reduce_big(1).astype(F32)
    gup = uncolumns(reduce_big(2), 1)
    gdown = reduce_big(3).astype(F32)

    gvec = jnp.stack([grads[l][4][:6].reshape(6 * d) for l in range(layers)])
    gb = jnp.stack([grads[l][5][0] for l in range(layers)]).reshape(layers, 3, 2, -1)[:, ::2]
    gu = jnp.stack([grads[l][6][0] for l in range(layers)]).reshape(layers, 2, -1)

    def spread(v):
        z = jnp.zeros_like(v)
        return jnp.where(c == 0, jnp.stack([v, z], axis=-2), jnp.stack([z, v], axis=-2)).reshape(layers, -1)

    small = lax.psum(jnp.concatenate([gvec, spread(gb), spread(gu)], axis=1), ("rep", "grp"))
    outs, at = [], 0
    for width in widths:
        outs.append(lax.dynamic_slice_in_dim(small[:, at:at + 4 * width], grp * width, width, 1))
        at += 4 * width
    gg1, gb1, gbout, gg2, gb2, gbdown, gbqv, gbup = outs
    return (activations, grad_tokens, gg1, gb1, gqkv, gbqv, gout, gbout, gg2, gb2, gup, gbup, gdown, gbdown)


def solution(mesh):
    rows3, mat, vec = P("rep", "grp", None), P(None, "grp", None), P(None, "grp")
    weights = (vec, vec, mat, vec, mat, vec, vec, vec, mat, vec, mat, vec)
    return jax.shard_map(
        local,
        mesh=mesh,
        in_specs=(rows3, rows3, P("rep"), P("rep", None)) + weights,
        out_specs=(rows3, rows3) + weights,
        check_vma=False,
    )
```

time: 2380 us -> 1490 us (0.63)
  waiting for transfers between devices: 1670 us -> 898 us
  matrix products: 317 us -> 0 us
  Pallas kernels: 0 us -> 188 us
  local copies, waits for them, and re-layouts: 138 us -> 191 us
  blocking collectives: 122 us -> 92.2 us
    reduce_scatter x16 -> x0, waiting for transfers between devices: 885 us -> none  [the longest x4 291 us: local(): lax.psum_scatter(terms[8].astype(jnp.bfloat16), 'grp', scatter_dimension=...]
    ppermute x0 -> x16, waiting for transfers between devices: none -> 388 us  [swap(): return lax.ppermute(value, 'grp', [(i, i ^ bit) for i in range(4)])]
    dot_general x72 -> x0, matrix products: 317 us -> none  [the longest x4 40.3 us: forward_block(): jnp.dot(normed_two, w_in, preferred_element_type=jnp.float32)]
    all_gather x16 -> x0, waiting for transfers between devices: 272 us -> none  [the longest x2 90.8 us: local(): lax.all_gather(pieces[8], 'grp', axis=0, tiled=True)]
    pallas_call x0 -> x4, Pallas kernels: none -> 188 us  [the longest x2 115 us: run_bwd(): pl.pallas_call(bwd_kernel, out_shape=[jax.ShapeDtypeStruct(s, t) for s, t...]
    psum x1 -> x2, waiting for transfers between devices: 351 us -> 510 us  [the longest x1 392 us: reduce_big(): return lax.psum(total, 'rep')]
    unnamed x39 -> x2, waiting for transfers between devices: 158 us -> 0.03 us
    dynamic_slice x0 -> x20, local copies, waits for them, and re-layouts: none -> 76.6 us  [the longest x8 60.9 us: pick(): return lax.dynamic_index_in_dim(value, index, axis, keepdims=False)]
  transfers between devices with their start and end apart: 36 -> 18, of which waited for: 27 -> 5; matrix products, arithmetic and copies ran while one was open for 15% -> 15% of each run, Pallas kernels for 0% -> 0%
where the time goes in v1:
time: 1490 us
  waiting for transfers between devices  898 us (60%)
  local copies, waits for them, and re-layouts  191 us (13%)
  Pallas kernels  188 us (13%)
  blocking collectives  92.2 us (6%)
  other arithmetic  84.2 us (6%)
  starting transfers between devices  17.3 us (1%)
  between operations  15.1 us (1%)
    psum x1, waiting for transfers between devices, reduce_big(): return lax.psum(total, 'rep')  392 us
    ppermute x16, waiting for transfers between devices, swap(): return lax.ppermute(value, 'grp', [(i, i ^ bit) for i in range(4)])  388 us
    psum x1, waiting for transfers between devices, local(): lax.psum(jnp.concatenate([gvec, spread(gb), spread(gu)], axis=1), ('rep',...  118 us
    pallas_call x2, Pallas kernels, run_bwd(): pl.pallas_call(bwd_kernel, out_shape=[jax.ShapeDtypeStruct(s, t) for s, t...  115 us
    all_gather x1, blocking collectives, local(): packed = lax.all_gather(jnp.concatenate(smalls, axis=1), 'grp', axis=0)  92.2 us
    pallas_call x2, Pallas kernels, run_fwd(): pl.pallas_call(fwd_kernel, out_shape=[jax.ShapeDtypeStruct(s, t) for s, t...  72.3 us
    dynamic_slice x8, local copies, waits for them, and re-layouts, pick(): return lax.dynamic_index_in_dim(value, index, axis, keepdims=False)  60.9 us
  transfers between devices with their start and end apart: 18, of which 5 were waited for; matrix products, arithmetic and copies ran while one was open for 15% of the time, Pallas kernels for 0%

profile of v1, /device:TPU:0, one launch (start us, length us, event | category | flops | bytes accessed | tf_op | source)
XLA Modules:
  0.0 1486.1 jit_solution(6874480323934187954)
XLA Ops:
  7.3 5.1 constant_dynamic-slice_fusion.13
  13.2 2.9 collective-permute-start
  16.1 7.6 reshape.222
  23.7 23.1 %dynamic-slice_reduce_fusion.3 = (bf16[2,256,3,2,256]{4,3,2,1,0:T(2,128)(2,1)}, bf16[2,256,3,2,256]{4,3,2,1,0:T(2,128)(2,1)}) fusion(bf16[2,256,3,2,2,256]{5,4,3,2,1,0:T(2,128)(2,1)S(1)} %reshape.222, s32[]{:T(128)S(6)} %select_n.202, s32[]{:T(128)S(6)} %select_n.206), kind=kLoop, calls=%fused_computation.39 | loop fusion | bytes 6291464 | tf_op jit(solution)/shard_map/jit(dynamic_index_in_dim)/dynamic_slice | solution.py:378
  46.8 4.8 reshape.224
  51.6 7.9 reshape.225
  59.6 32.1 %dynamic-slice_reduce_fusion.1 = (bf16[2,256,2,1024]{3,2,1,0:T(2,128)(2,1)S(1)}, bf16[2,256,2,1024]{3,2,1,0:T(2,128)(2,1)}) fusion(bf16[2,256,1,2,2,1024]{5,4,3,1,0,2:T(2,128)(2,1)} %reshape.225, s32[]{:T(128)S(6)} %select_n.202, s32[]{:T(128)S(6)} %select_n.206), kind=kLoop, calls=%fused_computation.30 | loop fusion | bytes 8388616 | tf_op jit(solution)/shard_map/jit(dynamic_index_in_dim)/dynamic_slice | solution.py:378
  91.7 4.5 reshape.227
  98.7 92.2 %all-gather.1 = bf16[4,2,3072]{2,1,0:T(2,128)(2,1)S(1)} all-gather(bf16[1,2,3072]{2,1,0:T(2,128)(2,1)S(1)} %bitcast.129), channel_id=2, replica_groups=mesh['rep'=8,'grp'=4] {'grp'}, dimensions={0}, use_global_device_ids=true | all-gather | bytes 61440 | tf_op jit(solution)/shard_map/all_gather | solution.py:412
  192.1 5.0 reshape.223
  197.1 2.8 reshape.226
  202.9 3.6 maximum_select_fusion.5
  209.4 4.9 maximum_select_fusion.3
  221.5 62.8 %collective-permute-done.8 = bf16[145,1024]{1,0:T(8,128)(2,1)} collective-permute-done((bf16[145,1024]{1,0:T(8,128)(2,1)}, bf16[145,1024]{1,0:T(8,128)(2,1)}, u32[]{:S(2)}, u32[]{:S(2)}) %collective-permute-start.8) | collective-permute-done | bytes 296992 | tf_op jit(solution)/shard_map/ppermute | solution.py:374
  286.6 2.6 maximum_select_fusion.7
  290.7 6.0 maximum_select_fusion.1
  296.7 3.8 slice_bitcast_fusion
  300.5 4.6 maximum_select_fusion.2
  305.1 3.1 slice_bitcast_fusion.4
  308.2 65.4 %collective-permute-done.5 = bf16[2,512,2048]{2,1,0:T(8,128)(2,1)} collective-permute-done((bf16[2,512,2048]{2,1,0:T(8,128)(2,1)}, bf16[2,512,2048]{2,1,0:T(8,128)(2,1)}, u32[]{:S(2)}, u32[]{:S(2)}) %collective-permute-start.5) | collective-permute-done | bytes 4194336 | tf_op jit(solution)/shard_map/ppermute | solution.py:374
  373.6 8.2 maximum_select_fusion
  381.8 3.9 slice_bitcast_fusion.1
  386.5 36.3 %layer_fwd.2 = (f32[304,1024]{1,0:T(8,128)}, f32[304,1024]{1,0:T(8,128)}, bf16[608,1024]{1,0:T(8,128)(2,1)}, bf16[608,1536]{1,0:T(8,128)(2,1)}, bf16[608,512]{1,...) custom-call(f32[304,1024]{1,0:T(8,128)} %fusion.15.x_ref, ...), custom_call_target="tpu_custom_call" | custom-call | flops 8000000000 | bytes 20000000 | tf_op jit(solution)/shard_map/layer_fwd/pallas_call | solution.py:328
  422.9 36.0 %layer_fwd.3 = (f32[304,1024]{1,0:T(8,128)}, f32[304,1024]{1,0:T(8,128)}, bf16[608,1024]{1,0:T(8,128)(2,1)}, bf16[608,1536]{1,0:T(8,128)(2,1)}, bf16[608,512]{1,...) custom-call(f32[304,1024]{1,0:T(8,128)} %get-tuple-element.46.x_ref, ...), custom_call_target="tpu_custom_call" | custom-call | flops 8000000000 | bytes 20000000 | tf_op jit(solution)/shard_map/layer_fwd/pallas_call | solution.py:328
  458.9 57.6 %layer_bwd.2 = (f32[304,1024]{1,0:T(8,128)}, bf16[1024,1536]{1,0:T(8,128)(2,1)}, bf16[512,1024]{1,0:T(8,128)(2,1)}, bf16[1024,2048]{1,0:T(8,128)(2,1)}, bf16[204...) custom-call(f32[304,1024]{1,0:T(8,128)} %convert_multiply_fusion.g3_ref, ...), custom_call_target="tpu_custom_call" | custom-call | flops 16999999488 | bytes 40000000 | tf_op jit(solution)/shard_map/layer_bwd/pallas_call | solution.py:354
  516.5 57.7 %layer_bwd.3 = (f32[304,1024]{1,0:T(8,128)}, bf16[1024,1536]{1,0:T(8,128)(2,1)}, bf16[512,1024]{1,0:T(8,128)(2,1)}, bf16[1024,2048]{1,0:T(8,128)(2,1)}, bf16[204...) custom-call(f32[304,1024]{1,0:T(8,128)} %get-tuple-element.55.g3_ref, ...), custom_call_target="tpu_custom_call" | custom-call | flops 16999999488 | bytes 40000000 | tf_op jit(solution)/shard_map/layer_bwd/pallas_call | solution.py:354
  574.3 5.0 fusion.2
  583.1 4.7 fusion
  592.1 259.9 %collective-permute-done.12 = bf16[2,256,1024]{2,1,0:T(8,128)(2,1)} collective-permute-done((bf16[2,256,1024]{2,1,0:T(8,128)(2,1)}, bf16[2,256,1024]{2,1,0:T(8,128)(2,1)}, u32[]{:S(2)}, u32[]{:S(2)}) %collective-permute-start.12) | collective-permute-done | bytes 1048608 | tf_op jit(solution)/shard_map/ppermute | solution.py:374
  851.9 2.9 add_convert_fusion.3
  854.8 4.6 add_convert_fusion.2
  860.4 4.6 add_convert_fusion.1
  865.0 4.6 add_convert_fusion
  879.4 392.5 %all-reduce.16.cloned.1.call-done = (bf16[2,512,1536]{2,1,0:T(8,128)(2,1)}, bf16[2,256,1024]{2,1,0:T(8,128)(2,1)}, bf16[2,512,2048]{2,1,0:T(8,128)(2,1)}, bf16[2,1024,1024]{2,1,0:T(8,128)(2,1)}) async-done(((bf16[2,512,1536]{2,1,0:T(8,128)(2,1)}, bf16[2,256,1024]{2,1,0:T(8,128)(2,1)}, bf16[2,512,2048]{2,1,0:T(8,128)(2,1)}, bf16[2,1024,1024]{2,1,0:T(8,128)(2,1)}), (bf16[2,512,1536]{2,1,0:T(8,128)(2,1)}, ...) | async-done | bytes 12582928 | tf_op jit(solution)/shard_map/psum | solution.py:471
  1271.9 4.1 constant_dynamic-slice_fusion.3
  1280.7 117.8 %all-reduce.14.cloned.1.call-done = f32[2,12288]{1,0:T(2,128)} async-done(((f32[2,12288]{1,0:T(2,128)}), f32[2,12288]{1,0:T(2,128)}) %all-reduce.14.cloned.1.call-update) | async-done | bytes 98320 | tf_op jit(solution)/shard_map/psum | solution.py:495
  1409.6 2.6 copy.129
  1412.2 2.6 copy.130
  1418.8 3.0 copy.136
  1421.8 6.6 convert_element_type.231
  1428.4 4.6 stack_reshape.26
  1434.9 2.9 fusion.7
  1437.8 6.6 copy.134
  1444.3 6.6 copy.143
  1450.9 4.5 stack.145
  1457.6 3.8 fusion.4
  1461.4 8.7 copy.140
  1470.1 8.9 copy.144
  (195 shorter events, 64.6 us)
Async XLA Ops:
  7.2 184.2 %copy-start = (s32[2,580]{1,0:T(2,128)S(1)}, s32[2,580]{1,0:T(2,128)}, u32[]{:S(2)}) copy-start(s32[2,580]{1,0:T(2,128)} %param.19) | copy-start | bytes 13924
  7.2 1264.7 %all-reduce.16.cloned.1.call-start = ((), (), s32[]{:S(2)}) async-start(), calls=%async_computation.1 | async-start | bytes 25165824 | tf_op jit(solution)/shard_map/psum | solution.py:471
  13.2 201.1 %collective-permute-start = (bf16[145,1024]{1,0:T(8,128)(2,1)}, bf16[145,1024]{1,0:T(8,128)(2,1)S(1)}, u32[]{:S(2)}, u32[]{:S(2)}) collective-permute-start(bf16[145,1024]{1,0:T(8,128)(2,1)} %bitcast.96), channel_id=1, source_target_pairs={{0,2},{1,3},{2,0},{3,1},{4,6},{5,7},{6,4},{7,5},{8,10},{9,11},{10,... | collective-permute-start | bytes 890888 | tf_op jit(solution)/shard_map/ppermute | solution.py:374
  51.6 151.3 %collective-permute-start.1 = (bf16[2,256,1536]{2,1,0:T(8,128)(2,1)}, bf16[2,256,1536]{2,1,0:T(8,128)(2,1)}, u32[]{:S(2)}, u32[]{:S(2)}) collective-permute-start(bf16[2,256,1536]{2,1,0:T(8,128)(2,1)} %reshape.224), channel_id=1, source_target_pairs={{0,1},{1,0},{2,3},{3,2},{4,5},{5,4},{6,7},{7,6},{8,9},{9,8},{10,11... | collective-permute-start | bytes 4718600 | tf_op jit(solution)/shard_map/ppermute | solution.py:374
  51.6 235.0 %collective-permute-start.3 = (bf16[2,256,1024]{2,1,0:T(8,128)(2,1)}, bf16[2,256,1024]{2,1,0:T(8,128)(2,1)}, u32[]{:S(2)}, u32[]{:S(2)}) collective-permute-start(bf16[2,256,1024]{2,1,0:T(8,128)(2,1)} %param.24), channel_id=1, source_target_pairs={{0,2},{1,3},{2,0},{3,1},{4,6},{5,7},{6,4},{7,5},{8,10},{9,11},{10,... | collective-permute-start | bytes 3145736 | tf_op jit(solution)/shard_map/ppermute | solution.py:374
  91.7 6.8 copy-start.23
  91.7 6.8 copy-start.24
  91.7 6.9 copy-start.25
  91.7 6.9 copy-start.26
  91.7 6.9 copy-start.27
  91.7 6.9 copy-start.28
  91.7 6.9 copy-start.22
  91.7 6.9 copy-start.21
  91.7 99.8 %copy-start.29 = (s32[2]{0:T(128)S(1)}, s32[2]{0:T(128)}, u32[]{:S(2)}) copy-start(s32[2]{0:T(128)} %param.18) | copy-start | bytes 28
  96.2 103.7 %copy-start.13 = (bf16[1,145,1024]{2,0,1:T(2,128)(2,1)S(1)}, bf16[1,145,1024]{2,0,1:T(2,128)(2,1)}, u32[]{:S(2)}) copy-start(bf16[1,145,1024]{2,0,1:T(2,128)(2,1)} %get-tuple-element.173) | copy-start | bytes 890884
  96.2 112.8 %collective-permute-start.4 = (bf16[2,256,2048]{2,1,0:T(8,128)(2,1)}, bf16[2,256,2048]{2,1,0:T(8,128)(2,1)}, u32[]{:S(2)}, u32[]{:S(2)}) collective-permute-start(bf16[2,256,2048]{2,1,0:T(8,128)(2,1)} %reshape.227), channel_id=1, source_target_pairs={{0,1},{1,0},{2,3},{3,2},{4,5},{5,4},{6,7},{7,6},{8,9},{9,8},{10,11... | collective-permute-start | bytes 6291464 | tf_op jit(solution)/shard_map/ppermute | solution.py:374
  96.8 193.9 %collective-permute-start.6 = (bf16[2,1024,1024]{2,1,0:T(8,128)(2,1)}, bf16[2,1024,1024]{2,1,0:T(8,128)(2,1)}, u32[]{:S(2)}, u32[]{:S(2)}) collective-permute-start(bf16[2,1024,1024]{2,1,0:T(8,128)(2,1)} %param.30), channel_id=1, source_target_pairs={{0,2},{1,3},{2,0},{3,1},{4,6},{5,7},{6,4},{7,5},{8,10},{9,11},{10,... | collective-permute-start | bytes 12582920 | tf_op jit(solution)/shard_map/ppermute | solution.py:374
  192.1 10.2 copy-start.20
  200.8 8.5 copy-start.9
  206.5 94.0 %collective-permute-start.2 = (bf16[2,512,1536]{2,1,0:T(8,128)(2,1)S(1)}, bf16[2,512,1536]{2,1,0:T(8,128)(2,1)}, u32[]{:S(2)}, u32[]{:S(2)}) collective-permute-start(bf16[2,512,1536]{2,1,0:T(8,128)(2,1)S(1)} %maximum_select_fusion.5), channel_id=1, source_target_pairs={{0,2},{1,3},{2,0},{3,1},{4,6},{5,7},{6,4},{7,5},{8,10},{9,11},{10,... | collective-permute-start | bytes 9437192 | tf_op jit(solution)/shard_map/ppermute | solution.py:374
  209.0 75.3 %collective-permute-start.8 = (bf16[145,1024]{1,0:T(8,128)(2,1)}, bf16[145,1024]{1,0:T(8,128)(2,1)}, u32[]{:S(2)}, u32[]{:S(2)}) collective-permute-start(bf16[145,1024]{1,0:T(8,128)(2,1)} %bitcast.94), channel_id=1, source_target_pairs={{0,2},{1,3},{2,0},{3,1},{4,6},{5,7},{6,4},{7,5},{8,10},{9,11},{10,... | collective-permute-start | bytes 890888 | tf_op jit(solution)/shard_map/ppermute | solution.py:374
  214.3 1.9 copy-start.17
  214.3 159.3 %collective-permute-start.5 = (bf16[2,512,2048]{2,1,0:T(8,128)(2,1)}, bf16[2,512,2048]{2,1,0:T(8,128)(2,1)}, u32[]{:S(2)}, u32[]{:S(2)}) collective-permute-start(bf16[2,512,2048]{2,1,0:T(8,128)(2,1)} %maximum_select_fusion.3), channel_id=1, source_target_pairs={{0,2},{1,3},{2,0},{3,1},{4,6},{5,7},{6,4},{7,5},{8,10},{9,11},{10,... | collective-permute-start | bytes 12582920 | tf_op jit(solution)/shard_map/ppermute | solution.py:374
  219.2 67.4 %copy-start.15 = (bf16[2,256,1024]{2,1,0:T(8,128)(2,1)S(1)}, bf16[2,256,1024]{2,1,0:T(8,128)(2,1)}, u32[]{:S(2)}) copy-start(bf16[2,256,1024]{2,1,0:T(8,128)(2,1)} %param.24) | copy-start | bytes 3145732
  286.6 4.1 copy-start.11
  574.2 6.7 copy-start.6
  574.2 6.7 copy-start.7
  579.2 280.2 %collective-permute-start.13 = (bf16[2,512,2048]{2,1,0:T(8,128)(2,1)}, bf16[2,512,2048]{2,1,0:T(8,128)(2,1)}, u32[]{:S(2)}, u32[]{:S(2)}) collective-permute-start(bf16[2,512,2048]{2,1,0:T(8,128)(2,1)} %fusion.2), channel_id=1, source_target_pairs={{0,2},{1,3},{2,0},{3,1},{4,6},{5,7},{6,4},{7,5},{8,10},{9,11},{10,... | collective-permute-start | bytes 12582920 | tf_op jit(solution)/shard_map/ppermute | solution.py:374
  582.9 272.0 %collective-permute-start.10 = (bf16[2,512,1536]{2,1,0:T(8,128)(2,1)}, bf16[2,512,1536]{2,1,0:T(8,128)(2,1)}, u32[]{:S(2)}, u32[]{:S(2)}) collective-permute-start(bf16[2,512,1536]{2,1,0:T(8,128)(2,1)} %fusion.5), channel_id=1, source_target_pairs={{0,2},{1,3},{2,0},{3,1},{4,6},{5,7},{6,4},{7,5},{8,10},{9,11},{10,... | collective-permute-start | bytes 9437192 | tf_op jit(solution)/shard_map/ppermute | solution.py:374
  587.8 277.2 %collective-permute-start.15 = (bf16[2,1024,1024]{2,1,0:T(8,128)(2,1)}, bf16[2,1024,1024]{2,1,0:T(8,128)(2,1)}, u32[]{:S(2)}, u32[]{:S(2)}) collective-permute-start(bf16[2,1024,1024]{2,1,0:T(8,128)(2,1)} %fusion), channel_id=1, source_target_pairs={{0,2},{1,3},{2,0},{3,1},{4,6},{5,7},{6,4},{7,5},{8,10},{9,11},{10,... | collective-permute-start | bytes 12582920 | tf_op jit(solution)/shard_map/ppermute | solution.py:374
  591.8 260.1 %collective-permute-start.12 = (bf16[2,256,1024]{2,1,0:T(8,128)(2,1)}, bf16[2,256,1024]{2,1,0:T(8,128)(2,1)}, u32[]{:S(2)}, u32[]{:S(2)}) collective-permute-start(bf16[2,256,1024]{2,1,0:T(8,128)(2,1)} %fusion.12), channel_id=1, source_target_pairs={{0,2},{1,3},{2,0},{3,1},{4,6},{5,7},{6,4},{7,5},{8,10},{9,11},{10,... | collective-permute-start | bytes 3145736 | tf_op jit(solution)/shard_map/ppermute | solution.py:374
  592.1 262.8 %copy-start.8 = (bf16[1024,1536]{1,0:T(8,128)(2,1)S(1)}, bf16[1024,1536]{1,0:T(8,128)(2,1)}, u32[]{:S(2)}) copy-start(bf16[1024,1536]{1,0:T(8,128)(2,1)} %get-tuple-element.70) | copy-start | bytes 9437188
  854.8 4.6 copy-start.3
  854.8 5.5 copy-start.5
  859.4 5.6 copy-start.2
  859.4 5.6 copy-start.4
  869.6 1.3 copy-start.14
  869.6 8.9 copy-start.18
  869.6 9.0 copy-start.19
  869.6 528.9 %all-reduce.14.cloned.1.call-start = ((), (), s32[]{:S(2)}) async-start(), calls=%async_computation | async-start | bytes 196608 | tf_op jit(solution)/shard_map/psum | solution.py:495
  871.8 533.6 %collective-permute-start.7 = (bf16[145,1024]{1,0:T(8,128)(2,1)}, bf16[145,1024]{1,0:T(8,128)(2,1)}, u32[]{:S(2)}, u32[]{:S(2)}) collective-permute-start(bf16[145,1024]{1,0:T(8,128)(2,1)} %get-tuple-element.171), channel_id=1, source_target_pairs={{0,2},{1,3},{2,0},{3,1},{4,6},{5,7},{6,4},{7,5},{8,10},{9,11},{10,... | collective-permute-start | bytes 890888 | tf_op jit(solution)/shard_map/ppermute | solution.py:374
  1271.9 4.1 copy-start.12
  1276.0 174.9 %collective-permute-start.14 = (bf16[2,256,2048]{2,1,0:T(8,128)(2,1)}, bf16[2,256,2048]{2,1,0:T(8,128)(2,1)}, u32[]{:S(2)}, u32[]{:S(2)}) collective-permute-start(bf16[2,256,2048]{2,1,0:T(8,128)(2,1)} %get-tuple-element.163), channel_id=1, source_target_pairs={{0,1},{1,0},{2,3},{3,2},{4,5},{5,4},{6,7},{7,6},{8,9},{9,8},{10,11... | collective-permute-start | bytes 6291464 | tf_op jit(solution)/shard_map/ppermute | solution.py:374
  1277.9 150.6 %collective-permute-start.11 = (bf16[2,256,1536]{2,1,0:T(8,128)(2,1)}, bf16[2,256,1536]{2,1,0:T(8,128)(2,1)}, u32[]{:S(2)}, u32[]{:S(2)}) collective-permute-start(bf16[2,256,1536]{2,1,0:T(8,128)(2,1)} %get-tuple-element.165), channel_id=1, source_target_pairs={{0,1},{1,0},{2,3},{3,2},{4,5},{5,4},{6,7},{7,6},{8,9},{9,8},{10,11... | collective-permute-start | bytes 4718600 | tf_op jit(solution)/shard_map/ppermute | solution.py:374
  1279.2 128.9 %collective-permute-start.9 = (bf16[145,1024]{1,0:T(8,128)(2,1)}, bf16[145,1024]{1,0:T(8,128)(2,1)S(1)}, u32[]{:S(2)}, u32[]{:S(2)}) collective-permute-start(bf16[145,1024]{1,0:T(8,128)(2,1)} %get-tuple-element.169), channel_id=1, source_target_pairs={{0,2},{1,3},{2,0},{3,1},{4,6},{5,7},{6,4},{7,5},{8,10},{9,11},{10,... | collective-permute-start | bytes 890888 | tf_op jit(solution)/shard_map/ppermute | solution.py:374
  1408.2 6.6 copy-start.16
  1433.0 1.9 copy-start.10
  1470.1 8.9 copy-start.1
Sparse Core Ops, SparseCore 0:
  869.7 402.0 all-reduce.15
  1278.9 119.5 all-reduce.13

commit v2 on v1

--- a/solution.py
+++ b/solution.py
@@ -12,7 +12,10 @@
 F32 = jnp.float32
 BF16 = jnp.bfloat16
 VMEM_LIMIT = 62 * 2**20
-G1, B1, BOUT, G2, B2, BDOWN = range(6)
+WIDE = 256
+STEP = 16
+G1, B1, BOUT, G2, B2, BDOWN, BQV, BUP = 0, 1, 2, 3, 4, 5, 6, 8
+SMALL = 16
 
 
 def nn(a, b):
@@ -27,8 +30,12 @@
     return lax.dot_general(a, b, (((0,), (0,)), ((), ())), preferred_element_type=F32)
 
 
-def cols(j, width):
-    return pl.ds(pl.multiple_of(j * width, width), width)
+def span(start, size):
+    return pl.ds(pl.multiple_of(start, size), size)
+
+
+def cols(j, width=WIDE):
+    return span(j * width, width)
 
 
 def loop(count, body):
@@ -39,12 +46,433 @@
     lax.fori_loop(0, count, step, 0)
 
 
+class Place:
+    def __init__(self):
+        self.rep, self.grp = lax.axis_index("rep"), lax.axis_index("grp")
+        rep, grp = self.rep, self.grp
+        self.x, self.c = grp // 2, grp % 2
+        self.y, self.z = rep % 2, (rep // 2) % 4
+        self.zlow = self.z % 2
+        core, chip = 1 - 2 * self.c, 2 - 4 * self.x
+        self.sib = (rep, grp + core)
+        self.xn = (rep, grp + chip)
+        self.xd = (rep, grp + chip + core)
+        yrep = rep + 1 - 2 * self.y
+        self.yn = (yrep, grp)
+        self.yd = (yrep, grp + core)
+        self.zn = (rep + 2 - 4 * self.zlow, grp)
+        self.inner = jnp.logical_or(self.z == 1, self.z == 2)
+        self.outer = jnp.logical_not(self.inner)
+        self.mid = (rep + 6 - 4 * self.z, grp)
+
+
+def greet(peers):
+    barrier = pltpu.get_barrier_semaphore()
+    for peer in peers:
+        pl.semaphore_signal(barrier, inc=1, device_id=peer, device_id_type=MESH)
+    pl.semaphore_wait(barrier, len(peers))
+
+
+def remote(src, dst, send, recv, peer):
+    return pltpu.make_async_remote_copy(
+        src_ref=src, dst_ref=dst, send_sem=send, recv_sem=recv, device_id=peer, device_id_type=MESH
+    )
+
+
+def settle(ref, sem):
+    pltpu.make_async_copy(ref, ref, sem).wait()
+
+
+def norm_rows(v):
+    mean = jnp.mean(v, axis=-1, keepdims=True)
+    off = v - mean
+    rstd = lax.rsqrt(jnp.mean(off * off, axis=-1, keepdims=True) + 1e-6)
+    return off * rstd, rstd
+
+
+def scores_t(k2, qa, mask):
+    st = jnp.where(mask, nt(k2, qa), -1e9)
+    top = jnp.max(st, axis=0, keepdims=True)
+    e = jnp.exp(st - top)
+    return e * (1.0 / jnp.sum(e, axis=0, keepdims=True))
+
+
+def half_lanes(v, a):
+    lane = lax.broadcasted_iota(jnp.int32, v.shape, 1)
+    return jnp.where((lane >= HEAD) == (a == 1), v, jnp.zeros_like(v))
+
+
+def chip_flags(at, tv_ref, rows, seq):
+    lengths = jnp.sum(tv_ref[...], axis=1, keepdims=True)
+    length = jnp.where(at.x == 0, lengths[0:1, :], lengths[1:2, :])
+    row = lax.broadcasted_iota(jnp.int32, (2 * rows, 1), 0)
+    core = jnp.where(row < rows, at.c, 1 - at.c)
+    row = jnp.where(row < rows, row, row - rows)
+    block = rows // 2
+    chip = jnp.where(row < block, at.x, 1 - at.x)
+    row = jnp.where(row < block, row, row - block)
+    slot = (2 * chip + core) * seq + row
+    return jnp.logical_and(row < seq, slot < length)
+
+
+class Plan:
+    def __init__(self):
+        self.now, self.events, self.done = 0.0, [], set()
+
+    def add(self, when, name, action):
+        self.events.append((when, name, action))
+
+    def order(self):
+        self.events.sort(key=lambda e: e[0])
+
+    def poll(self):
+        while self.events and self.events[0][0] <= self.now:
+            self.fire()
+
+    def fire(self):
+        when, name, action = self.events.pop(0)
+        self.now = max(self.now, when)
+        action()
+        self.done.add(name)
+
+    def need(self, name):
+        while name not in self.done:
+            self.fire()
+
+    def spend(self, us):
+        self.now += us
+        self.poll()
+
+
+KINDS = ("qkv", "out", "up", "down")
+
+
+def fwd_kernel(
+    seq, tok_ref, cot_ref, pack_ref, tv_ref, wqkv_in, wout_in, wup_in, wdown_in,
+    vqkv, vout, vup, vdown, xs, x2s, h1s, qkvs, as_, h2s, zs, gps, cot_out, act_out, vec_out,
+    wqkv, wout, wup, wdown, x_ref, x2_ref, h1, qkv, att, h2, z, gp, put, got, tok, vec, bup,
+    s_rx, s_ry, s_rz, s_ra, s_rb, s_rs, s_loc, s_send, s_core, r_core, s_save, s_misc, r_misc,
+):
+    at = Place()
+    layers = vqkv.shape[0]
+    rows, d = x_ref.shape
+    block = rows // 2
+    hc, f = att.shape[1], z.shape[1]
+    own, other = pl.ds(0, rows), pl.ds(rows, rows)
+    x, c = at.x, at.c
+    quarter = at.y * 2 + at.zlow
+    ins = dict(qkv=wqkv_in, out=wout_in, up=wup_in, down=wdown_in)
+    full = dict(qkv=wqkv, out=wout, up=wup, down=wdown)
+    saves = dict(qkv=vqkv, out=vout, up=vup, down=vdown)
+    runs = dict(qkv=(d // 4, 6), up=(f // 2, 2))
+    plan = Plan()
+    index = {}
+    for l in range(layers):
+        for kind in KINDS:
+            index[l, kind] = len(index)
+
+    greet((at.sib, at.xn, at.xd, at.yn, at.zn))
+
+    first = [
+        remote(tok_ref.at[1 - x], tok.at[1], s_misc.at[0], r_misc.at[0], at.xn),
+        pltpu.make_async_copy(tok_ref.at[x], tok.at[0], s_misc.at[3]),
+    ]
+    here = vec.at[:, span(at.grp * WIDE, WIDE)]
+    first += [
+        pltpu.make_async_copy(pack_ref, here, s_misc.at[4]),
+        remote(pack_ref, here, s_misc.at[5], r_misc.at[5], at.sib),
+        remote(pack_ref, here, s_misc.at[6], r_misc.at[6], at.xn),
+        remote(pack_ref, here, s_misc.at[7], r_misc.at[7], at.xd),
+    ]
+    for copy in first:
+        copy.start()
+
+    def launch(l, kind):
+        i = index[l, kind]
+        src, dst = ins[kind].at[l], full[kind].at[l]
+        n = src.shape[0]
+        q = n // 4
+        part = span(quarter * q, q)
+        if kind in runs:
+            width, count = runs[kind]
+            mine = 2 * x + c
+            for j in range(count):
+                to = pl.ds(j * width, width)
+                keep = span((2 * j + c) * width, width)
+                give = span((2 * j + 1 - c) * width, width)
+                remote(src.at[part, keep], dst.at[mine, part, to], s_send.at[i], s_rx.at[i], at.xn).start()
+                remote(src.at[part, give], dst.at[mine, part, to], s_send.at[i], s_rx.at[i], at.xd).start()
+            for j in range(count):
+                to = pl.ds(j * width, width)
+                keep = span((2 * j + c) * width, width)
+                give = span((2 * j + 1 - c) * width, width)
+                remote(src.at[:, give], dst.at[mine, :, to], s_send.at[i], s_rs.at[i], at.sib).start()
+                pltpu.make_async_copy(src.at[:, keep], dst.at[mine, :, to], s_loc.at[i]).start()
+        else:
+            remote(src.at[part], dst.at[x, part], s_send.at[i], s_rx.at[i], at.xn).start()
+            pltpu.make_async_copy(src, dst.at[x], s_loc.at[i]).start()
+
+    def theirs(l, kind, part):
+        dst = full[kind].at[l]
+        if kind in runs:
+            return dst.at[span(2 * (1 - x), 2), part]
+        return dst.at[pl.ds(1 - x, 1), part]
+
+    def part_of(kind, y, zlow, half=None):
+        q = full[kind].shape[2] // 4
+        if half is None:
+            return span((2 * y + zlow) * q, q)
+        return span((4 * y + 2 * zlow + half) * (q // 2), q // 2)
+
+    def relay1(l, kind):
+        i = index[l, kind]
+        piece = theirs(l, kind, part_of(kind, at.y, at.zlow))
+        settle(piece, s_rx.at[i])
+        remote(piece, piece, s_send.at[i], s_ry.at[i], at.yn).start()
+        remote(piece, piece, s_send.at[i], s_rz.at[i], at.zn).start()
+
+    def relay2(l, kind):
+        i = index[l, kind]
+        settle(theirs(l, kind, part_of(kind, 1 - at.y, at.zlow)), s_ry.at[i])
+        piece = theirs(l, kind, part_of(kind, 1 - at.y, at.zlow, 0))
+        remote(piece, piece, s_send.at[i], s_ra.at[i], at.zn).start()
+        settle(theirs(l, kind, part_of(kind, at.y, 1 - at.zlow)), s_rz.at[i])
+        piece = theirs(l, kind, part_of(kind, at.y, 1 - at.zlow, 1))
+        remote(piece, piece, s_send.at[i], s_rb.at[i], at.yn).start()
+
+    def ready(l, kind):
+        i = index[l, kind]
+        settle(theirs(l, kind, part_of(kind, 1 - at.y, 1 - at.zlow, 0)), s_ra.at[i])
+        settle(theirs(l, kind, part_of(kind, 1 - at.y, 1 - at.zlow, 1)), s_rb.at[i])
+        if kind in runs:
+            settle(full[kind].at[l, 0], s_rs.at[i])
+        settle(full[kind].at[l, 0], s_loc.at[i])
+        pltpu.make_async_copy(full[kind].at[l], saves[kind].at[l], s_loc.at[i]).start()
+
+    x_time, yz_time = 9.0, 16.0
+    for l in range(layers):
+        for kind in KINDS:
+            launch(l, kind)
+            mb = full[kind].shape[1] * full[kind].shape[2] * full[kind].shape[3] / 2**20
+            mb *= 2
+            x_time += mb / 4 / 0.094 * 1.05
+            plan.add(x_time + 1.5, ("r1", l, kind), functools.partial(relay1, l, kind))
+            yz_time = max(yz_time, x_time + 1.5)
+            plan.add(yz_time + mb / 4 / 0.094 + 1.5, ("r2", l, kind), functools.partial(relay2, l, kind))
+            yz_time += mb * 3 / 8 / 0.094 * 1.05
+            plan.add(yz_time + 4, ("ok", l, kind), functools.partial(ready, l, kind))
+    plan.order()
+    late = [
+        remote(cot_ref.at[1 - x], cot_out.at[1], s_misc.at[1], r_misc.at[1], at.xn),
+        pltpu.make_async_copy(cot_ref.at[x], cot_out.at[0], s_misc.at[8]),
+    ]
+    for copy in late:
+        copy.start()
+
+    first[1].wait()
+    first[2].wait()
+    for copy in (first[0], *first[3:]):
+        copy.wait()
+    for i in range(2):
+        for j in range(block // STEP):
+            x_ref[pl.ds(i * block + j * STEP, STEP), :] = tok[i, pl.ds(j * STEP, STEP), :].astype(F32)
+    vec_save = pltpu.make_async_copy(vec, vec_out, s_misc.at[9])
+    vec_save.start()
+    for l in range(layers):
+        for j in range(f // WIDE):
+            half, sub = divmod(j, f // WIDE // 2)
+            bup[l:l + 1, pl.ds(j * WIDE, WIDE)] = vec[
+                l * SMALL + BUP + sub:l * SMALL + BUP + sub + 1, span((2 * half + c) * WIDE, WIDE)
+            ]
+    mask = chip_flags(at, tv_ref, rows, seq)
+    plan.now = 12.0
+    plan.poll()
+
+    def save(src, dst, slot):
+        copy = pltpu.make_async_copy(src, dst, s_save.at[slot])
+        copy.start()
+        return copy
+
+    pending = {}
+    for l in range(layers):
+        def row(name, l=l):
+            return vec[l * SMALL + name:l * SMALL + name + 1, :]
+
+        def norm_out(src_ref, dst_ref, gain, shift, l=l):
+            for i in range(rows // STEP):
+                r = pl.ds(i * STEP, STEP)
+                hat, _ = norm_rows(src_ref[r, :])
+                dst_ref[r, :] = (hat * row(gain) + row(shift)).astype(BF16)
+
+        def weight(kind, cs, l=l):
+            w = full[kind][l, :, :, cs]
+            return w.reshape(w.shape[0] * w.shape[1], w.shape[2])
+
+        norm_out(x_ref, h1, G1, B1)
+        cp = remote(h1.at[own], h1.at[other], s_core.at[0], r_core.at[0], at.sib)
+        cp.start()
+        x_saved = save(x_ref, xs.at[l], 0)
+        plan.spend(2)
+        plan.need(("ok", l, "qkv"))
+        if l:
+            pending["qkv"].wait()
+        bq = jnp.where(c == 0, row(BQV), vec[l * SMALL + BQV + 1:l * SMALL + BQV + 2, :])
+        scale = HEAD ** -0.5
+        parts = (
+            (0, bq[:, :hc] * scale, scale), (hc, jnp.zeros((1, hc), F32), 1.0), (2 * hc, bq[:, hc:], 1.0)
+        )
+
+        def qkv_rows(r, l=l, parts=parts):
+            for base, bias, factor in parts:
+                for j in range(hc // WIDE):
+                    cs = pl.ds(base + j * WIDE, WIDE)
+                    out = nn(h1[r, :], weight("qkv", cs))
+                    qkv[r, cs] = (out * factor + bias[:, j * WIDE:(j + 1) * WIDE]).astype(BF16)
+
+        qkv_rows(own)
+        plan.spend(2)
+        cp.wait()
+        qkv_rows(other)
+        h1_saved = save(h1, h1s.at[l], 1)
+        pending["qkv"] = save(qkv, qkvs.at[l], 2)
+        plan.spend(2)
+        if l:
+            pending["att"].wait()
+        for p in range(hc // 128):
+            q2 = qkv[:, p * 128:(p + 1) * 128]
+            k2 = qkv[:, hc + p * 128:hc + (p + 1) * 128]
+            v2 = qkv[:, 2 * hc + p * 128:2 * hc + (p + 1) * 128]
+            vt = v2.T
+            outs = []
+            for a in range(2):
+                pt = scores_t(k2, half_lanes(q2, a), mask)
+                outs.append(nn(vt[a * HEAD:(a + 1) * HEAD, :], pt.astype(BF16)))
+            att[:, p * 128:(p + 1) * 128] = jnp.concatenate(outs, axis=0).T.astype(BF16)
+            plan.spend(3)
+        pending["att"] = save(att, as_.at[l], 3)
+
+        def exchange(left, kind, base, bias, out, slot):
+            def far(j):
+                put[:, cols(j)] = nn(left[other, :], weight(kind, cols(j))).astype(BF16)
+
+            loop(d // WIDE, far)
+            cp = remote(put, got.at[slot], s_core.at[1], r_core.at[1], at.sib)
+            cp.start()
+
+            def near(j):
+                out[:, cols(j)] = nn(left[own, :], weight(kind, cols(j))) + base[:, cols(j)] + vec[
+                    l * SMALL + bias:l * SMALL + bias + 1, cols(j)
+                ]
+
+            loop(d // WIDE, near)
+            cp.wait()
+            out[...] += got[slot].astype(F32)
+
+        plan.need(("ok", l, "out"))
+        if l:
+            pending["x2"].wait()
+        exchange(att, "out", x_ref, BOUT, x2_ref, 0)
+        pending["x2"] = save(x2_ref, x2s.at[l], 4)
+        plan.spend(3)
+        norm_out(x2_ref, h2, G2, B2)
+        cp = remote(h2.at[own], h2.at[other], s_core.at[2], r_core.at[2], at.sib)
+        cp.start()
+        plan.spend(2)
+        plan.need(("ok", l, "up"))
+        if l:
+            pending["z"].wait()
+            pending["gp"].wait()
+
+        def up_rows(r):
+            def body(j):
+                u = nn(h2[r, :], weight("up", cols(j))) + bup[l:l + 1, cols(j)]
+                phi = 0.5 + 0.5 * lax.erf(u * 0.7071067811865476)
+                z[r, cols(j)] = (u * phi).astype(BF16)
+                gp[r, cols(j)] = (phi + u * jnp.exp(u * u * -0.5) * 0.3989422804014327).astype(BF16)
+
+            loop(f // WIDE, body)
+
+        up_rows(own)
+        plan.spend(4)
+        cp.wait()
+        up_rows(other)
+        h2_saved = save(h2, h2s.at[l], 5)
+        pending["z"] = save(z, zs.at[l], 6)
+        pending["gp"] = save(gp, gps.at[l], 7)
+        plan.spend(4)
+        plan.need(("ok", l, "down"))
+        for copy in (x_saved, h1_saved, h2_saved):
+            copy.wait()
+        exchange(z, "down", x2_ref, BDOWN, x_ref, 1)
+        plan.spend(4)
+
+    for i in range(2):
+        for j in range(block // STEP):
+            tok[i, pl.ds(j * STEP, STEP), :] = x_ref[pl.ds(i * block + j * STEP, STEP), :].astype(BF16)
+    act = [
+        remote(tok.at[1], act_out.at[x], s_misc.at[2], r_misc.at[2], at.xn),
+        pltpu.make_async_copy(tok.at[0], act_out.at[x], s_misc.at[10]),
+    ]
+    for copy in act:
+        copy.start()
+    for copy in (*act, *late, vec_save):
+        copy.wait()
+    for name in ("qkv", "att", "x2", "z", "gp"):
+        pending[name].wait()
+    for (l, kind), i in index.items():
+        settle(full[kind].at[l, pl.ds(0, 3 if kind in runs else 1)], s_send.at[i])
+        settle(full[kind].at[l], s_loc.at[i])
+
+
+ANY = pl.BlockSpec(memory_space=pl.ANY)
+VM = pl.BlockSpec(memory_space=pltpu.VMEM)
+
+
+def dma(*shape):
+    return pltpu.SemaphoreType.DMA(shape)
+
+
+def run_fwd(tok, cot, pack, tv, w_qkv, w_out, w_up, w_down, seq):
+    layers, n, d3 = w_qkv.shape
+    d = d3 // 3
+    hc, f = d // 2, 2 * w_down.shape[1]
+    block = tok.shape[1]
+    rows, both = 2 * block, 4 * block
+    weights = [(4, n, 3 * hc), (2, n, d), (4, n, f), (2, w_down.shape[1], d)]
+    acts = [
+        ((rows, d), F32), ((rows, d), F32), ((both, d), BF16), ((both, 3 * hc), BF16),
+        ((both, hc), BF16), ((both, d), BF16), ((both, f), BF16), ((both, f), BF16),
+    ]
+    shapes = [((layers, *s), BF16) for s in weights] + [((layers, *s), t) for s, t in acts]
+    shapes += [((2, block, d), BF16), ((2, block, d), BF16), ((layers * SMALL, d), F32)]
+    count = layers * len(KINDS)
+    return pl.pallas_call(
+        functools.partial(fwd_kernel, seq),
+        out_shape=[jax.ShapeDtypeStruct(s, t) for s, t in shapes],
+        in_specs=[ANY, ANY, VM, VM, ANY, ANY, ANY, ANY],
+        out_specs=[ANY] * len(shapes),
+        scratch_shapes=[pltpu.VMEM((layers, *s), BF16) for s in weights]
+        + [pltpu.VMEM(s, t) for s, t in acts]
+        + [
+            pltpu.VMEM((rows, d), BF16), pltpu.VMEM((2, rows, d), BF16),
+            pltpu.VMEM((2, block, d), BF16), pltpu.VMEM((layers * SMALL, d), F32), pltpu.VMEM((8, f), F32),
+        ]
+        + [dma(count)] * 8
+        + [dma(3), dma(3), dma(8), dma(11), dma(8)],
+        compiler_params=pltpu.CompilerParams(
+            collective_id=1, has_side_effects=True, vmem_limit_bytes=VMEM_LIMIT
+        ),
+        cost_estimate=pl.CostEstimate(flops=17 * 10**9, bytes_accessed=80 * 10**6, transcendentals=0),
+        name="forward",
+    )(tok, cot, pack, tv, w_qkv, w_out, w_up, w_down)
+
+
 def mates():
     rep, grp = lax.axis_index("rep"), lax.axis_index("grp")
     return (rep, grp + 1 - 2 * (grp % 2))
 
 
-def greet():
+def greet_mate():
     barrier = pltpu.get_barrier_semaphore()
     pl.semaphore_signal(barrier, inc=1, device_id=mates(), device_id_type=MESH)
     pl.semaphore_wait(barrier, 1)
@@ -59,114 +487,6 @@
         device_id=mates(),
         device_id_type=MESH,
     )
-
-
-def norm_rows(v):
-    mean = jnp.mean(v, axis=-1, keepdims=True)
-    off = v - mean
-    rstd = lax.rsqrt(jnp.mean(off * off, axis=-1, keepdims=True) + 1e-6)
-    return off * rstd, rstd
-
-
-def scores_t(k2, qa, mask):
-    st = jnp.where(mask > 0, nt(k2, qa), -1e9)
-    top = jnp.max(st, axis=0, keepdims=True)
-    e = jnp.exp(st - top)
-    return e * (1.0 / jnp.sum(e, axis=0, keepdims=True))
-
-
-def half_lanes(v, a):
-    lane = lax.broadcasted_iota(jnp.int32, v.shape, 1)
-    return jnp.where((lane >= HEAD) == (a == 1), v, jnp.zeros_like(v))
-
-
-def fwd_kernel(
-    x_ref, vec_ref, bqkv_ref, bup_ref, mask_ref, wqkv_ref, wout_ref, wup_ref, wdown_ref,
-    x2_ref, x3_ref, h1_ref, qkv_ref, a_ref, h2_ref, z_ref, gp_ref,
-    put_ref, got_ref, send, recv,
-):
-    rows, d = x_ref.shape
-    hc = a_ref.shape[1]
-    f = z_ref.shape[1]
-    own, sib = pl.ds(0, rows), pl.ds(rows, rows)
-    step = 16
-    greet()
-
-    def norm_out(src_ref, dst_ref, gain, shift):
-        for i in range(rows // step):
-            r = pl.ds(i * step, step)
-            hat, _ = norm_rows(src_ref[r, :])
-            dst_ref[r, :] = (hat * vec_ref[gain:gain + 1, :] + vec_ref[shift:shift + 1, :]).astype(BF16)
-
-    norm_out(x_ref, h1_ref, G1, B1)
-    cp = to_mate(h1_ref.at[own], h1_ref.at[sib], send, recv, 0)
-    cp.start()
-
-    wide = 256
-
-    def qkv_rows(r):
-        def body(j):
-            c = cols(j, wide)
-            out = nn(h1_ref[r, :], wqkv_ref[:, c]) + bqkv_ref[0:1, c]
-            qkv_ref[r, c] = (out * bqkv_ref[1:2, c]).astype(BF16)
-
-        loop(3 * hc // wide, body)
-
-    qkv_rows(own)
-    cp.wait()
-    qkv_rows(sib)
-
-    mask = mask_ref[:, 0:1]
-
-    def pair(p):
-        q2 = qkv_ref[:, pl.ds(pl.multiple_of(p * 128, 128), 128)]
-        k2 = qkv_ref[:, pl.ds(pl.multiple_of(hc + p * 128, 128), 128)]
-        v2 = qkv_ref[:, pl.ds(pl.multiple_of(2 * hc + p * 128, 128), 128)]
-        vt = v2.T
-        parts = []
-        for a in range(2):
-            pt = scores_t(k2, half_lanes(q2, a), mask)
-            parts.append(nn(vt[a * HEAD:(a + 1) * HEAD, :], pt.astype(BF16)))
-        a_ref[:, pl.ds(pl.multiple_of(p * 128, 128), 128)] = jnp.concatenate(parts, axis=0).T.astype(BF16)
-
-    loop(hc // 128, pair)
-
-    def exchange(left_ref, w_ref, base_ref, bias, out_ref, slot):
-        def theirs(j):
-            c = cols(j, wide)
-            put_ref[slot, :, c] = nn(left_ref[sib, :], w_ref[:, c]).astype(BF16)
-
-        loop(d // wide, theirs)
-        cp = to_mate(put_ref.at[slot], got_ref.at[slot], send, recv, 1 + slot)
-        cp.start()
-
-        def ours(j):
-            c = cols(j, wide)
-            out_ref[:, c] = nn(left_ref[own, :], w_ref[:, c]) + base_ref[:, c] + vec_ref[bias:bias + 1, c]
-
-        loop(d // wide, ours)
-        cp.wait()
-        out_ref[...] += got_ref[slot].astype(F32)
-
-    exchange(a_ref, wout_ref, x_ref, BOUT, x2_ref, 0)
-    norm_out(x2_ref, h2_ref, G2, B2)
-    cp = to_mate(h2_ref.at[own], h2_ref.at[sib], send, recv, 3)
-    cp.start()
-
-    def up_rows(r):
-        def body(j):
-            c = cols(j, wide)
-            u = nn(h2_ref[r, :], wup_ref[:, c]) + bup_ref[0:1, c]
-            phi = 0.5 + 0.5 * lax.erf(u * 0.7071067811865476)
-            z_ref[r, c] = (u * phi).astype(BF16)
-            gp_ref[r, c] = (phi + u * jnp.exp(u * u * -0.5) * 0.3989422804014327).astype(BF16)
-
-        loop(f // wide, body)
-
-    up_rows(own)
-    cp.wait()
-    up_rows(sib)
-    exchange(z_ref, wdown_ref, x2_ref, BDOWN, x3_ref, 1)
 
 
 def bwd_kernel(
@@ -181,7 +501,7 @@
     own, sib = pl.ds(0, rows), pl.ds(rows, rows)
     step = 16
     wide = 256
-    greet()
+    greet_mate()
 
     def send_round(src_ref, sum_row, slot):
         total = jnp.zeros((8, d), F32)
@@ -272,7 +592,7 @@
         gwout_ref[c, :] = tn(a_ref[:, c], dm_ref[1]).astype(BF16)
 
     loop(hc // wide, grads_out)
-    mask = mask_ref[:, 0:1]
+    mask = mask_ref[:, 0:1] > 0
 
     def pair(p):
         cq = pl.ds(pl.multiple_of(p * 128, 128), 128)
@@ -313,35 +633,6 @@
     norm_back(x_ref, dx2_ref, g0_ref, G1, B1, 1)
 
 
-VM = pl.BlockSpec(memory_space=pltpu.VMEM)
-
-
-def run_fwd(x, vec, bqkv, bup, mask, wqkv, wout, wup, wdown):
-    rows, d = x.shape
-    hc, f = wout.shape[0], wdown.shape[0]
-    both = 2 * rows
-    shapes = [
-        ((rows, d), F32), ((rows, d), F32), ((both, d), BF16), ((both, 3 * hc), BF16),
-        ((both, hc), BF16), ((both, d), BF16), ((both, f), BF16), ((both, f), BF16),
-    ]
-    args = (x, vec, bqkv, bup, mask, wqkv, wout, wup, wdown)
-    return pl.pallas_call(
-        fwd_kernel,
-        out_shape=[jax.ShapeDtypeStruct(s, t) for s, t in shapes],
-        in_specs=[VM] * len(args),
-        out_specs=[VM] * len(shapes),
-        scratch_shapes=[
-            pltpu.VMEM((2, rows, d), BF16), pltpu.VMEM((2, rows, d), BF16),
-            pltpu.SemaphoreType.DMA((4,)), pltpu.SemaphoreType.DMA((4,)),
-        ],
-        compiler_params=pltpu.CompilerParams(
-            collective_id=1, has_side_effects=True, vmem_limit_bytes=VMEM_LIMIT
-        ),
-        cost_estimate=pl.CostEstimate(flops=8 * 10**9, bytes_accessed=20 * 10**6, transcendentals=0),
-        name="layer_fwd",
-    )(*args)
-
-
 def run_bwd(g3, saved, vec, mask, wqkv, wout, wup, wdown):
     rows, d = g3.shape
     hc, f = wout.shape[0], wdown.shape[0]
@@ -363,7 +654,7 @@
             pltpu.SemaphoreType.DMA((4,)), pltpu.SemaphoreType.DMA((4,)),
         ],
         compiler_params=pltpu.CompilerParams(
-            collective_id=2, has_side_effects=True, vmem_limit_bytes=VMEM_LIMIT
+            collective_id=2, has_side_effects=True, vmem_limit_bytes=int(63.5 * 2**20)
         ),
         cost_estimate=pl.CostEstimate(flops=17 * 10**9, bytes_accessed=40 * 10**6, transcendentals=0),
         name="layer_bwd",
@@ -389,77 +680,44 @@
     hc = d // 2
     f = 2 * w_down.shape[1] * 1
     seq = tokens.shape[1]
-    real = 2 * seq
-    rows = -(-real // 16) * 16
-
-    def mine(value):
-        got = swap(pick(value, 1 - x, 0), 2)
-        return jnp.concatenate([pick(value, x, 0), got], axis=0)
+    block = -(-seq // 32) * 32
+    rows = 2 * block
+
 
     def pad(value):
-        return jnp.pad(value, [(0, rows - real)] + [(0, 0)] * (value.ndim - 1))
-
+        return jnp.pad(value, ((0, 0), (0, block - seq), (0, 0)))
+
+    layer_rows = [
+        w.reshape(layers, -1, d // 4)
+        for w in (norm1_gain, norm1_bias, b_out, norm2_gain, norm2_bias, b_down, b_qv, b_up)
+    ]
+    pack = jnp.concatenate(layer_rows, axis=1).astype(F32)
+    pack = jnp.pad(pack, ((0, 0), (0, SMALL - pack.shape[1]), (0, 0))).reshape(layers * SMALL, d // 4)
+    (vqkv, vout, vup, vdown, xs, x2s, h1s, qkvs, atts, h2s, zs, gps, cot, act, vec) = run_fwd(
+        pad(tokens), pad(cotangent), pack, token_valid, w_qkv, w_out, w_up, w_down, seq
+    )
+    smalls = [norm1_gain, norm1_bias, b_out, norm2_gain, norm2_bias, b_down, b_qv, b_up]
+    widths = [s.shape[1] for s in smalls]
+    activations = act[:, :seq]
     flags = pick(token_valid, x, 0).reshape(2, 2, seq)
-    own_flags = pad(jnp.concatenate([pick(pick(flags, x, 0), c, 0), pick(pick(flags, 1 - x, 0), c, 0)]))
-    sib_flags = pad(jnp.concatenate([pick(pick(flags, x, 0), 1 - c, 0), pick(pick(flags, 1 - x, 0), 1 - c, 0)]))
+    pf = lambda a: jnp.pad(a, (0, block - seq))
+    own_flags = jnp.concatenate([pf(pick(pick(flags, x, 0), c, 0)), pf(pick(pick(flags, 1 - x, 0), c, 0))])
+    sib_flags = jnp.concatenate([pf(pick(pick(flags, x, 0), 1 - c, 0)), pf(pick(pick(flags, 1 - x, 0), 1 - c, 0))])
     mask = jnp.broadcast_to(jnp.concatenate([own_flags, sib_flags])[:, None], (2 * rows, 128))
     weight = (own_flags * pick(image_valid, x, 0)).astype(F32)
-    hidden = pad(mine(tokens)).astype(F32)
-    flow = pad(mine(cotangent)).astype(F32) * weight[:, None]
-
-    smalls = [norm1_gain, norm1_bias, b_out, norm2_gain, norm2_bias, b_down, b_qv, b_up]
-    widths = [s.shape[1] for s in smalls]
-    packed = lax.all_gather(jnp.concatenate(smalls, axis=1), "grp", axis=0)
-    parts, at = [], 0
-    for width in widths:
-        parts.append(packed[:, :, at:at + width].transpose(1, 0, 2).reshape(layers, 4 * width).astype(F32))
-        at += width
-    vecs = jnp.stack(parts[:6] + [jnp.zeros_like(parts[0])] * 2, axis=1)
-
-    def halves(value, axis):
-        return pick(value, c, axis)
-
-    bq = halves(parts[6][:, :d].reshape(layers, 2, 2, d // 4), 2).reshape(layers, hc)
-    bv = halves(parts[6][:, d:].reshape(layers, 2, 2, d // 4), 2).reshape(layers, hc)
-    bqkv = jnp.concatenate([bq, jnp.zeros_like(bq), bv], axis=1)
-    scale = jnp.concatenate([jnp.full_like(bq, HEAD ** -0.5), jnp.ones((layers, 2 * hc), F32)], axis=1)
-    bqkv = jnp.pad(jnp.stack([bqkv, scale], axis=1), ((0, 0), (0, 6), (0, 0)))
-    bup = halves(parts[7].reshape(layers, 2, 2, -1), 2).reshape(layers, 1, -1)
-    bup = jnp.pad(bup, ((0, 0), (0, 7), (0, 0)))
-
-    def by_core(value, other):
-        return jnp.where(c == 0, jnp.concatenate([value, other], axis=1), jnp.concatenate([other, value], axis=1))
-
-    def by_chip(value):
-        other = swap(value, 2)
-        return jnp.where(x == 0, jnp.concatenate([value, other], axis=1), jnp.concatenate([other, value], axis=1))
-
-    def columns(w, groups):
-        w = w.reshape(layers, w.shape[1], groups, 2, 2, -1)
-        keep = pick(w, c, 4).reshape(layers, w.shape[1], -1)
-        give = pick(w, 1 - c, 4).reshape(layers, w.shape[1], -1)
-        return by_chip(by_core(keep, swap(give, 1)))
-
-    wqkv = columns(w_qkv, 3)
-    wup = columns(w_up, 1)
-    wout = by_chip(w_out)
-    wdown = by_chip(w_down)
-
-    saved = []
-    for l in range(layers):
-        x2, x3, *rest = run_fwd(hidden, vecs[l], bqkv[l], bup[l], mask, wqkv[l], wout[l], wup[l], wdown[l])
-        saved.append((hidden, x2, *rest))
-        hidden = x3
+    flow = cot.reshape(rows, d).astype(F32) * weight[:, None]
+    vecs = vec.reshape(layers, SMALL, d)[:, :8]
+    grads = [None] * layers
+    for l in reversed(range(layers)):
+        saved = (xs[l], x2s[l], h1s[l], qkvs[l], atts[l], h2s[l], zs[l], gps[l])
+        wq, wo, wu, wd = (w[l].reshape(-1, w.shape[-1]) for w in (vqkv, vout, vup, vdown))
+        flow, *grads[l] = run_bwd(flow, saved, vecs[l], mask, wq, wo, wu, wd)
 
     def give_back(value):
-        value = value[:real].astype(BF16).reshape(2, seq, d)
+        value = value.astype(BF16).reshape(2, block, d)[:, :seq]
         got = swap(value[1], 2)
         return jnp.where(x == 0, jnp.stack([value[0], got]), jnp.stack([got, value[0]]))
 
-    activations = give_back(hidden)
-    grads = [None] * layers
-    for l in reversed(range(layers)):
-        flow, *grads[l] = run_bwd(flow, saved[l], vecs[l], mask, wqkv[l], wout[l], wup[l], wdown[l])
     grad_tokens = give_back(flow)
 
     def reduce_big(index):

time: 1490 us -> 1250 us (0.84)
  waiting for transfers between devices: 898 us -> 772 us
  blocking collectives: 92.2 us -> 0 us
  Pallas kernels: 188 us -> 278 us
  local copies, waits for them, and re-layouts: 191 us -> 118 us
  other arithmetic: 84.2 us -> 49.6 us
    ppermute x16 -> x7, waiting for transfers between devices: 388 us -> 260 us  [swap(): return lax.ppermute(value, 'grp', [(i, i ^ bit) for i in range(4)])]
    all_gather x1 -> x0, blocking collectives: 92.2 us -> none  [local(): packed = lax.all_gather(jnp.concatenate(smalls, axis=1), 'grp', axis=0)]
    pallas_call x2 -> x1, Pallas kernels: 72.3 us -> 160 us  [run_fwd(): pl.pallas_call(functools.partial(fwd_kernel, seq), out_shape=[jax.ShapeDt...]
    dynamic_slice x8 -> x3, local copies, waits for them, and re-layouts: 60.9 us -> 0.62 us  [pick(): return lax.dynamic_index_in_dim(value, index, axis, keepdims=False)]
    reshape x9 -> x8, local copies, waits for them, and re-layouts: 32.8 us -> 0.05 us  [local(): w.reshape(layers, -1, d // 4)]
    select_n x6 -> x0, other arithmetic: 29.9 us -> none  [the longest x4 21.3 us: by_chip(): jnp.where(x == 0, jnp.concatenate([value, other], axis=1), jnp.concatenat...]
  transfers between devices with their start and end apart: 18 -> 9, of which waited for: 5 -> 3; matrix products, arithmetic and copies ran while one was open for 15% -> 6% of each run, Pallas kernels for 0% -> 0%
where the time goes in v2:
time: 1250 us; the launch traced here: 1240 us
  waiting for transfers between devices  772 us (62%)
  Pallas kernels  278 us (22%)
  local copies, waits for them, and re-layouts  118 us (9%)
  other arithmetic  49.6 us (4%)
  between operations  16.5 us (1%)
    psum x1, waiting for transfers between devices, reduce_big(): return lax.psum(total, 'rep')  397 us
    ppermute x7, waiting for transfers between devices, swap(): return lax.ppermute(value, 'grp', [(i, i ^ bit) for i in range(4)])  260 us
    pallas_call x1, Pallas kernels, run_fwd(): pl.pallas_call(functools.partial(fwd_kernel, seq), out_shape=[jax.ShapeDt...  160 us
    pallas_call x2, Pallas kernels, run_bwd(): pl.pallas_call(bwd_kernel, out_shape=[jax.ShapeDtypeStruct(s, t) for s, t...  118 us
    psum x1, waiting for transfers between devices, local(): lax.psum(jnp.concatenate([gvec, spread(gb), spread(gu)], axis=1), ('rep',...  115 us
    unnamed x88, local copies, waits for them, and re-layouts  26.2 us
  transfers between devices with their start and end apart: 9, of which 3 were waited for; matrix products, arithmetic and copies ran while one was open for 6% of the time, Pallas kernels for 0%

profile of v2, /device:TPU:0, one launch (start us, length us, event | category | flops | bytes accessed | tf_op | source)
XLA Modules:
  0.0 1239.5 jit_solution(6609825317578567732)
XLA Ops:
  8.2 1.2 copy.74
  9.4 1.2 copy.75
  14.0 160.2 %forward.1 = (bf16[2,4,256,1536]{3,2,1,0:T(8,128)(2,1)}, bf16[2,2,256,1024]{3,2,1,0:T(8,128)(2,1)}, bf16[2,4,256,2048]{3,2,1,0:T(8,128)(2,1)}, bf16[2,2,1024,102...) custom-call(bf16[2,160,1024]{2,1,0:T(8,128)(2,1)} %pad.29.tok_ref, ...), custom_call_target="tpu_custom_call" | custom-call | flops 16999999488 | bytes 80000000 | tf_op jit(solution)/shard_map/forward/pallas_call | solution.py:449
  174.3 4.5 slice_bitcast_fusion.4
  180.6 3.9 fusion.14
  184.5 1.5 fusion.15
  186.0 1.7 slice-done.3
  187.7 4.3 fusion.13
  192.9 3.9 fusion.12
  197.5 1.2 convert_multiply_fusion.g3_ref
  198.7 5.0 slice_bitcast_fusion.8
  203.7 2.8 slice_bitcast_fusion.6
  206.5 1.4 slice-done.4
  208.2 4.1 slice_bitcast_fusion
  213.2 58.8 %layer_bwd.2 = (f32[320,1024]{1,0:T(8,128)}, bf16[1024,1536]{1,0:T(8,128)(2,1)}, bf16[512,1024]{1,0:T(8,128)(2,1)}, bf16[1024,2048]{1,0:T(8,128)(2,1)}, bf16[204...) custom-call(f32[320,1024]{1,0:T(8,128)} %convert_multiply_fusion.g3_ref, ...), custom_call_target="tpu_custom_call" | custom-call | flops 16999999488 | bytes 40000000 | tf_op jit(solution)/shard_map/layer_bwd/pallas_call | solution.py:645
  272.0 58.8 %layer_bwd.3 = (f32[320,1024]{1,0:T(8,128)}, bf16[1024,1536]{1,0:T(8,128)(2,1)}, bf16[512,1024]{1,0:T(8,128)(2,1)}, bf16[1024,2048]{1,0:T(8,128)(2,1)}, bf16[204...) custom-call(f32[320,1024]{1,0:T(8,128)} %get-tuple-element.60.g3_ref, ...), custom_call_target="tpu_custom_call" | custom-call | flops 16999999488 | bytes 40000000 | tf_op jit(solution)/shard_map/layer_bwd/pallas_call | solution.py:645
  330.8 5.0 fusion.2
  336.7 1.9 fusion.5
  339.7 4.7 fusion
  345.2 2.2 fusion.8
  348.7 259.9 %collective-permute-done.3 = bf16[2,256,1024]{2,1,0:T(8,128)(2,1)} collective-permute-done((bf16[2,256,1024]{2,1,0:T(8,128)(2,1)}, bf16[2,256,1024]{2,1,0:T(8,128)(2,1)}, u32[]{:S(2)}, u32[]{:S(2)}) %collective-permute-start.3) | collective-permute-done | bytes 1048608 | tf_op jit(solution)/shard_map/ppermute | solution.py:665
  608.5 2.9 add_convert_fusion.3
  611.4 4.6 add_convert_fusion.2
  617.0 4.9 add_convert_fusion.1
  621.9 4.9 add_convert_fusion
  630.6 396.5 %all-reduce.17.cloned.1.call-done = (bf16[2,512,1536]{2,1,0:T(8,128)(2,1)}, bf16[2,256,1024]{2,1,0:T(8,128)(2,1)}, bf16[2,512,2048]{2,1,0:T(8,128)(2,1)}, bf16[2,1024,1024]{2,1,0:T(8,128)(2,1)}) async-done(((bf16[2,512,1536]{2,1,0:T(8,128)(2,1)}, bf16[2,256,1024]{2,1,0:T(8,128)(2,1)}, bf16[2,512,2048]{2,1,0:T(8,128)(2,1)}, bf16[2,1024,1024]{2,1,0:T(8,128)(2,1)}), (bf16[2,512,1536]{2,1,0:T(8,128)(2,1)}, ...) | async-done | bytes 12582928 | tf_op jit(solution)/shard_map/psum | solution.py:729
  1027.1 3.9 constant_dynamic-slice_fusion.9
  1031.0 1.8 constant_dynamic-slice_fusion.3
  1034.2 1.5 collective-permute-start
  1036.8 1.4 copy.96
  1038.2 115.2 %all-reduce.15.cloned.1.call-done = f32[2,12288]{1,0:T(2,128)} async-done(((f32[2,12288]{1,0:T(2,128)}), f32[2,12288]{1,0:T(2,128)}) %all-reduce.15.cloned.1.call-update) | async-done | bytes 98320 | tf_op jit(solution)/shard_map/psum | solution.py:753
  1160.5 1.4 copy.97
  1161.9 2.9 copy.84
  1164.8 2.6 copy.85
  1167.4 1.6 convert_element_type.88
  1168.9 2.5 copy.90
  1171.4 3.0 copy.91
  1174.4 6.6 convert_element_type.97
  1181.1 4.6 stack_reshape.26
  1185.6 1.8 copy.86
  1187.5 2.9 fusion.7
  1190.4 6.6 copy.89
  1197.0 6.6 copy.98
  1203.5 4.5 stack.110
  1208.0 2.2 copy.92
  1210.2 3.8 fusion.4
  1214.0 8.7 copy.95
  1222.7 8.9 copy.99
  (155 shorter events, 26.3 us)
Async XLA Ops:
  8.0 4.4 copy-start.24
  8.0 4.4 copy-start.25
  8.0 4.4 copy-start.26
  8.0 4.4 copy-start.27
  8.1 4.4 copy-start.28
  8.1 4.5 copy-start.29
  8.1 4.5 copy-start.22
  8.1 4.5 copy-start.21
  8.1 5.2 copy-start.23
  8.1 5.3 copy-start.30
  8.1 1019.0 %all-reduce.17.cloned.1.call-start = ((), (), s32[]{:S(2)}) async-start(), calls=%async_computation.1 | async-start | bytes 25165824 | tf_op jit(solution)/shard_map/psum | solution.py:729
  174.2 4.6 copy-start.14
  174.2 5.7 copy-start.18
  174.3 6.3 copy-start.7
  180.6 5.4 slice-start.2
  180.6 3.9 copy-start.13
  180.6 7.1 slice-start.3
  184.5 7.5 slice-start
  187.7 5.1 slice-start.1
  192.9 4.6 copy-start.17
  192.9 5.8 copy-start.12
  197.4 9.1 slice-start.6
  198.7 5.0 copy-start.10
  198.7 5.0 copy-start.11
  198.7 7.8 slice-start.7
  203.7 4.2 slice-start.4
  203.7 4.4 slice-start.5
  330.8 5.9 copy-start.4
  330.8 5.8 copy-start.5
  335.8 280.2 %collective-permute-start.4 = (bf16[2,512,2048]{2,1,0:T(8,128)(2,1)}, bf16[2,512,2048]{2,1,0:T(8,128)(2,1)}, u32[]{:S(2)}, u32[]{:S(2)}) collective-permute-start(bf16[2,512,2048]{2,1,0:T(8,128)(2,1)} %fusion.2), channel_id=1, source_target_pairs={{0,2},{1,3},{2,0},{3,1},{4,6},{5,7},{6,4},{7,5},{8,10},{9,11},{10,... | collective-permute-start | bytes 12582920 | tf_op jit(solution)/shard_map/ppermute | solution.py:665
  338.5 272.9 %collective-permute-start.1 = (bf16[2,512,1536]{2,1,0:T(8,128)(2,1)}, bf16[2,512,1536]{2,1,0:T(8,128)(2,1)}, u32[]{:S(2)}, u32[]{:S(2)}) collective-permute-start(bf16[2,512,1536]{2,1,0:T(8,128)(2,1)} %fusion.5), channel_id=1, source_target_pairs={{0,2},{1,3},{2,0},{3,1},{4,6},{5,7},{6,4},{7,5},{8,10},{9,11},{10,... | collective-permute-start | bytes 9437192 | tf_op jit(solution)/shard_map/ppermute | solution.py:665
  344.4 277.5 %collective-permute-start.6 = (bf16[2,1024,1024]{2,1,0:T(8,128)(2,1)}, bf16[2,1024,1024]{2,1,0:T(8,128)(2,1)}, u32[]{:S(2)}, u32[]{:S(2)}) collective-permute-start(bf16[2,1024,1024]{2,1,0:T(8,128)(2,1)} %fusion), channel_id=1, source_target_pairs={{0,2},{1,3},{2,0},{3,1},{4,6},{5,7},{6,4},{7,5},{8,10},{9,11},{10,... | collective-permute-start | bytes 12582920 | tf_op jit(solution)/shard_map/ppermute | solution.py:665
  347.5 261.0 %collective-permute-start.3 = (bf16[2,256,1024]{2,1,0:T(8,128)(2,1)}, bf16[2,256,1024]{2,1,0:T(8,128)(2,1)}, u32[]{:S(2)}, u32[]{:S(2)}) collective-permute-start(bf16[2,256,1024]{2,1,0:T(8,128)(2,1)} %fusion.8), channel_id=1, source_target_pairs={{0,2},{1,3},{2,0},{3,1},{4,6},{5,7},{6,4},{7,5},{8,10},{9,11},{10,... | collective-permute-start | bytes 3145736 | tf_op jit(solution)/shard_map/ppermute | solution.py:665
  348.7 262.8 %copy-start.6 = (bf16[1024,1536]{1,0:T(8,128)(2,1)S(1)}, bf16[1024,1536]{1,0:T(8,128)(2,1)}, u32[]{:S(2)}) copy-start(bf16[1024,1536]{1,0:T(8,128)(2,1)} %get-tuple-element.68) | copy-start | bytes 9437188
  611.4 4.6 copy-start.1
  611.4 5.5 copy-start.3
  616.0 5.9 copy-start
  616.0 5.9 copy-start.2
  626.8 3.7 copy-start.19
  626.8 3.7 copy-start.20
  626.8 526.6 %all-reduce.15.cloned.1.call-start = ((), (), s32[]{:S(2)}) async-start(), calls=%async_computation | async-start | bytes 196608 | tf_op jit(solution)/shard_map/psum | solution.py:753
  1027.1 3.9 copy-start.9
  1031.0 150.1 %collective-permute-start.2 = (bf16[2,256,1536]{2,1,0:T(8,128)(2,1)}, bf16[2,256,1536]{2,1,0:T(8,128)(2,1)}, u32[]{:S(2)}, u32[]{:S(2)}) collective-permute-start(bf16[2,256,1536]{2,1,0:T(8,128)(2,1)} %get-tuple-element.151), channel_id=1, source_target_pairs={{0,1},{1,0},{2,3},{3,2},{4,5},{5,4},{6,7},{7,6},{8,9},{9,8},{10,11... | collective-permute-start | bytes 4718600 | tf_op jit(solution)/shard_map/ppermute | solution.py:665
  1031.0 3.0 copy-start.15
  1032.8 170.8 %collective-permute-start.5 = (bf16[2,256,2048]{2,1,0:T(8,128)(2,1)}, bf16[2,256,2048]{2,1,0:T(8,128)(2,1)}, u32[]{:S(2)}, u32[]{:S(2)}) collective-permute-start(bf16[2,256,2048]{2,1,0:T(8,128)(2,1)} %get-tuple-element.147), channel_id=1, source_target_pairs={{0,1},{1,0},{2,3},{3,2},{4,5},{5,4},{6,7},{7,6},{8,9},{9,8},{10,11... | collective-permute-start | bytes 6291464 | tf_op jit(solution)/shard_map/ppermute | solution.py:665
  1034.2 126.2 %collective-permute-start = (bf16[145,1024]{1,0:T(8,128)(2,1)S(1)}, bf16[145,1024]{1,0:T(8,128)(2,1)S(1)}, u32[]{:S(2)}, u32[]{:S(2)}) collective-permute-start(bf16[145,1024]{1,0:T(8,128)(2,1)S(1)} %get-tuple-element.165), channel_id=1, source_target_pairs={{0,2},{1,3},{2,0},{3,1},{4,6},{5,7},{6,4},{7,5},{8,10},{9,11},{10,... | collective-permute-start | bytes 890888 | tf_op jit(solution)/shard_map/ppermute | solution.py:665
  1161.9 5.5 copy-start.16
  1185.6 1.9 copy-start.8
Sparse Core Ops, SparseCore 0:
  626.9 400.0 all-reduce.16
Sparse Core Ops, SparseCore 1:
  1034.1 119.3 all-reduce.14

commit v3 on v2

--- a/solution.py
+++ b/solution.py
@@ -467,206 +467,484 @@
     )(tok, cot, pack, tv, w_qkv, w_out, w_up, w_down)
 
 
-def mates():
-    rep, grp = lax.axis_index("rep"), lax.axis_index("grp")
-    return (rep, grp + 1 - 2 * (grp % 2))
-
-
-def greet_mate():
-    barrier = pltpu.get_barrier_semaphore()
-    pl.semaphore_signal(barrier, inc=1, device_id=mates(), device_id_type=MESH)
-    pl.semaphore_wait(barrier, 1)
-
-
-def to_mate(src, dst, send, recv, slot):
-    return pltpu.make_async_remote_copy(
-        src_ref=src,
-        dst_ref=dst,
-        send_sem=send.at[slot],
-        recv_sem=recv.at[slot],
-        device_id=mates(),
-        device_id_type=MESH,
+NS, NY, NZ, NT = 6, 3, 4, 6
+CHUNK = 256
+
+
+class Ring:
+    def __init__(self, at, plan, chunks, outs, bufs, sems):
+        self.at, self.plan, self.chunks, self.outs = at, plan, chunks, outs
+        self.g, self.xr, self.yr, self.zr, self.wr, self.t = bufs
+        (self.x_send, self.x_recv, self.y_send, self.y_recv, self.z_send, self.z_recv, self.w_send, self.w_recv,
+         self.f_send, self.f_recv, self.cx, self.cy, self.cz, self.cw, self.cb) = sems
+        self.count = len(chunks)
+        self.x_free = 0.0
+        self.copies = {}
+
+    def size(self, u):
+        return 64 if self.chunks[u][0] == "small" else CHUNK
+
+    def reserve(self, u):
+        if u >= NS:
+            self.plan.need(("s2", u - NS))
+
+    def launch(self, u):
+        n = self.size(u)
+        if u >= NS:
+            pl.semaphore_wait(self.cx, 1)
+        copy = remote(
+            self.g.at[u % NS, 0, pl.ds(0, n)], self.xr.at[u % NS, pl.ds(0, n)],
+            self.x_send.at[u % NS], self.x_recv.at[u % NS], self.at.xn,
+        )
+        copy.start()
+        self.copies["x", u] = copy
+        plan = self.plan
+        self.x_free = max(plan.now, self.x_free) + 11.3 * n / CHUNK
+        t = self.x_free + 2
+        for k, lag in enumerate((0, 8, 16, 24, 32, 43)):
+            plan.add(t + lag, (f"s{k + 1}", u), functools.partial(getattr(self, f"s{k + 1}"), u))
+        plan.order()
+
+    def credit(self, sem, u, slots, peer):
+        if u + slots < self.count:
+            pl.semaphore_signal(sem, inc=1, device_id=peer, device_id_type=MESH)
+
+    def claim(self, sem, u, slots):
+        if u >= slots:
+            pl.semaphore_wait(sem, 1)
+
+    def add(self, dst, src, count, base=None, base_at=None):
+        def body(j):
+            r = cols(j, 32)
+            b = dst[r, :] if base is None else base[pl.ds(pl.multiple_of(base_at + j * 32, 32), 32), :]
+            dst[r, :] = (b.astype(F32) + src[r, :].astype(F32)).astype(BF16)
+
+        loop(count // 32, body)
+
+    def s1(self, u):
+        n, at = self.size(u), self.at
+        slot = u % NS
+        self.copies["x", u].wait()
+        self.add(self.g.at[slot, 1], self.xr.at[slot], n)
+        self.credit(self.cx, u, NS, at.xn)
+        self.claim(self.cy, u, NY)
+        copy = remote(
+            self.g.at[slot, 1, span((1 - at.y) * (n // 2), n // 2)], self.yr.at[u % NY, pl.ds(0, n // 2)],
+            self.y_send.at[slot], self.y_recv.at[u % NY], at.yn,
+        )
+        copy.start()
+        self.copies["y", u] = copy
+
+    def part(self, ref, u, slots):
+        return ref.at[u % slots, pl.ds(0, self.size(u) // 2)]
+
+    def s2(self, u):
+        n, at = self.size(u), self.at
+        t = self.part(self.t, u, NT)
+        self.copies["y", u].wait()
+        self.add(t, self.part(self.yr, u, NY), n // 2, self.g.at[u % NS, 1], at.y * (n // 2))
+        self.credit(self.cy, u, NY, at.yn)
+
+        @pl.when(at.outer)
+        def _():
+            self.claim(self.cz, u, NZ)
+            remote(t, self.part(self.zr, u, NZ), self.z_send.at[u % NT], self.z_recv.at[u % NZ], at.zn).start()
+
+    def s3(self, u):
+        n, at = self.size(u), self.at
+        t = self.part(self.t, u, NT)
+
+        @pl.when(at.outer)
+        def _():
+            settle(t, self.z_send.at[u % NT])
+
+        @pl.when(at.inner)
+        def _():
+            got = self.part(self.zr, u, NZ)
+            settle(got, self.z_recv.at[u % NZ])
+            self.add(t, got, n // 2)
+            self.credit(self.cz, u, NZ, at.zn)
+            self.claim(self.cw, u, NZ)
+            remote(t, self.part(self.wr, u, NZ), self.z_send.at[u % NT], self.w_recv.at[u % NZ], at.mid).start()
+
+    def s4(self, u):
+        n, at = self.size(u), self.at
+
+        @pl.when(at.inner)
+        def _():
+            t = self.part(self.t, u, NT)
+            got = self.part(self.wr, u, NZ)
+            settle(got, self.w_recv.at[u % NZ])
+            settle(t, self.z_send.at[u % NT])
+            self.add(t, got, n // 2)
+            self.credit(self.cw, u, NZ, at.mid)
+            self.claim(self.cb, u, NZ)
+            remote(t, self.part(self.zr, u, NZ), self.w_send.at[u % NT], self.z_recv.at[u % NZ], at.zn).start()
+
+    def s5(self, u):
+        n, at = self.size(u), self.at
+        t = self.part(self.t, u, NT)
+
+        @pl.when(at.outer)
+        def _():
+            got = self.part(self.zr, u, NZ)
+            settle(got, self.z_recv.at[u % NZ])
+
+            def body(j):
+                t[cols(j, 32), :] = got[cols(j, 32), :]
+
+            loop(n // 64, body)
+            self.credit(self.cb, u, NZ, at.zn)
+
+        kind, l, i = self.chunks[u]
+        out = self.outs[kind]
+        sent = self.f_send.at[u % NT]
+        if kind == "small":
+            pltpu.make_async_copy(t, out, sent).start()
+            return
+        half = n // 2
+        width = t.shape[1]
+
+        def deliver(src, dst, mine, kind_index):
+            if mine:
+                pltpu.make_async_copy(src, dst, sent).start()
+                remote(src, dst, sent, self.f_recv.at[kind_index], at.yn).start()
+            else:
+                remote(src, dst, sent, self.f_recv.at[kind_index], at.sib).start()
+                remote(src, dst, sent, self.f_recv.at[kind_index], at.yd).start()
+
+        if kind in ("down", "out"):
+            deliver(t, out.at[l, span(i * n + at.y * half, half)], True, KINDS.index(kind))
+        elif kind == "up":
+            side, run = divmod(i, 2)
+            deliver(t, out.at[l, span(at.y * half, half), span((2 * run + at.c) * width, width)], side == 0, 2)
+        else:
+            for side in range(2):
+                for run in range(2):
+                    src = t.at[:, pl.ds((2 * side + run) * WIDE, WIDE)]
+                    dst = out.at[l, span(at.y * half, half), span(i * width + (2 * run + at.c) * WIDE, WIDE)]
+                    deliver(src, dst, side == 0, 0)
+
+    def s6(self, u):
+        at = self.at
+        t = self.part(self.t, u, NT)
+        if self.chunks[u][0] == "small":
+            settle(t, self.f_send.at[u % NT])
+        else:
+            settle(self.g.at[0, 0], self.f_send.at[u % NT])
+
+        @pl.when(at.inner)
+        def _():
+            settle(t, self.w_send.at[u % NT])
+
+    def finish(self):
+        while self.plan.events:
+            self.plan.fire()
+        for i, kind in enumerate(KINDS):
+            out = self.outs[kind]
+            rows = out.shape[1]
+            settle(out.at[:, pl.ds(0, rows // 2 if kind in ("out", "down") else rows * 3 // 4)], self.f_recv.at[i])
+
+
+def bwd_kernel(
+    seq, cot_ref, vec_ref, tv_ref, iv_ref, vqkv, vout, vup, vdown, xs, x2s, h1s, qkvs, as_, h2s, zs, gps,
+    oqkv, oout, oup, odown, osmall, otok,
+    wqkv, wout, wup, wdown, x_ref, x2_ref, h1, qkv, att, h2, z, gp,
+    tok, g_ref, dm, da, dj, dx2, dh, put, got, small, small_put, small_got, ring_g, ring_x, ring_y, ring_z, ring_w, ring_t,
+    s_load, s_core, r_core, s_misc, r_misc, *ring_sems,
+):
+    at = Place()
+    layers = vqkv.shape[0]
+    rows, d = x_ref.shape
+    block = rows // 2
+    hc, f = att.shape[1], z.shape[1]
+    own, other = pl.ds(0, rows), pl.ds(rows, rows)
+    x, c = at.x, at.c
+    plan = Plan()
+    chunks = []
+    for l in reversed(range(layers)):
+        chunks += [("down", l, i) for i in range(4)] + [("up", l, i) for i in range(4)]
+        chunks += [("out", l, 0)] + [("qkv", l, i) for i in range(3)]
+    chunks.append(("small", 0, 0))
+    ring = Ring(
+        at, plan, chunks, dict(qkv=oqkv, out=oout, up=oup, down=odown, small=osmall),
+        (ring_g, ring_x, ring_y, ring_z, ring_w, ring_t), ring_sems,
     )
-
-
-def bwd_kernel(
-    g3_ref, x_ref, x2_ref, h1_ref, qkv_ref, a_ref, h2_ref, z_ref, gp_ref,
-    vec_ref, mask_ref, wqkv_ref, wout_ref, wup_ref, wdown_ref,
-    g0_ref, gwqkv_ref, gwout_ref, gwup_ref, gwdown_ref, gvec_ref, gbqkv_ref, gbup_ref,
-    dm_ref, du_ref, da_ref, dj_ref, dx2_ref, dh_ref, put_ref, got_ref, send, recv,
-):
-    rows, d = g3_ref.shape
-    hc = a_ref.shape[1]
-    f = z_ref.shape[1]
-    own, sib = pl.ds(0, rows), pl.ds(rows, rows)
-    step = 16
-    wide = 256
-    greet_mate()
-
-    def send_round(src_ref, sum_row, slot):
-        total = jnp.zeros((8, d), F32)
-        for i in range(rows // step):
-            r = pl.ds(i * step, step)
-            low = src_ref[r, :].astype(BF16)
-            dm_ref[slot, r, :] = low
-            low = low.astype(F32)
-            total = total + low[0:8, :] + low[8:16, :]
-        gvec_ref[sum_row:sum_row + 1, :] = jnp.sum(total, axis=0, keepdims=True)
-        cp = to_mate(dm_ref.at[slot, own], dm_ref.at[slot, sib], send, recv, slot)
-        cp.start()
-        return cp
-
-    def exchange(left_ref, w_ref, slot):
-        def theirs(j):
-            c = cols(j, wide)
-            put_ref[slot, :, c] = nt(left_ref[sib, :], w_ref[c, :]).astype(BF16)
-
-        loop(d // wide, theirs)
-        cp = to_mate(put_ref.at[slot], got_ref.at[slot], send, recv, 2 + slot)
-        cp.start()
-
-        def ours(j):
-            c = cols(j, wide)
-            dh_ref[:, c] = nt(left_ref[own, :], w_ref[c, :])
-
-        loop(d // wide, ours)
-        return cp
-
-    def norm_back(value_ref, base_ref, out_ref, gain, shift, slot):
-        total_g = jnp.zeros((8, d), F32)
-        total_b = jnp.zeros((8, d), F32)
-        for i in range(rows // step):
-            r = pl.ds(i * step, step)
-            hat, rstd = norm_rows(value_ref[r, :])
-            dh = dh_ref[r, :] + got_ref[slot, r, :].astype(F32)
-            prod = dh * hat
-            total_g = total_g + prod[0:8, :] + prod[8:16, :]
-            total_b = total_b + dh[0:8, :] + dh[8:16, :]
-            dhat = dh * vec_ref[gain:gain + 1, :]
-            m1 = jnp.mean(dhat, axis=-1, keepdims=True)
-            m2 = jnp.mean(dhat * hat, axis=-1, keepdims=True)
-            out_ref[r, :] = base_ref[r, :] + rstd * (dhat - m1 - hat * m2)
-        gvec_ref[gain:gain + 1, :] = jnp.sum(total_g, axis=0, keepdims=True)
-        gvec_ref[shift:shift + 1, :] = jnp.sum(total_b, axis=0, keepdims=True)
-
-    cp = send_round(g3_ref, BDOWN, 0)
-
-    def dz_rows(r):
-        def body(j):
-            c = cols(j, wide)
-            dz = nt(dm_ref[0, r, :], wdown_ref[c, :])
-            du_ref[r, c] = (dz * gp_ref[r, c].astype(F32)).astype(BF16)
-
-        loop(f // wide, body)
-
-    dz_rows(own)
-    cp.wait()
-    dz_rows(sib)
-
-    def grads_ff(j):
-        c = cols(j, wide)
-        gwdown_ref[c, :] = tn(z_ref[:, c], dm_ref[0]).astype(BF16)
-        du = du_ref[:, c]
-        gwup_ref[:, c] = tn(h2_ref[...], du).astype(BF16)
-        gbup_ref[0:1, c] = jnp.sum(du.astype(F32), axis=0, keepdims=True)
-
-    cp = exchange(du_ref, wup_ref, 0)
-    loop(f // wide, grads_ff)
-    cp.wait()
-    norm_back(x2_ref, g3_ref, dx2_ref, G2, B2, 0)
-    cp = send_round(dx2_ref, BOUT, 1)
-
-    def da_rows(r):
-        def body(j):
-            c = cols(j, wide)
-            da_ref[r, c] = nt(dm_ref[1, r, :], wout_ref[c, :]).astype(BF16)
-
-        loop(hc // wide, body)
-
-    da_rows(own)
-    cp.wait()
-    da_rows(sib)
-
-    def grads_out(j):
-        c = cols(j, wide)
-        gwout_ref[c, :] = tn(a_ref[:, c], dm_ref[1]).astype(BF16)
-
-    loop(hc // wide, grads_out)
-    mask = mask_ref[:, 0:1] > 0
-
-    def pair(p):
-        cq = pl.ds(pl.multiple_of(p * 128, 128), 128)
-        ck = pl.ds(pl.multiple_of(hc + p * 128, 128), 128)
-        cv = pl.ds(pl.multiple_of(2 * hc + p * 128, 128), 128)
-        q2, k2, v2, da2 = qkv_ref[:, cq], qkv_ref[:, ck], qkv_ref[:, cv], da_ref[:, cq]
-        kt = k2.T
-        dk = dv = None
-        parts = []
-        for a in range(2):
-            qa, daa = half_lanes(q2, a), half_lanes(da2, a)
-            pt = scores_t(k2, qa, mask)
-            dpt = nt(v2, daa)
-            delta = jnp.sum(dpt * pt, axis=0, keepdims=True)
-            dst = (pt * (dpt - delta)).astype(BF16)
-            dva = nn(pt.astype(BF16), daa)
-            dka = nn(dst, qa)
-            parts.append(nn(kt[a * HEAD:(a + 1) * HEAD, :], dst))
-            dk = dka if dk is None else dk + dka
-            dv = dva if dv is None else dv + dva
-        dq = (jnp.concatenate(parts, axis=0).T * HEAD ** -0.5).astype(BF16)
-        dv = dv.astype(BF16)
-        dj_ref[:, cq] = dq
-        dj_ref[:, ck] = dk.astype(BF16)
-        dj_ref[:, cv] = dv
-        gbqkv_ref[0:1, cq] = jnp.sum(dq.astype(F32), axis=0, keepdims=True)
-        gbqkv_ref[0:1, cv] = jnp.sum(dv.astype(F32), axis=0, keepdims=True)
-
-    loop(hc // 128, pair)
-    cp = exchange(dj_ref, wqkv_ref, 1)
-
-    def grads_qkv(j):
-        c = cols(j, wide)
-        gwqkv_ref[:, c] = tn(h1_ref[...], dj_ref[:, c]).astype(BF16)
-
-    loop(3 * hc // wide, grads_qkv)
-    cp.wait()
-    norm_back(x_ref, dx2_ref, g0_ref, G1, B1, 1)
-
-
-def run_bwd(g3, saved, vec, mask, wqkv, wout, wup, wdown):
-    rows, d = g3.shape
-    hc, f = wout.shape[0], wdown.shape[0]
-    both = 2 * rows
-    shapes = [
-        ((rows, d), F32), (wqkv.shape, BF16), (wout.shape, BF16), (wup.shape, BF16), (wdown.shape, BF16),
-        ((8, d), F32), ((8, 3 * hc), F32), ((8, f), F32),
+    number = {chunk: u for u, chunk in enumerate(chunks)}
+
+    stores = dict(
+        z=(zs, z), wdown=(vdown, wdown), gp=(gps, gp), h2=(h2s, h2), wup=(vup, wup), x2=(x2s, x2_ref),
+        wout=(vout, wout), att=(as_, att), qkv=(qkvs, qkv), wqkv=(vqkv, wqkv), h1=(h1s, h1), x=(xs, x_ref),
+    )
+    slots = {name: i for i, name in enumerate(stores)}
+    loads = {}
+
+    def load(name, l):
+        if l < 0:
+            return
+        src, dst = stores[name]
+        loads[name, l] = pltpu.make_async_copy(src.at[l], dst, s_load.at[slots[name]])
+        loads[name, l].start()
+
+    cot_load = pltpu.make_async_copy(cot_ref, tok, s_misc.at[0])
+    cot_load.start()
+    for name in stores:
+        load(name, layers - 1)
+    greet((at.sib, at.xn, at.yn, at.yd, at.zn, at.mid))
+
+    def by_half(hh):
+        return hh * x + (1 - hh) * (1 - x)
+
+    mask = chip_flags(at, tv_ref, rows, seq)
+    valid = jnp.where(x == 0, iv_ref[0:1, 0:1], iv_ref[1:2, 0:1]).astype(F32)
+    weight = mask[:rows].astype(F32) * valid
+    small[...] = jnp.zeros_like(small)
+    cot_load.wait()
+    for i in range(2):
+        for j in range(block // STEP):
+            r = i * block + j * STEP
+            g_ref[pl.ds(r, STEP), :] = tok[i, pl.ds(j * STEP, STEP), :].astype(F32) * weight[r:r + STEP, :]
+
+    for l in reversed(range(layers)):
+        def row(name, l=l):
+            return vec_ref[l * SMALL + name:l * SMALL + name + 1, :]
+
+        def set_small(name, value, l=l):
+            small[l * SMALL + name:l * SMALL + name + 1, :] = value
+
+        def send_round(src_ref, name, slot):
+            total = jnp.zeros((8, d), F32)
+            for i in range(rows // STEP):
+                r = pl.ds(i * STEP, STEP)
+                low = src_ref[r, :].astype(BF16)
+                dm[slot, r, :] = low
+                low = low.astype(F32)
+                total = total + low[0:8, :] + low[8:16, :]
+            set_small(name, jnp.sum(total, axis=0, keepdims=True))
+            copy = remote(dm.at[slot, own], dm.at[slot, other], s_core.at[slot], r_core.at[slot], at.sib)
+            copy.start()
+            return copy
+
+        def exchange(left, w):
+            per = w.shape[1]
+
+            def piece(j):
+                b = j // (per // WIDE)
+                return w[b, span((j % (per // WIDE)) * WIDE, WIDE), :]
+
+            def far(j):
+                put[:, cols(j)] = nt(left[other, :], piece(j)).astype(BF16)
+
+            loop(d // WIDE, far)
+            copy = remote(put, got, s_core.at[2], r_core.at[2], at.sib)
+            copy.start()
+
+            def near(j):
+                dh[:, cols(j)] = nt(left[own, :], piece(j))
+
+            loop(d // WIDE, near)
+            copy.wait()
+
+        def norm_back(value_ref, base_ref, out_ref, gain, shift):
+            total_g = jnp.zeros((8, d), F32)
+            total_b = jnp.zeros((8, d), F32)
+            for i in range(rows // STEP):
+                r = pl.ds(i * STEP, STEP)
+                hat, rstd = norm_rows(value_ref[r, :])
+                grad = dh[r, :] + got[r, :].astype(F32)
+                prod = grad * hat
+                total_g = total_g + prod[0:8, :] + prod[8:16, :]
+                total_b = total_b + grad[0:8, :] + grad[8:16, :]
+                dhat = grad * row(gain)
+                m1 = jnp.mean(dhat, axis=-1, keepdims=True)
+                m2 = jnp.mean(dhat * hat, axis=-1, keepdims=True)
+                out_ref[r, :] = base_ref[r, :] + rstd * (dhat - m1 - hat * m2)
+            set_small(gain, jnp.sum(total_g, axis=0, keepdims=True))
+            set_small(shift, jnp.sum(total_b, axis=0, keepdims=True))
+
+        def produce(chunk, maker, us):
+            u = number[chunk]
+            ring.reserve(u)
+            loop(2, lambda hh: maker(ring_g.at[u % NS, hh], by_half(hh)))
+            ring.launch(u)
+            plan.spend(us)
+
+        copy = send_round(g_ref, BDOWN, 0)
+        loads["z", l].wait()
+        plan.spend(2)
+        copy.wait()
+        for i in range(4):
+            def make(dst, h, i=i):
+                dst[...] = tn(z[:, span(h * (f // 2) + i * CHUNK, CHUNK)], dm[0]).astype(BF16)
+
+            produce(("down", l, i), make, 1.3)
+        load("z", l - 1)
+        loads["wdown", l].wait()
+        loads["gp", l].wait()
+
+        def dz_body(j):
+            b = j // (f // 2 // WIDE)
+            w = wdown[b, span((j % (f // 2 // WIDE)) * WIDE, WIDE), :]
+            for r in (own, other):
+                low = (nt(dm[0, r, :], w) * gp[r, cols(j)].astype(F32)).astype(BF16)
+                gp[r, cols(j)] = low
+
+        loop(f // WIDE, dz_body)
+        plan.spend(4)
+        load("wdown", l - 1)
+        for j in range(f // WIDE):
+            half, sub = divmod(j, f // WIDE // 2)
+            small[l * SMALL + BUP + sub:l * SMALL + BUP + sub + 1, span((2 * half + c) * WIDE, WIDE)] = jnp.sum(
+                gp[:, j * WIDE:(j + 1) * WIDE].astype(F32), axis=0, keepdims=True
+            )
+        loads["h2", l].wait()
+        loads["wup", l].wait()
+        for i in range(4):
+            side, run = divmod(i, 2)
+
+            def make(dst, h, side=side, run=run):
+                rh = c if side == 0 else 1 - c
+                left = h2[:, span(h * (d // 2) + rh * CHUNK, CHUNK)]
+                dst[...] = tn(left, gp[:, run * (f // 2):(run + 1) * (f // 2)]).astype(BF16)
+
+            if i == 2:
+                exchange(gp, wup)
+                load("wup", l - 1)
+                loads["x2", l].wait()
+                plan.spend(4)
+                norm_back(x2_ref, g_ref, dx2, G2, B2)
+                load("x2", l - 1)
+                plan.spend(3)
+                copy = send_round(dx2, BOUT, 1)
+            produce(("up", l, i), make, 1.3)
+        load("gp", l - 1)
+        load("h2", l - 1)
+
+        loads["wout", l].wait()
+        loads["att", l].wait()
+        copy.wait()
+        for j in range(hc // WIDE):
+            for r in (own, other):
+                da[r, pl.ds(j * WIDE, WIDE)] = nt(dm[1, r, :], wout[j]).astype(BF16)
+        load("wout", l - 1)
+
+        def make(dst, h):
+            dst[...] = tn(att[:, span(h * CHUNK, CHUNK)], dm[1]).astype(BF16)
+
+        produce(("out", l, 0), make, 2)
+        load("att", l - 1)
+        loads["qkv", l].wait()
+        sums = {}
+        for p in range(hc // 128):
+            cq, ck, cv = (pl.ds(k * hc + p * 128, 128) for k in range(3))
+            q2, k2, v2, da2 = qkv[:, cq], qkv[:, ck], qkv[:, cv], da[:, cq]
+            kt = k2.T
+            dk = dv = None
+            parts = []
+            for a in range(2):
+                qa, daa = half_lanes(q2, a), half_lanes(da2, a)
+                pt = scores_t(k2, qa, mask)
+                dpt = nt(v2, daa)
+                delta = jnp.sum(dpt * pt, axis=0, keepdims=True)
+                dst = (pt * (dpt - delta)).astype(BF16)
+                dva = nn(pt.astype(BF16), daa)
+                dka = nn(dst, qa)
+                parts.append(nn(kt[a * HEAD:(a + 1) * HEAD, :], dst))
+                dk = dka if dk is None else dk + dka
+                dv = dva if dv is None else dv + dva
+            dq = (jnp.concatenate(parts, axis=0).T * HEAD ** -0.5).astype(BF16)
+            dv = dv.astype(BF16)
+            dj[:, cq] = dq
+            dj[:, ck] = dk.astype(BF16)
+            dj[:, cv] = dv
+            for k, value in ((0, dq), (1, dv)):
+                total = jnp.sum(value.astype(F32), axis=0, keepdims=True)
+                for core in range(2):
+                    r = l * SMALL + BQV + core
+                    small[r:r + 1, k * hc + p * 128:k * hc + (p + 1) * 128] = jnp.where(
+                        c == core, total, jnp.zeros_like(total)
+                    )
+            plan.spend(5.5)
+        load("qkv", l - 1)
+        loads["wqkv", l].wait()
+        loads["h1", l].wait()
+        for i in range(3):
+            def make(dst, h, i=i):
+                for side in range(2):
+                    rh = c if side == 0 else 1 - c
+                    left = h1[:, span(h * (d // 2) + rh * CHUNK, CHUNK)]
+                    dst[:, side * hc:(side + 1) * hc] = tn(left, dj[:, i * hc:(i + 1) * hc]).astype(BF16)
+
+            if i == 1:
+                exchange(dj, wqkv)
+                load("wqkv", l - 1)
+                loads["x", l].wait()
+                plan.spend(4)
+                norm_back(x_ref, dx2, g_ref, G1, B1)
+                load("x", l - 1)
+                plan.spend(3)
+            produce(("qkv", l, i), make, 1.3)
+        load("h1", l - 1)
+
+    for i in range(2):
+        for j in range(block // STEP):
+            tok[i, pl.ds(j * STEP, STEP), :] = g_ref[pl.ds(i * block + j * STEP, STEP), :].astype(BF16)
+    back = [
+        remote(tok.at[1], otok.at[x], s_misc.at[1], r_misc.at[1], at.xn),
+        pltpu.make_async_copy(tok.at[0], otok.at[x], s_misc.at[2]),
     ]
-    args = (g3, *saved, vec, mask, wqkv, wout, wup, wdown)
+    small_put[...] = small[...].astype(BF16)
+    copy = remote(small_put, small_got, s_misc.at[3], r_misc.at[3], at.sib)
+    copy.start()
+    copy.wait()
+    total = (small_put[...].astype(F32) + small_got[...].astype(F32)).astype(BF16)
+    u = number["small", 0, 0]
+    ring.reserve(u)
+    n = total.shape[0]
+    for hh in range(2):
+        for k in range(2):
+            ring_g[u % NS, hh, k * n:(k + 1) * n, :] = total
+    ring.launch(u)
+    for copy in back:
+        copy.start()
+    ring.finish()
+    for copy in back:
+        copy.wait()
+
+
+def run_bwd(cot, vec, tv, iv, weights, acts, seq):
+    layers, _, n, hc3 = weights[0].shape
+    d = acts[0].shape[2]
+    rows = acts[0].shape[1]
+    block, both = rows // 2, 2 * rows
+    hc, f = hc3 // 3, weights[2].shape[3]
+    outs = [(layers, n, 3 * d), (layers, n, d), (layers, n, 2 * f), (layers, f // 2, d), (layers * SMALL, d), (2, block, d)]
+    args = (cot, vec, tv, iv, *weights, *acts)
     return pl.pallas_call(
-        bwd_kernel,
-        out_shape=[jax.ShapeDtypeStruct(s, t) for s, t in shapes],
-        in_specs=[VM] * len(args),
-        out_specs=[VM] * len(shapes),
-        scratch_shapes=[
-            pltpu.VMEM((2, both, d), BF16), pltpu.VMEM((both, f), BF16), pltpu.VMEM((both, hc), BF16),
-            pltpu.VMEM((both, 3 * hc), BF16), pltpu.VMEM((rows, d), F32), pltpu.VMEM((rows, d), F32),
-            pltpu.VMEM((2, rows, d), BF16), pltpu.VMEM((2, rows, d), BF16),
-            pltpu.SemaphoreType.DMA((4,)), pltpu.SemaphoreType.DMA((4,)),
-        ],
+        functools.partial(bwd_kernel, seq),
+        out_shape=[jax.ShapeDtypeStruct(s, BF16) for s in outs],
+        in_specs=[ANY, VM, VM, VM] + [ANY] * 12,
+        out_specs=[ANY] * len(outs),
+        scratch_shapes=[pltpu.VMEM(w.shape[1:], w.dtype) for w in (*weights, *acts)]
+        + [
+            pltpu.VMEM((2, block, d), BF16), pltpu.VMEM((rows, d), F32), pltpu.VMEM((2, both, d), BF16),
+            pltpu.VMEM((both, hc), BF16), pltpu.VMEM((both, 3 * hc), BF16), pltpu.VMEM((rows, d), F32),
+            pltpu.VMEM((rows, d), F32), pltpu.VMEM((rows, d), BF16), pltpu.VMEM((rows, d), BF16),
+            pltpu.VMEM((layers * SMALL, d), F32), pltpu.VMEM((layers * SMALL, d), BF16),
+            pltpu.VMEM((layers * SMALL, d), BF16),
+            pltpu.VMEM((NS, 2, CHUNK, d), BF16), pltpu.VMEM((NS, CHUNK, d), BF16),
+            pltpu.VMEM((NY, CHUNK // 2, d), BF16), pltpu.VMEM((NZ, CHUNK // 2, d), BF16),
+            pltpu.VMEM((NZ, CHUNK // 2, d), BF16), pltpu.VMEM((NT, CHUNK // 2, d), BF16),
+            dma(12), dma(3), dma(3), dma(4), dma(4),
+            dma(NS), dma(NS), dma(NS), dma(NY), dma(NT), dma(NZ), dma(NT), dma(NZ), dma(NT), dma(4),
+        ]
+        + [pltpu.SemaphoreType.REGULAR] * 5,
         compiler_params=pltpu.CompilerParams(
-            collective_id=2, has_side_effects=True, vmem_limit_bytes=int(63.5 * 2**20)
+            collective_id=2, has_side_effects=True, vmem_limit_bytes=VMEM_LIMIT
         ),
-        cost_estimate=pl.CostEstimate(flops=17 * 10**9, bytes_accessed=40 * 10**6, transcendentals=0),
-        name="layer_bwd",
+        cost_estimate=pl.CostEstimate(flops=34 * 10**9, bytes_accessed=120 * 10**6, transcendentals=0),
+        name="backward",
     )(*args)
-
-
-def swap(value, bit):
-    return lax.ppermute(value, "grp", [(i, i ^ bit) for i in range(4)])
-
-
-def pick(value, index, axis):
-    return lax.dynamic_index_in_dim(value, index, axis, keepdims=False)
 
 
 def local(
@@ -674,89 +952,38 @@
     norm1_gain, norm1_bias, w_qkv, b_qv, w_out, b_out, norm2_gain, norm2_bias, w_up, b_up, w_down, b_down,
 ):
     grp = lax.axis_index("grp")
-    x, c = grp // 2, grp % 2
-    layers, dq, d3 = w_qkv.shape
-    d = d3 // 3
-    hc = d // 2
-    f = 2 * w_down.shape[1] * 1
-    seq = tokens.shape[1]
+    layers, n, _ = w_qkv.shape
+    seq, d = tokens.shape[1:]
     block = -(-seq // 32) * 32
-    rows = 2 * block
-
 
     def pad(value):
         return jnp.pad(value, ((0, 0), (0, block - seq), (0, 0)))
 
-    layer_rows = [
-        w.reshape(layers, -1, d // 4)
-        for w in (norm1_gain, norm1_bias, b_out, norm2_gain, norm2_bias, b_down, b_qv, b_up)
-    ]
-    pack = jnp.concatenate(layer_rows, axis=1).astype(F32)
+    smalls = (norm1_gain, norm1_bias, b_out, norm2_gain, norm2_bias, b_down, b_qv, b_up)
+    pack = jnp.concatenate([w.reshape(layers, -1, d // 4) for w in smalls], axis=1).astype(F32)
     pack = jnp.pad(pack, ((0, 0), (0, SMALL - pack.shape[1]), (0, 0))).reshape(layers * SMALL, d // 4)
-    (vqkv, vout, vup, vdown, xs, x2s, h1s, qkvs, atts, h2s, zs, gps, cot, act, vec) = run_fwd(
-        pad(tokens), pad(cotangent), pack, token_valid, w_qkv, w_out, w_up, w_down, seq
+    res = run_fwd(pad(tokens), pad(cotangent), pack, token_valid, w_qkv, w_out, w_up, w_down, seq)
+    weights, acts, (cot, act, vec) = res[:4], res[4:12], res[12:]
+    gqkv, gout, gup, gdown, gsmall, gtok = run_bwd(
+        cot, vec, token_valid, image_valid[:, None], weights, acts, seq
     )
-    smalls = [norm1_gain, norm1_bias, b_out, norm2_gain, norm2_bias, b_down, b_qv, b_up]
-    widths = [s.shape[1] for s in smalls]
-    activations = act[:, :seq]
-    flags = pick(token_valid, x, 0).reshape(2, 2, seq)
-    pf = lambda a: jnp.pad(a, (0, block - seq))
-    own_flags = jnp.concatenate([pf(pick(pick(flags, x, 0), c, 0)), pf(pick(pick(flags, 1 - x, 0), c, 0))])
-    sib_flags = jnp.concatenate([pf(pick(pick(flags, x, 0), 1 - c, 0)), pf(pick(pick(flags, 1 - x, 0), 1 - c, 0))])
-    mask = jnp.broadcast_to(jnp.concatenate([own_flags, sib_flags])[:, None], (2 * rows, 128))
-    weight = (own_flags * pick(image_valid, x, 0)).astype(F32)
-    flow = cot.reshape(rows, d).astype(F32) * weight[:, None]
-    vecs = vec.reshape(layers, SMALL, d)[:, :8]
-    grads = [None] * layers
-    for l in reversed(range(layers)):
-        saved = (xs[l], x2s[l], h1s[l], qkvs[l], atts[l], h2s[l], zs[l], gps[l])
-        wq, wo, wu, wd = (w[l].reshape(-1, w.shape[-1]) for w in (vqkv, vout, vup, vdown))
-        flow, *grads[l] = run_bwd(flow, saved, vecs[l], mask, wq, wo, wu, wd)
-
-    def give_back(value):
-        value = value.astype(BF16).reshape(2, block, d)[:, :seq]
-        got = swap(value[1], 2)
-        return jnp.where(x == 0, jnp.stack([value[0], got]), jnp.stack([got, value[0]]))
-
-    grad_tokens = give_back(flow)
-
-    def reduce_big(index):
-        g = jnp.stack([grads[l][index] for l in range(layers)])
-        n = g.shape[1] // 2
-        keep = lax.dynamic_slice_in_dim(g, x * n, n, 1)
-        give = lax.dynamic_slice_in_dim(g, (1 - x) * n, n, 1)
-        total = (keep.astype(F32) + swap(give, 2).astype(F32)).astype(BF16)
-        return lax.psum(total, "rep")
-
-    def uncolumns(g, groups):
-        n = g.shape[1] // 2
-        keep = lax.dynamic_slice_in_dim(g, c * n, n, 1)
-        give = lax.dynamic_slice_in_dim(g, (1 - c) * n, n, 1)
-        got = swap(give, 1)
-        keep = keep.reshape(layers, n, groups, 2, -1)
-        got = got.reshape(layers, n, groups, 2, -1)
-        return jnp.where(c == 0, jnp.stack([keep, got], axis=4), jnp.stack([got, keep], axis=4)).reshape(layers, n, -1).astype(F32)
-
-    gqkv = uncolumns(reduce_big(0), 3)
-    gout = reduce_big(1).astype(F32)
-    gup = uncolumns(reduce_big(2), 1)
-    gdown = reduce_big(3).astype(F32)
-
-    gvec = jnp.stack([grads[l][4][:6].reshape(6 * d) for l in range(layers)])
-    gb = jnp.stack([grads[l][5][0] for l in range(layers)]).reshape(layers, 3, 2, -1)[:, ::2]
-    gu = jnp.stack([grads[l][6][0] for l in range(layers)]).reshape(layers, 2, -1)
-
-    def spread(v):
-        z = jnp.zeros_like(v)
-        return jnp.where(c == 0, jnp.stack([v, z], axis=-2), jnp.stack([z, v], axis=-2)).reshape(layers, -1)
-
-    small = lax.psum(jnp.concatenate([gvec, spread(gb), spread(gu)], axis=1), ("rep", "grp"))
+    blocks = lax.axis_size("rep") // 8
+    if blocks > 1:
+        groups = [[i + 8 * b for b in range(blocks)] for i in range(8)]
+        gqkv, gout, gup, gdown, gsmall = (
+            lax.psum(g, "rep", axis_index_groups=groups) for g in (gqkv, gout, gup, gdown, gsmall)
+        )
+    gsmall = lax.dynamic_slice_in_dim(gsmall, grp * (d // 4), d // 4, 1).astype(F32).reshape(layers, SMALL, d // 4)
     outs, at = [], 0
-    for width in widths:
-        outs.append(lax.dynamic_slice_in_dim(small[:, at:at + 4 * width], grp * width, width, 1))
-        at += 4 * width
+    for w in smalls:
+        take = w.shape[1] // (d // 4)
+        outs.append(gsmall[:, at:at + take].reshape(layers, -1))
+        at += take
     gg1, gb1, gbout, gg2, gb2, gbdown, gbqv, gbup = outs
-    return (activations, grad_tokens, gg1, gb1, gqkv, gbqv, gout, gbout, gg2, gb2, gup, gbup, gdown, gbdown)
+    return (
+        act[:, :seq], gtok[:, :seq], gg1, gb1, gqkv.astype(F32), gbqv, gout.astype(F32), gbout, gg2, gb2,
+        gup.astype(F32), gbup, gdown.astype(F32), gbdown,
+    )
 
 
 def solution(mesh):

time: 1250 us -> 561 us (0.45)
  waiting for transfers between devices: 772 us -> 0 us
  Pallas kernels: 278 us -> 520 us
  local copies, waits for them, and re-layouts: 118 us -> 13.9 us
  other arithmetic: 49.6 us -> 16.7 us
  between operations: 16.5 us -> 1.08 us
    psum x2 -> x0, waiting for transfers between devices: 512 us -> none  [the longest x1 397 us: reduce_big(): return lax.psum(total, 'rep')]
    ppermute x7 -> x0, waiting for transfers between devices: 260 us -> none  [swap(): return lax.ppermute(value, 'grp', [(i, i ^ bit) for i in range(4)])]
    pallas_call x2 -> x1, Pallas kernels: 118 us -> 359 us  [run_bwd(): pl.pallas_call(functools.partial(bwd_kernel, seq), out_shape=[jax.ShapeDt...]
    unnamed x88 -> x32, local copies, waits for them, and re-layouts: 26.2 us -> 6.57 us
    another operation x8 -> x0, local copies, waits for them, and re-layouts: 18.6 us -> none  [the longest x6 18.6 us: uncolumns(): jnp.stack([keep, got], axis=4)]
    squeeze x6 -> x0, local copies, waits for them, and re-layouts: 18.1 us -> none  [the longest x5 17.5 us: local(): saved = (xs[l], x2s[l], h1s[l], qkvs[l], atts[l], h2s[l], zs[l], gps[l])]
    slice x13 -> x3, local copies, waits for them, and re-layouts: 20.3 us -> 2.26 us  [the longest x1 1.12 us: local(): act[:, :seq]]
    convert_element_type x10 -> x4, other arithmetic: 33 us -> 16 us  [the longest x1 5.54 us: local(): gqkv.astype(F32)]
  transfers between devices with their start and end apart: 9 -> 0, of which waited for: 3 -> 0; matrix products, arithmetic and copies ran while one was open for 6% -> 0% of each run, Pallas kernels for 0% -> 0%
where the time goes in v3:
time: 561 us; the launch traced here: 551 us
  Pallas kernels  520 us (93%)
  other arithmetic  16.7 us (3%)
  local copies, waits for them, and re-layouts  13.9 us (2%)
    pallas_call x1, Pallas kernels, run_bwd(): pl.pallas_call(functools.partial(bwd_kernel, seq), out_shape=[jax.ShapeDt...  359 us
    pallas_call x1, Pallas kernels, run_fwd(): pl.pallas_call(functools.partial(fwd_kernel, seq), out_shape=[jax.ShapeDt...  160 us

profile of v3, /device:TPU:0, one launch (start us, length us, event | category | flops | bytes accessed | tf_op | source)
XLA Modules:
  0.0 551.2 jit_solution(7559114979228109637)
XLA Ops:
  0.6 0.0 copy-start.5
  0.7 0.0 copy-start.6
  0.7 0.0 copy-start.7
  0.7 0.0 copy-start.8
  0.7 0.0 copy-start.9
  0.7 0.0 copy-start.10
  0.7 0.0 copy-start.4
  0.7 0.0 copy-start.3
  0.7 1.3 copy.30
  2.0 0.9 pad.12.tok_ref
  2.9 1.2 copy.31
  4.1 0.9 pad.13.cot_ref
  5.0 0.0 copy-done.5
  5.0 0.0 copy-done.6
  5.0 0.0 copy-done.7
  5.1 0.0 copy-done.8
  5.1 0.0 copy-done.9
  5.1 0.0 copy-done.10
  5.1 0.0 copy-done.4
  5.1 0.0 copy-done.3
  5.2 0.1 concatenate.3
  5.2 0.6 bitcast_convert_fusion.pack_ref
  5.9 0.0 copy-start.11
  5.9 160.2 %forward.1 = (bf16[2,4,256,1536]{3,2,1,0:T(8,128)(2,1)}, bf16[2,2,256,1024]{3,2,1,0:T(8,128)(2,1)}, bf16[2,4,256,2048]{3,2,1,0:T(8,128)(2,1)}, bf16[2,2,1024,102...) custom-call(bf16[2,160,1024]{2,1,0:T(8,128)(2,1)} %pad.12.tok_ref, ...), custom_call_target="tpu_custom_call" | custom-call | flops 16999999488 | bytes 80000000 | tf_op jit(solution)/shard_map/forward/pallas_call | solution.py:449
  166.1 1.1 slice.30
  167.2 1.4 copy.45
  168.6 0.0 copy-done.11
  168.6 0.6 copy.38.iv_ref
  169.3 359.4 %backward.1 = (bf16[2,256,3072]{2,1,0:T(8,128)(2,1)}, bf16[2,256,1024]{2,1,0:T(8,128)(2,1)}, bf16[2,256,4096]{2,1,0:T(8,128)(2,1)}, bf16[2,1024,1024]{2,1,0:T(8,...) custom-call(bf16[2,160,1024]{2,1,0:T(8,128)(2,1)} %get-tuple-element.36.cot_ref, ...), custom_call_target="tpu_custom_call" | custom-call | flops 33999998976 | bytes 120000000 | tf_op jit(solution)/shard_map/backward/pallas_call | solution.py:923
  528.7 1.1 slice.31
  529.8 1.4 copy.46
  531.3 0.7 constant_dynamic-slice_fusion
  532.0 0.6 copy_bitcast_fusion.4
  532.6 0.0 copy-start.2
  532.6 0.0 copy-start.1
  532.6 5.5 %convert_element_type.19 = f32[2,256,3072]{2,1,0:T(8,128)} convert(bf16[2,256,3072]{2,1,0:T(8,128)(2,1)} %get-tuple-element.52) | non-fusion elementwise | flops 1572864 | bytes 9437184 | tf_op jit(solution)/shard_map/convert_element_type | solution.py:984
  538.1 0.6 copy.53
  538.7 0.0 copy-done.2
  538.7 1.6 convert_element_type.20
  540.3 0.6 copy_bitcast_fusion.2
  540.9 0.6 copy_bitcast_fusion
  541.5 0.0 copy-done.1
  541.5 0.0 copy-start
  541.5 4.5 convert_element_type.21
  546.0 0.6 copy.54
  546.6 0.0 copy-done
  546.6 4.4 convert_element_type.22
  (13 shorter events, 0.1 us)
Async XLA Ops:
  0.6 4.4 copy-start.5
  0.7 4.4 copy-start.6
  0.7 4.4 copy-start.7
  0.7 4.4 copy-start.8
  0.7 4.4 copy-start.9
  0.7 4.4 copy-start.10
  0.7 4.4 copy-start.4
  0.7 4.4 copy-start.3
  5.9 162.8 %copy-start.11 = (s32[2]{0:T(128)S(1)}, s32[2]{0:T(128)}, u32[]{:S(2)}) copy-start(s32[2]{0:T(128)} %param.18) | copy-start | bytes 28
  532.6 6.2 %copy-start.2 = (bf16[2,256,1024]{2,1,0:T(8,128)(2,1)S(1)}, bf16[2,256,1024]{2,1,0:T(8,128)(2,1)}, u32[]{:S(2)}) copy-start(bf16[2,256,1024]{2,1,0:T(8,128)(2,1)} %get-tuple-element.53) | copy-start | bytes 3145732
  532.6 8.9 %copy-start.1 = (bf16[2,256,4096]{2,1,0:T(8,128)(2,1)S(1)}, bf16[2,256,4096]{2,1,0:T(8,128)(2,1)}, u32[]{:S(2)}) copy-start(bf16[2,256,4096]{2,1,0:T(8,128)(2,1)} %get-tuple-element.54) | copy-start | bytes 12582916
  541.5 5.1 copy-start

commit v4 on v3

--- a/solution.py
+++ b/solution.py
@@ -16,6 +16,7 @@
 STEP = 16
 G1, B1, BOUT, G2, B2, BDOWN, BQV, BUP = 0, 1, 2, 3, 4, 5, 6, 8
 SMALL = 16
+WIDER = ("down",)
 
 
 def nn(a, b):
@@ -148,9 +149,9 @@
 
 
 def fwd_kernel(
-    seq, tok_ref, cot_ref, pack_ref, tv_ref, wqkv_in, wout_in, wup_in, wdown_in,
-    vqkv, vout, vup, vdown, xs, x2s, h1s, qkvs, as_, h2s, zs, gps, cot_out, act_out, vec_out,
-    wqkv, wout, wup, wdown, x_ref, x2_ref, h1, qkv, att, h2, z, gp, put, got, tok, vec, bup,
+    seq, tok_ref, cot_ref, g1_in, b1_in, bo_in, g2_in, b2_in, bd_in, bqv_in, bup_in, tv_ref, iv_ref, wqkv_in, wout_in, wup_in, wdown_in,
+    vqkv, vout, vup, vdown, xs, x2s, h1s, qkvs, as_, h2s, zs, gps, dm_out, act_out, vec_out,
+    wqkv, wout, wup, wdown, x_ref, x2_ref, h1, qkv, att, h2, z, gp, put, got, tok, vec, bup, cot, dm, pack_ref,
     s_rx, s_ry, s_rz, s_ra, s_rb, s_rs, s_loc, s_send, s_core, r_core, s_save, s_misc, r_misc,
 ):
     at = Place()
@@ -171,21 +172,30 @@
         for kind in KINDS:
             index[l, kind] = len(index)
 
+    at_row = 0
+    for ref in (g1_in, b1_in, bo_in, g2_in, b2_in, bd_in, bqv_in, bup_in):
+        values = ref[...].astype(F32)
+        for j in range(ref.shape[1] // WIDE):
+            for l in range(layers):
+                pack_ref[l * SMALL + at_row:l * SMALL + at_row + 1, :] = values[l:l + 1, j * WIDE:(j + 1) * WIDE]
+            at_row += 1
+    for l in range(layers):
+        pack_ref[l * SMALL + at_row:(l + 1) * SMALL, :] = jnp.zeros((SMALL - at_row, WIDE), F32)
     greet((at.sib, at.xn, at.xd, at.yn, at.zn))
 
-    first = [
-        remote(tok_ref.at[1 - x], tok.at[1], s_misc.at[0], r_misc.at[0], at.xn),
-        pltpu.make_async_copy(tok_ref.at[x], tok.at[0], s_misc.at[3]),
-    ]
     here = vec.at[:, span(at.grp * WIDE, WIDE)]
-    first += [
+    packs = [
         pltpu.make_async_copy(pack_ref, here, s_misc.at[4]),
         remote(pack_ref, here, s_misc.at[5], r_misc.at[5], at.sib),
         remote(pack_ref, here, s_misc.at[6], r_misc.at[6], at.xn),
         remote(pack_ref, here, s_misc.at[7], r_misc.at[7], at.xd),
     ]
-    for copy in first:
+    for copy in packs:
         copy.start()
+
+    def wider_parts(kind, y=at.y, zlow=at.zlow):
+        q = full[kind].shape[2] // 4
+        return span(y * q, q), span((2 + zlow) * q, q)
 
     def launch(l, kind):
         i = index[l, kind]
@@ -209,7 +219,8 @@
                 remote(src.at[:, give], dst.at[mine, :, to], s_send.at[i], s_rs.at[i], at.sib).start()
                 pltpu.make_async_copy(src.at[:, keep], dst.at[mine, :, to], s_loc.at[i]).start()
         else:
-            remote(src.at[part], dst.at[x, part], s_send.at[i], s_rx.at[i], at.xn).start()
+            for part in wider_parts(kind) if kind in WIDER else (part,):
+                remote(src.at[part], dst.at[x, part], s_send.at[i], s_rx.at[i], at.xn).start()
             pltpu.make_async_copy(src, dst.at[x], s_loc.at[i]).start()
 
     def theirs(l, kind, part):
@@ -226,6 +237,12 @@
 
     def relay1(l, kind):
         i = index[l, kind]
+        if kind in WIDER:
+            settle(theirs(l, kind, pl.ds(0, full[kind].shape[2] // 2)), s_rx.at[i])
+            by_y, by_z = (theirs(l, kind, part) for part in wider_parts(kind))
+            remote(by_y, by_y, s_send.at[i], s_ry.at[i], at.yn).start()
+            remote(by_z, by_z, s_send.at[i], s_rz.at[i], at.zn).start()
+            return
         piece = theirs(l, kind, part_of(kind, at.y, at.zlow))
         settle(piece, s_rx.at[i])
         remote(piece, piece, s_send.at[i], s_ry.at[i], at.yn).start()
@@ -242,40 +259,77 @@
 
     def ready(l, kind):
         i = index[l, kind]
-        settle(theirs(l, kind, part_of(kind, 1 - at.y, 1 - at.zlow, 0)), s_ra.at[i])
-        settle(theirs(l, kind, part_of(kind, 1 - at.y, 1 - at.zlow, 1)), s_rb.at[i])
+        if kind in WIDER:
+            by_y, by_z = (theirs(l, kind, part) for part in wider_parts(kind, 1 - at.y, 1 - at.zlow))
+            settle(by_y, s_ry.at[i])
+            settle(by_z, s_rz.at[i])
+        else:
+            settle(theirs(l, kind, part_of(kind, 1 - at.y, 1 - at.zlow, 0)), s_ra.at[i])
+            settle(theirs(l, kind, part_of(kind, 1 - at.y, 1 - at.zlow, 1)), s_rb.at[i])
         if kind in runs:
             settle(full[kind].at[l, 0], s_rs.at[i])
         settle(full[kind].at[l, 0], s_loc.at[i])
         pltpu.make_async_copy(full[kind].at[l], saves[kind].at[l], s_loc.at[i]).start()
 
-    x_time, yz_time = 9.0, 16.0
-    for l in range(layers):
-        for kind in KINDS:
-            launch(l, kind)
-            mb = full[kind].shape[1] * full[kind].shape[2] * full[kind].shape[3] / 2**20
-            mb *= 2
-            x_time += mb / 4 / 0.094 * 1.05
-            plan.add(x_time + 1.5, ("r1", l, kind), functools.partial(relay1, l, kind))
-            yz_time = max(yz_time, x_time + 1.5)
-            plan.add(yz_time + mb / 4 / 0.094 + 1.5, ("r2", l, kind), functools.partial(relay2, l, kind))
-            yz_time += mb * 3 / 8 / 0.094 * 1.05
-            plan.add(yz_time + 4, ("ok", l, kind), functools.partial(ready, l, kind))
-    plan.order()
+    line = list(index)
+    tokens = [
+        remote(tok_ref.at[1 - x], tok.at[1], s_misc.at[0], r_misc.at[0], at.xn),
+        pltpu.make_async_copy(tok_ref.at[x], tok.at[0], s_misc.at[3]),
+    ]
+    x_time, yz_time = 4.0, 0.0
+    for n, (l, kind) in enumerate(line):
+        if n == 2:
+            for copy in tokens:
+                copy.start()
+            x_time += 7.3
+        launch(l, kind)
+        mb = 2 * full[kind].shape[1] * full[kind].shape[2] * full[kind].shape[3] / 2**20
+        hop = mb / 4 / 0.094 * 1.05
+        x_time += 2 * hop if kind in WIDER else hop
+        plan.add(x_time + 1, ("r1", l, kind), functools.partial(relay1, l, kind))
+        yz_time = max(yz_time, x_time + 1.5)
+        if kind in WIDER:
+            yz_time += hop
+        else:
+            plan.add(yz_time + hop + 1.5, ("r2", l, kind), functools.partial(relay2, l, kind))
+            yz_time += 1.5 * hop
+        plan.add(yz_time + 3, ("ok", l, kind), functools.partial(ready, l, kind))
     late = [
-        remote(cot_ref.at[1 - x], cot_out.at[1], s_misc.at[1], r_misc.at[1], at.xn),
-        pltpu.make_async_copy(cot_ref.at[x], cot_out.at[0], s_misc.at[8]),
+        remote(cot_ref.at[1 - x], cot.at[1], s_misc.at[1], r_misc.at[1], at.xn),
+        pltpu.make_async_copy(cot_ref.at[x], cot.at[0], s_misc.at[8]),
     ]
     for copy in late:
         copy.start()
-
-    first[1].wait()
-    first[2].wait()
-    for copy in (first[0], *first[3:]):
+    mask = chip_flags(at, tv_ref, rows, seq)
+    saved = []
+
+    def seed():
+        for copy in late:
+            copy.wait()
+        valid = jnp.where(x == 0, iv_ref[0:1, 0:1], iv_ref[0:1, 1:2]).astype(F32)
+        weight = mask[:rows].astype(F32) * valid
+        for i in range(2):
+            for j in range(block // STEP):
+                r = i * block + j * STEP
+                dm[pl.ds(r, STEP), :] = (
+                    cot[i, pl.ds(j * STEP, STEP), :].astype(F32) * weight[r:r + STEP, :]
+                ).astype(BF16)
+        copy = remote(dm.at[own], dm.at[other], s_misc.at[2], r_misc.at[2], at.sib)
+        copy.start()
+        saved.append(copy)
+
+    def seeded():
+        saved[0].wait()
+        copy = pltpu.make_async_copy(dm, dm_out, s_misc.at[10])
+        copy.start()
+        saved.append(copy)
+
+    plan.add(x_time + 9, "seed", seed)
+    plan.add(x_time + 14, "seeded", seeded)
+    plan.order()
+
+    for copy in packs:
         copy.wait()
-    for i in range(2):
-        for j in range(block // STEP):
-            x_ref[pl.ds(i * block + j * STEP, STEP), :] = tok[i, pl.ds(j * STEP, STEP), :].astype(F32)
     vec_save = pltpu.make_async_copy(vec, vec_out, s_misc.at[9])
     vec_save.start()
     for l in range(layers):
@@ -284,9 +338,14 @@
             bup[l:l + 1, pl.ds(j * WIDE, WIDE)] = vec[
                 l * SMALL + BUP + sub:l * SMALL + BUP + sub + 1, span((2 * half + c) * WIDE, WIDE)
             ]
-    mask = chip_flags(at, tv_ref, rows, seq)
-    plan.now = 12.0
+    plan.now = 18.0
     plan.poll()
+    for copy in tokens:
+        copy.wait()
+    for i in range(2):
+        for j in range(block // STEP):
+            x_ref[pl.ds(i * block + j * STEP, STEP), :] = tok[i, pl.ds(j * STEP, STEP), :].astype(F32)
+    plan.spend(1)
 
     def save(src, dst, slot):
         copy = pltpu.make_async_copy(src, dst, s_save.at[slot])
@@ -328,14 +387,13 @@
                     cs = pl.ds(base + j * WIDE, WIDE)
                     out = nn(h1[r, :], weight("qkv", cs))
                     qkv[r, cs] = (out * factor + bias[:, j * WIDE:(j + 1) * WIDE]).astype(BF16)
+                    plan.spend(0.35)
 
         qkv_rows(own)
-        plan.spend(2)
         cp.wait()
         qkv_rows(other)
         h1_saved = save(h1, h1s.at[l], 1)
         pending["qkv"] = save(qkv, qkvs.at[l], 2)
-        plan.spend(2)
         if l:
             pending["att"].wait()
         for p in range(hc // 128):
@@ -347,8 +405,8 @@
             for a in range(2):
                 pt = scores_t(k2, half_lanes(q2, a), mask)
                 outs.append(nn(vt[a * HEAD:(a + 1) * HEAD, :], pt.astype(BF16)))
+                plan.spend(1.4)
             att[:, p * 128:(p + 1) * 128] = jnp.concatenate(outs, axis=0).T.astype(BF16)
-            plan.spend(3)
         pending["att"] = save(att, as_.at[l], 3)
 
         def exchange(left, kind, base, bias, out, slot):
@@ -358,6 +416,7 @@
             loop(d // WIDE, far)
             cp = remote(put, got.at[slot], s_core.at[1], r_core.at[1], at.sib)
             cp.start()
+            plan.spend(1)
 
             def near(j):
                 out[:, cols(j)] = nn(left[own, :], weight(kind, cols(j))) + base[:, cols(j)] + vec[
@@ -365,15 +424,16 @@
                 ]
 
             loop(d // WIDE, near)
+            plan.spend(1)
             cp.wait()
             out[...] += got[slot].astype(F32)
+            plan.spend(1)
 
         plan.need(("ok", l, "out"))
         if l:
             pending["x2"].wait()
         exchange(att, "out", x_ref, BOUT, x2_ref, 0)
         pending["x2"] = save(x2_ref, x2s.at[l], 4)
-        plan.spend(3)
         norm_out(x2_ref, h2, G2, B2)
         cp = remote(h2.at[own], h2.at[other], s_core.at[2], r_core.at[2], at.sib)
         cp.start()
@@ -390,32 +450,29 @@
                 z[r, cols(j)] = (u * phi).astype(BF16)
                 gp[r, cols(j)] = (phi + u * jnp.exp(u * u * -0.5) * 0.3989422804014327).astype(BF16)
 
-            loop(f // WIDE, body)
+            for part in range(2):
+                loop(f // WIDE // 2, lambda j: body(j + part * (f // WIDE // 2)))
+                plan.spend(1.9)
 
         up_rows(own)
-        plan.spend(4)
         cp.wait()
         up_rows(other)
         h2_saved = save(h2, h2s.at[l], 5)
         pending["z"] = save(z, zs.at[l], 6)
         pending["gp"] = save(gp, gps.at[l], 7)
-        plan.spend(4)
         plan.need(("ok", l, "down"))
         for copy in (x_saved, h1_saved, h2_saved):
             copy.wait()
         exchange(z, "down", x2_ref, BDOWN, x_ref, 1)
-        plan.spend(4)
 
     for i in range(2):
         for j in range(block // STEP):
             tok[i, pl.ds(j * STEP, STEP), :] = x_ref[pl.ds(i * block + j * STEP, STEP), :].astype(BF16)
-    act = [
-        remote(tok.at[1], act_out.at[x], s_misc.at[2], r_misc.at[2], at.xn),
-        pltpu.make_async_copy(tok.at[0], act_out.at[x], s_misc.at[10]),
-    ]
-    for copy in act:
-        copy.start()
-    for copy in (*act, *late, vec_save):
+    act = pltpu.make_async_copy(tok, act_out, s_misc.at[11])
+    act.start()
+    while plan.events:
+        plan.fire()
+    for copy in (act, vec_save, saved[1]):
         copy.wait()
     for name in ("qkv", "att", "x2", "z", "gp"):
         pending[name].wait()
@@ -432,7 +489,7 @@
     return pltpu.SemaphoreType.DMA(shape)
 
 
-def run_fwd(tok, cot, pack, tv, w_qkv, w_out, w_up, w_down, seq):
+def run_fwd(tok, cot, smalls, tv, iv, w_qkv, w_out, w_up, w_down, seq):
     layers, n, d3 = w_qkv.shape
     d = d3 // 3
     hc, f = d // 2, 2 * w_down.shape[1]
@@ -444,31 +501,53 @@
         ((both, hc), BF16), ((both, d), BF16), ((both, f), BF16), ((both, f), BF16),
     ]
     shapes = [((layers, *s), BF16) for s in weights] + [((layers, *s), t) for s, t in acts]
-    shapes += [((2, block, d), BF16), ((2, block, d), BF16), ((layers * SMALL, d), F32)]
+    shapes += [((both, d), BF16), ((2, block, d), BF16), ((layers * SMALL, d), F32)]
     count = layers * len(KINDS)
     return pl.pallas_call(
         functools.partial(fwd_kernel, seq),
         out_shape=[jax.ShapeDtypeStruct(s, t) for s, t in shapes],
-        in_specs=[ANY, ANY, VM, VM, ANY, ANY, ANY, ANY],
+        in_specs=[ANY, ANY] + [VM] * 10 + [ANY] * 4,
         out_specs=[ANY] * len(shapes),
         scratch_shapes=[pltpu.VMEM((layers, *s), BF16) for s in weights]
         + [pltpu.VMEM(s, t) for s, t in acts]
         + [
             pltpu.VMEM((rows, d), BF16), pltpu.VMEM((2, rows, d), BF16),
             pltpu.VMEM((2, block, d), BF16), pltpu.VMEM((layers * SMALL, d), F32), pltpu.VMEM((8, f), F32),
+            pltpu.VMEM((2, block, d), BF16), pltpu.VMEM((both, d), BF16), pltpu.VMEM((layers * SMALL, WIDE), F32),
         ]
         + [dma(count)] * 8
-        + [dma(3), dma(3), dma(8), dma(11), dma(8)],
+        + [dma(3), dma(3), dma(8), dma(12), dma(8)],
         compiler_params=pltpu.CompilerParams(
             collective_id=1, has_side_effects=True, vmem_limit_bytes=VMEM_LIMIT
         ),
         cost_estimate=pl.CostEstimate(flops=17 * 10**9, bytes_accessed=80 * 10**6, transcendentals=0),
         name="forward",
-    )(tok, cot, pack, tv, w_qkv, w_out, w_up, w_down)
+    )(tok, cot, *smalls, tv, iv, w_qkv, w_out, w_up, w_down)
 
 
 NS, NY, NZ, NT = 6, 3, 4, 6
 CHUNK = 256
+
+
+def chunks_of(layers):
+    chunks = []
+    for l in reversed(range(layers)):
+        chunks += [("down", l, i) for i in range(4)] + [("up", l, i) for i in range(4)]
+        chunks += [("out", l, 0)] + [("qkv", l, i) for i in range(3)]
+    return chunks + [("small", 0, 0)]
+
+
+def units_of(chunks):
+    units, first, last = [], [], []
+    for k, (kind, l, i) in enumerate(chunks):
+        pieces = {("qkv", 0, 1): (128, 128), ("qkv", 0, 2): (128, 64, 64), ("small", 0, 0): (64,)}
+        start = 0
+        first.append(len(units))
+        for n in pieces.get((kind, l, i), (CHUNK,)):
+            units.append((k, start, n))
+            start += n
+        last.append(len(units) - 1)
+    return units, first, last
 
 
 class Ring:
@@ -477,33 +556,51 @@
         self.g, self.xr, self.yr, self.zr, self.wr, self.t = bufs
         (self.x_send, self.x_recv, self.y_send, self.y_recv, self.z_send, self.z_recv, self.w_send, self.w_recv,
          self.f_send, self.f_recv, self.cx, self.cy, self.cz, self.cw, self.cb) = sems
-        self.count = len(chunks)
+        self.units, self.first, self.last = units_of(chunks)
+        self.count = len(self.units)
         self.x_free = 0.0
-        self.copies = {}
+        self.copies, self.done, self.when = {}, set(), {}
 
     def size(self, u):
-        return 64 if self.chunks[u][0] == "small" else CHUNK
-
-    def reserve(self, u):
-        if u >= NS:
-            self.plan.need(("s2", u - NS))
-
-    def launch(self, u):
-        n = self.size(u)
-        if u >= NS:
+        return self.units[u][2]
+
+    def reserve(self, k):
+        if k >= NS:
+            self.plan.now = max(self.plan.now, self.when[2, self.last[k - NS]])
+            self.plan.poll()
+
+    def launch(self, k):
+        if k >= NS:
             pl.semaphore_wait(self.cx, 1)
-        copy = remote(
-            self.g.at[u % NS, 0, pl.ds(0, n)], self.xr.at[u % NS, pl.ds(0, n)],
-            self.x_send.at[u % NS], self.x_recv.at[u % NS], self.at.xn,
-        )
-        copy.start()
-        self.copies["x", u] = copy
         plan = self.plan
-        self.x_free = max(plan.now, self.x_free) + 11.3 * n / CHUNK
-        t = self.x_free + 2
-        for k, lag in enumerate((0, 8, 16, 24, 32, 43)):
-            plan.add(t + lag, (f"s{k + 1}", u), functools.partial(getattr(self, f"s{k + 1}"), u))
+        for u in range(self.first[k], self.last[k] + 1):
+            _, start, n = self.units[u]
+            copy = remote(
+                self.g.at[k % NS, 0, pl.ds(start, n)], self.xr.at[k % NS, pl.ds(start, n)],
+                self.x_send.at[u], self.x_recv.at[u], self.at.xn,
+            )
+            copy.start()
+            self.copies["x", u] = copy
+            part = n / CHUNK
+            self.x_free = max(plan.now, self.x_free) + 11.3 * part
+            t = self.x_free + 1.5
+            for i, lag in enumerate((0, 8 * part + 1.5, *[6 * part + 2] * 3, 11 * part + 2)):
+                t += lag
+                self.when[i + 1, u] = t
+                plan.add(t, (i + 1, u), functools.partial(self.run, i + 1, u))
         plan.order()
+
+    def run(self, stage, u):
+        if u < 0 or (stage, u) in self.done:
+            return
+        self.done.add((stage, u))
+        if stage > 1:
+            self.run(stage - 1, u)
+        self.run(stage, u - 1)
+        free = {1: ((2, NY),), 2: ((3, NZ), (6, NT)), 3: ((4, NZ),), 4: ((5, NZ),)}
+        for other, slots in free.get(stage, ()):
+            self.run(other, u - slots)
+        (self.s1, self.s2, self.s3, self.s4, self.s5, self.s6)[stage - 1](u)
 
     def credit(self, sem, u, slots, peer):
         if u + slots < self.count:
@@ -522,15 +619,17 @@
         loop(count // 32, body)
 
     def s1(self, u):
-        n, at = self.size(u), self.at
-        slot = u % NS
+        at = self.at
+        k, start, n = self.units[u]
+        slot = k % NS
         self.copies["x", u].wait()
-        self.add(self.g.at[slot, 1], self.xr.at[slot], n)
-        self.credit(self.cx, u, NS, at.xn)
+        self.add(self.g.at[slot, 1, pl.ds(start, n)], self.xr.at[slot, pl.ds(start, n)], n)
+        if u == self.last[k] and k + NS < len(self.chunks):
+            pl.semaphore_signal(self.cx, inc=1, device_id=at.xn, device_id_type=MESH)
         self.claim(self.cy, u, NY)
         copy = remote(
-            self.g.at[slot, 1, span((1 - at.y) * (n // 2), n // 2)], self.yr.at[u % NY, pl.ds(0, n // 2)],
-            self.y_send.at[slot], self.y_recv.at[u % NY], at.yn,
+            self.g.at[slot, 1, span(start + (1 - at.y) * (n // 2), n // 2)], self.yr.at[u % NY, pl.ds(0, n // 2)],
+            self.y_send.at[u], self.y_recv.at[u % NY], at.yn,
         )
         copy.start()
         self.copies["y", u] = copy
@@ -539,10 +638,11 @@
         return ref.at[u % slots, pl.ds(0, self.size(u) // 2)]
 
     def s2(self, u):
-        n, at = self.size(u), self.at
+        at = self.at
+        k, start, n = self.units[u]
         t = self.part(self.t, u, NT)
         self.copies["y", u].wait()
-        self.add(t, self.part(self.yr, u, NY), n // 2, self.g.at[u % NS, 1], at.y * (n // 2))
+        self.add(t, self.part(self.yr, u, NY), n // 2, self.g.at[k % NS, 1], start + at.y * (n // 2))
         self.credit(self.cy, u, NY, at.yn)
 
         @pl.when(at.outer)
@@ -596,7 +696,8 @@
             loop(n // 64, body)
             self.credit(self.cb, u, NZ, at.zn)
 
-        kind, l, i = self.chunks[u]
+        k, start, n = self.units[u]
+        kind, l, i = self.chunks[k]
         out = self.outs[kind]
         sent = self.f_send.at[u % NT]
         if kind == "small":
@@ -614,24 +715,22 @@
                 remote(src, dst, sent, self.f_recv.at[kind_index], at.yd).start()
 
         if kind in ("down", "out"):
-            deliver(t, out.at[l, span(i * n + at.y * half, half)], True, KINDS.index(kind))
+            deliver(t, out.at[l, span(i * CHUNK + start + at.y * half, half)], True, KINDS.index(kind))
         elif kind == "up":
             side, run = divmod(i, 2)
-            deliver(t, out.at[l, span(at.y * half, half), span((2 * run + at.c) * width, width)], side == 0, 2)
+            deliver(t, out.at[l, span(start + at.y * half, half), span((2 * run + at.c) * width, width)], side == 0, 2)
         else:
             for side in range(2):
                 for run in range(2):
                     src = t.at[:, pl.ds((2 * side + run) * WIDE, WIDE)]
-                    dst = out.at[l, span(at.y * half, half), span(i * width + (2 * run + at.c) * WIDE, WIDE)]
+                    dst = out.at[l, span(start + at.y * half, half), span(i * width + (2 * run + at.c) * WIDE, WIDE)]
                     deliver(src, dst, side == 0, 0)
 
     def s6(self, u):
         at = self.at
         t = self.part(self.t, u, NT)
-        if self.chunks[u][0] == "small":
-            settle(t, self.f_send.at[u % NT])
-        else:
-            settle(self.g.at[0, 0], self.f_send.at[u % NT])
+        k, _, n = self.units[u]
+        settle(t if self.chunks[k][0] == "small" else self.g.at[0, 0, pl.ds(0, n)], self.f_send.at[u % NT])
 
         @pl.when(at.inner)
         def _():
@@ -647,8 +746,8 @@
 
 
 def bwd_kernel(
-    seq, cot_ref, vec_ref, tv_ref, iv_ref, vqkv, vout, vup, vdown, xs, x2s, h1s, qkvs, as_, h2s, zs, gps,
-    oqkv, oout, oup, odown, osmall, otok,
+    seq, dm_ref, act_ref, vec_ref, tv_ref, vqkv, vout, vup, vdown, xs, x2s, h1s, qkvs, as_, h2s, zs, gps,
+    oqkv, oout, oup, odown, osmall, otok, oact,
     wqkv, wout, wup, wdown, x_ref, x2_ref, h1, qkv, att, h2, z, gp,
     tok, g_ref, dm, da, dj, dx2, dh, put, got, small, small_put, small_got, ring_g, ring_x, ring_y, ring_z, ring_w, ring_t,
     s_load, s_core, r_core, s_misc, r_misc, *ring_sems,
@@ -661,11 +760,7 @@
     own, other = pl.ds(0, rows), pl.ds(rows, rows)
     x, c = at.x, at.c
     plan = Plan()
-    chunks = []
-    for l in reversed(range(layers)):
-        chunks += [("down", l, i) for i in range(4)] + [("up", l, i) for i in range(4)]
-        chunks += [("out", l, 0)] + [("qkv", l, i) for i in range(3)]
-    chunks.append(("small", 0, 0))
+    chunks = chunks_of(layers)
     ring = Ring(
         at, plan, chunks, dict(qkv=oqkv, out=oout, up=oup, down=odown, small=osmall),
         (ring_g, ring_x, ring_y, ring_z, ring_w, ring_t), ring_sems,
@@ -686,8 +781,8 @@
         loads[name, l] = pltpu.make_async_copy(src.at[l], dst, s_load.at[slots[name]])
         loads[name, l].start()
 
-    cot_load = pltpu.make_async_copy(cot_ref, tok, s_misc.at[0])
-    cot_load.start()
+    dm_load = pltpu.make_async_copy(dm_ref, dm.at[0], s_misc.at[0])
+    dm_load.start()
     for name in stores:
         load(name, layers - 1)
     greet((at.sib, at.xn, at.yn, at.yd, at.zn, at.mid))
@@ -696,15 +791,11 @@
         return hh * x + (1 - hh) * (1 - x)
 
     mask = chip_flags(at, tv_ref, rows, seq)
-    valid = jnp.where(x == 0, iv_ref[0:1, 0:1], iv_ref[1:2, 0:1]).astype(F32)
-    weight = mask[:rows].astype(F32) * valid
     small[...] = jnp.zeros_like(small)
-    cot_load.wait()
-    for i in range(2):
-        for j in range(block // STEP):
-            r = i * block + j * STEP
-            g_ref[pl.ds(r, STEP), :] = tok[i, pl.ds(j * STEP, STEP), :].astype(F32) * weight[r:r + STEP, :]
-
+    act = [
+        remote(act_ref.at[1], oact.at[x], s_misc.at[4], r_misc.at[4], at.xn),
+        pltpu.make_async_copy(act_ref.at[0], oact.at[x], s_misc.at[5]),
+    ]
     for l in reversed(range(layers)):
         def row(name, l=l):
             return vec_ref[l * SMALL + name:l * SMALL + name + 1, :]
@@ -712,15 +803,22 @@
         def set_small(name, value, l=l):
             small[l * SMALL + name:l * SMALL + name + 1, :] = value
 
-        def send_round(src_ref, name, slot):
+        def round_rows(src_ref, name, slot):
             total = jnp.zeros((8, d), F32)
             for i in range(rows // STEP):
                 r = pl.ds(i * STEP, STEP)
-                low = src_ref[r, :].astype(BF16)
-                dm[slot, r, :] = low
-                low = low.astype(F32)
+                if src_ref is None:
+                    low = dm[slot, r, :].astype(F32)
+                    g_ref[r, :] = low
+                else:
+                    low = src_ref[r, :].astype(BF16)
+                    dm[slot, r, :] = low
+                    low = low.astype(F32)
                 total = total + low[0:8, :] + low[8:16, :]
             set_small(name, jnp.sum(total, axis=0, keepdims=True))
+
+        def send_round(src_ref, name, slot):
+            round_rows(src_ref, name, slot)
             copy = remote(dm.at[slot, own], dm.at[slot, other], s_core.at[slot], r_core.at[slot], at.sib)
             copy.start()
             return copy
@@ -736,6 +834,7 @@
                 put[:, cols(j)] = nt(left[other, :], piece(j)).astype(BF16)
 
             loop(d // WIDE, far)
+            plan.spend(1.5)
             copy = remote(put, got, s_core.at[2], r_core.at[2], at.sib)
             copy.start()
 
@@ -743,7 +842,9 @@
                 dh[:, cols(j)] = nt(left[own, :], piece(j))
 
             loop(d // WIDE, near)
+            plan.spend(1.5)
             copy.wait()
+            plan.spend(0.5)
 
         def norm_back(value_ref, base_ref, out_ref, gain, shift):
             total_g = jnp.zeros((8, d), F32)
@@ -769,15 +870,23 @@
             ring.launch(u)
             plan.spend(us)
 
-        copy = send_round(g_ref, BDOWN, 0)
-        loads["z", l].wait()
-        plan.spend(2)
-        copy.wait()
+        if l == layers - 1:
+            dm_load.wait()
+            loads["z", l].wait()
+        else:
+            copy = send_round(g_ref, BDOWN, 0)
+            loads["z", l].wait()
+            plan.spend(2)
+            copy.wait()
         for i in range(4):
             def make(dst, h, i=i):
                 dst[...] = tn(z[:, span(h * (f // 2) + i * CHUNK, CHUNK)], dm[0]).astype(BF16)
 
             produce(("down", l, i), make, 1.3)
+        if l == layers - 1:
+            round_rows(None, BDOWN, 0)
+            for copy in act:
+                copy.start()
         load("z", l - 1)
         loads["wdown", l].wait()
         loads["gp", l].wait()
@@ -789,8 +898,9 @@
                 low = (nt(dm[0, r, :], w) * gp[r, cols(j)].astype(F32)).astype(BF16)
                 gp[r, cols(j)] = low
 
-        loop(f // WIDE, dz_body)
-        plan.spend(4)
+        for part in range(2):
+            loop(f // WIDE // 2, lambda j: dz_body(j + part * (f // WIDE // 2)))
+            plan.spend(2)
         load("wdown", l - 1)
         for j in range(f // WIDE):
             half, sub = divmod(j, f // WIDE // 2)
@@ -811,7 +921,6 @@
                 exchange(gp, wup)
                 load("wup", l - 1)
                 loads["x2", l].wait()
-                plan.spend(4)
                 norm_back(x2_ref, g_ref, dx2, G2, B2)
                 load("x2", l - 1)
                 plan.spend(3)
@@ -852,6 +961,7 @@
                 parts.append(nn(kt[a * HEAD:(a + 1) * HEAD, :], dst))
                 dk = dka if dk is None else dk + dka
                 dv = dva if dv is None else dv + dva
+                plan.spend(2.7)
             dq = (jnp.concatenate(parts, axis=0).T * HEAD ** -0.5).astype(BF16)
             dv = dv.astype(BF16)
             dj[:, cq] = dq
@@ -864,7 +974,6 @@
                     small[r:r + 1, k * hc + p * 128:k * hc + (p + 1) * 128] = jnp.where(
                         c == core, total, jnp.zeros_like(total)
                     )
-            plan.spend(5.5)
         load("qkv", l - 1)
         loads["wqkv", l].wait()
         loads["h1", l].wait()
@@ -879,7 +988,6 @@
                 exchange(dj, wqkv)
                 load("wqkv", l - 1)
                 loads["x", l].wait()
-                plan.spend(4)
                 norm_back(x_ref, dx2, g_ref, G1, B1)
                 load("x", l - 1)
                 plan.spend(3)
@@ -908,22 +1016,24 @@
     for copy in back:
         copy.start()
     ring.finish()
-    for copy in back:
+    for copy in (*back, *act):
         copy.wait()
 
 
-def run_bwd(cot, vec, tv, iv, weights, acts, seq):
+def run_bwd(dm, act, vec, tv, weights, acts, seq):
     layers, _, n, hc3 = weights[0].shape
     d = acts[0].shape[2]
     rows = acts[0].shape[1]
     block, both = rows // 2, 2 * rows
     hc, f = hc3 // 3, weights[2].shape[3]
-    outs = [(layers, n, 3 * d), (layers, n, d), (layers, n, 2 * f), (layers, f // 2, d), (layers * SMALL, d), (2, block, d)]
-    args = (cot, vec, tv, iv, *weights, *acts)
+    units = len(units_of(chunks_of(layers))[0])
+    outs = [(layers, n, 3 * d), (layers, n, d), (layers, n, 2 * f), (layers, f // 2, d), (layers * SMALL, d)]
+    outs += [(2, block, d)] * 2
+    args = (dm, act, vec, tv, *weights, *acts)
     return pl.pallas_call(
         functools.partial(bwd_kernel, seq),
         out_shape=[jax.ShapeDtypeStruct(s, BF16) for s in outs],
-        in_specs=[ANY, VM, VM, VM] + [ANY] * 12,
+        in_specs=[ANY, ANY, VM, VM] + [ANY] * 12,
         out_specs=[ANY] * len(outs),
         scratch_shapes=[pltpu.VMEM(w.shape[1:], w.dtype) for w in (*weights, *acts)]
         + [
@@ -935,8 +1045,8 @@
             pltpu.VMEM((NS, 2, CHUNK, d), BF16), pltpu.VMEM((NS, CHUNK, d), BF16),
             pltpu.VMEM((NY, CHUNK // 2, d), BF16), pltpu.VMEM((NZ, CHUNK // 2, d), BF16),
             pltpu.VMEM((NZ, CHUNK // 2, d), BF16), pltpu.VMEM((NT, CHUNK // 2, d), BF16),
-            dma(12), dma(3), dma(3), dma(4), dma(4),
-            dma(NS), dma(NS), dma(NS), dma(NY), dma(NT), dma(NZ), dma(NT), dma(NZ), dma(NT), dma(4),
+            dma(12), dma(3), dma(3), dma(6), dma(6),
+            dma(units), dma(units), dma(units), dma(NY), dma(NT), dma(NZ), dma(NT), dma(NZ), dma(NT), dma(4),
         ]
         + [pltpu.SemaphoreType.REGULAR] * 5,
         compiler_params=pltpu.CompilerParams(
@@ -947,42 +1057,70 @@
     )(*args)
 
 
+def finish_kernel(gqkv, gout, gup, gdown, small, oqkv, oout, oup, odown, *vectors):
+    for src, dst in ((gqkv, oqkv), (gout, oout), (gup, oup), (gdown, odown)):
+        dst[...] = src[...].astype(F32)
+    mine = span(lax.axis_index("grp") * WIDE, WIDE)
+    layers = vectors[0].shape[0]
+    rows = [small[l * SMALL:(l + 1) * SMALL, mine].astype(F32) for l in range(layers)]
+    at = 0
+    for out in vectors:
+        for j in range(out.shape[1] // WIDE):
+            for l in range(layers):
+                out[l:l + 1, j * WIDE:(j + 1) * WIDE] = rows[l][at:at + 1, :]
+            at += 1
+
+
+def run_finish(gqkv, gout, gup, gdown, small, widths):
+    bigs = (gqkv, gout, gup, gdown)
+    layers = gqkv.shape[0]
+    steps = 4
+
+    def big(g):
+        return pl.BlockSpec((1, g.shape[1] // steps, g.shape[2]), lambda l, s: (l, s, 0))
+
+    def flat(shape):
+        return pl.BlockSpec(shape, lambda l, s: (0, 0))
+
+    vectors = [(layers, w) for w in widths]
+    return pl.pallas_call(
+        finish_kernel,
+        grid=(layers, steps),
+        out_shape=[jax.ShapeDtypeStruct(g.shape, F32) for g in bigs]
+        + [jax.ShapeDtypeStruct(v, F32) for v in vectors],
+        in_specs=[big(g) for g in bigs] + [flat(small.shape)],
+        out_specs=[big(g) for g in bigs] + [flat(v) for v in vectors],
+        compiler_params=pltpu.CompilerParams(vmem_limit_bytes=VMEM_LIMIT),
+        name="finish",
+    )(*bigs, small)
+
+
 def local(
     tokens, cotangent, image_valid, token_valid,
     norm1_gain, norm1_bias, w_qkv, b_qv, w_out, b_out, norm2_gain, norm2_bias, w_up, b_up, w_down, b_down,
 ):
-    grp = lax.axis_index("grp")
-    layers, n, _ = w_qkv.shape
-    seq, d = tokens.shape[1:]
+    seq = tokens.shape[1]
     block = -(-seq // 32) * 32
 
     def pad(value):
         return jnp.pad(value, ((0, 0), (0, block - seq), (0, 0)))
 
     smalls = (norm1_gain, norm1_bias, b_out, norm2_gain, norm2_bias, b_down, b_qv, b_up)
-    pack = jnp.concatenate([w.reshape(layers, -1, d // 4) for w in smalls], axis=1).astype(F32)
-    pack = jnp.pad(pack, ((0, 0), (0, SMALL - pack.shape[1]), (0, 0))).reshape(layers * SMALL, d // 4)
-    res = run_fwd(pad(tokens), pad(cotangent), pack, token_valid, w_qkv, w_out, w_up, w_down, seq)
-    weights, acts, (cot, act, vec) = res[:4], res[4:12], res[12:]
-    gqkv, gout, gup, gdown, gsmall, gtok = run_bwd(
-        cot, vec, token_valid, image_valid[:, None], weights, acts, seq
+    res = run_fwd(
+        pad(tokens), pad(cotangent), smalls, token_valid, image_valid[None, :], w_qkv, w_out, w_up, w_down, seq
     )
+    weights, acts, (dm, act, vec) = res[:4], res[4:12], res[12:]
+    gqkv, gout, gup, gdown, gsmall, gtok, act = run_bwd(dm, act, vec, token_valid, weights, acts, seq)
     blocks = lax.axis_size("rep") // 8
     if blocks > 1:
         groups = [[i + 8 * b for b in range(blocks)] for i in range(8)]
         gqkv, gout, gup, gdown, gsmall = (
             lax.psum(g, "rep", axis_index_groups=groups) for g in (gqkv, gout, gup, gdown, gsmall)
         )
-    gsmall = lax.dynamic_slice_in_dim(gsmall, grp * (d // 4), d // 4, 1).astype(F32).reshape(layers, SMALL, d // 4)
-    outs, at = [], 0
-    for w in smalls:
-        take = w.shape[1] // (d // 4)
-        outs.append(gsmall[:, at:at + take].reshape(layers, -1))
-        at += take
-    gg1, gb1, gbout, gg2, gb2, gbdown, gbqv, gbup = outs
+    gqkv, gout, gup, gdown, *vectors = run_finish(gqkv, gout, gup, gdown, gsmall, [w.shape[1] for w in smalls])
+    gg1, gb1, gbout, gg2, gb2, gbdown, gbqv, gbup = vectors
     return (
-        act[:, :seq], gtok[:, :seq], gg1, gb1, gqkv.astype(F32), gbqv, gout.astype(F32), gbout, gg2, gb2,
-        gup.astype(F32), gbup, gdown.astype(F32), gbdown,
+        act[:, :seq], gtok[:, :seq], gg1, gb1, gqkv, gbqv, gout, gbout, gg2, gb2, gup, gbup, gdown, gbdown,
     )
 
 

time: 561 us -> 507 us (0.904)
  Pallas kernels: 520 us -> 488 us
  other arithmetic: 16.7 us -> 0 us
    pallas_call x1, Pallas kernels: 160 us -> 130 us  [run_fwd(): pl.pallas_call(functools.partial(fwd_kernel, seq), out_shape=[jax.ShapeDt...]
    convert_element_type x4 -> x0, other arithmetic: 16 us -> none  [the longest x1 5.54 us: local(): gqkv.astype(F32)]
    pallas_call x1, Pallas kernels: 359 us -> 344 us  [run_bwd(): pl.pallas_call(functools.partial(bwd_kernel, seq), out_shape=[jax.ShapeDt...]
    pallas_call x0 -> x1, Pallas kernels: none -> 14 us  [run_finish(): pl.pallas_call(finish_kernel, grid=(layers, steps), out_shape=[jax.ShapeD...]
where the time goes in v4:
time: 507 us; the launch traced here: 498 us
  Pallas kernels  488 us (96%)
  local copies, waits for them, and re-layouts  9.31 us (2%)
    pallas_call x1, Pallas kernels, run_bwd(): pl.pallas_call(functools.partial(bwd_kernel, seq), out_shape=[jax.ShapeDt...  344 us
    pallas_call x1, Pallas kernels, run_fwd(): pl.pallas_call(functools.partial(fwd_kernel, seq), out_shape=[jax.ShapeDt...  130 us
    pallas_call x1, Pallas kernels, run_finish(): pl.pallas_call(finish_kernel, grid=(layers, steps), out_shape=[jax.ShapeD...  14 us

profile of v4, /device:TPU:0, one launch (start us, length us, event | category | flops | bytes accessed | tf_op | source)
XLA Modules:
  0.0 498.5 jit_solution(3378177832064039957)
XLA Ops:
  0.6 1.2 copy.30
  1.9 0.9 pad.7.tok_ref
  2.8 1.2 copy.31
  4.0 0.9 pad.8.cot_ref
  4.9 130.5 %forward.1 = (bf16[2,4,256,1536]{3,2,1,0:T(8,128)(2,1)}, bf16[2,2,256,1024]{3,2,1,0:T(8,128)(2,1)}, bf16[2,4,256,2048]{3,2,1,0:T(8,128)(2,1)}, bf16[2,2,1024,102...) custom-call(bf16[2,160,1024]{2,1,0:T(8,128)(2,1)} %pad.7.tok_ref, ...), custom_call_target="tpu_custom_call" | custom-call | flops 16999999488 | bytes 80000000 | tf_op jit(solution)/shard_map/forward/pallas_call | solution.py:506
  135.3 343.6 %backward.1 = (bf16[2,256,3072]{2,1,0:T(8,128)(2,1)}, bf16[2,256,1024]{2,1,0:T(8,128)(2,1)}, bf16[2,256,4096]{2,1,0:T(8,128)(2,1)}, bf16[2,1024,1024]{2,1,0:T(8,...) custom-call(bf16[640,1024]{1,0:T(8,128)(2,1)} %get-tuple-element.48.dm_ref, ...), custom_call_target="tpu_custom_call" | custom-call | flops 33999998976 | bytes 120000000 | tf_op jit(solution)/shard_map/backward/pallas_call | solution.py:1033
  478.9 1.1 slice.6
  480.0 1.4 copy.32
  481.5 1.1 slice.7
  482.6 1.4 copy.33
  484.0 14.0 %finish.1 = (f32[2,256,3072]{2,1,0:T(8,128)}, f32[2,256,1024]{2,1,0:T(8,128)}, f32[2,256,4096]{2,1,0:T(8,128)}, f32[2,1024,1024]{2,1,0:T(8,128)}, f32[2,256]{1,0...) custom-call(bf16[2,256,3072]{2,1,0:T(8,128)(2,1)} %get-tuple-element, ...), custom_call_target="tpu_custom_call" | custom-call | tf_op jit(solution)/shard_map/finish/pallas_call | solution.py:1086

commit v5 on v4

--- a/solution.py
+++ b/solution.py
@@ -62,8 +62,9 @@
         self.yn = (yrep, grp)
         self.yd = (yrep, grp + core)
         self.zn = (rep + 2 - 4 * self.zlow, grp)
-        self.inner = jnp.logical_or(self.z == 1, self.z == 2)
-        self.outer = jnp.logical_not(self.inner)
+        self.inn = ((self.z + 1) // 2) % 2
+        self.inner = self.inn == 1
+        self.outer = self.inn == 0
         self.mid = (rep + 6 - 4 * self.z, grp)
 
 
@@ -525,8 +526,10 @@
     )(tok, cot, *smalls, tv, iv, w_qkv, w_out, w_up, w_down)
 
 
-NS, NY, NZ, NT = 6, 3, 4, 6
+LINK, HOP, STAGE = 11.5, 2.5, 0.6
+NS, NY, NZ, NT = 6, 3, 3, 6
 CHUNK = 256
+CROSS = (("down", 1), ("down", 3), ("up", 1))
 
 
 def chunks_of(layers):
@@ -537,70 +540,166 @@
     return chunks + [("small", 0, 0)]
 
 
+def crossed(chunk):
+    return (chunk[0], chunk[2]) in CROSS
+
+
 def units_of(chunks):
-    units, first, last = [], [], []
+    units, first, last = [], {}, {}
     for k, (kind, l, i) in enumerate(chunks):
+        if crossed(chunks[k]):
+            continue
         pieces = {("qkv", 0, 1): (128, 128), ("qkv", 0, 2): (128, 64, 64), ("small", 0, 0): (64,)}
         start = 0
-        first.append(len(units))
+        first[k] = len(units)
         for n in pieces.get((kind, l, i), (CHUNK,)):
             units.append((k, start, n))
             start += n
-        last.append(len(units) - 1)
+        last[k] = len(units) - 1
     return units, first, last
 
 
 class Ring:
     def __init__(self, at, plan, chunks, outs, bufs, sems):
         self.at, self.plan, self.chunks, self.outs = at, plan, chunks, outs
-        self.g, self.xr, self.yr, self.zr, self.wr, self.t = bufs
+        self.g, self.xr, self.yr, self.zr, self.wr, self.t, self.zd, self.xd, self.yd, self.cd, self.td = bufs
         (self.x_send, self.x_recv, self.y_send, self.y_recv, self.z_send, self.z_recv, self.w_send, self.w_recv,
-         self.f_send, self.f_recv, self.cx, self.cy, self.cz, self.cw, self.cb) = sems
+         self.f_send, self.f_recv) = sems[:10]
+        self.d_send, self.d_recv, self.d_out, self.cx, self.cy, self.cz, self.cw, self.cb = sems[10:]
         self.units, self.first, self.last = units_of(chunks)
+        self.turn = {k: a for a, k in enumerate(self.first)}
+        self.cross = [k for k, chunk in enumerate(chunks) if crossed(chunk)]
         self.count = len(self.units)
-        self.x_free = 0.0
-        self.copies, self.done, self.when = {}, set(), {}
+        self.link = dict(x=0.0, y=0.0, out=0.0, mid=0.0, back=0.0)
+        self.copies, self.done, self.ready = {}, set(), {}
 
     def size(self, u):
         return self.units[u][2]
 
+    def send(self, links, rows):
+        t = max(self.plan.now, *(self.link[name] for name in links)) + LINK * rows / CHUNK
+        for name in links:
+            self.link[name] = t
+        return t + HOP
+
+    def pick(self, limit):
+        best = None
+        for (stage, u), t in self.ready.items():
+            if t > limit or (best and best[0] <= t):
+                continue
+            ahead = [(stage, u - 1)]
+            ahead += {1: [(2, u - NY)], 2: [(3, u - NZ), (6, u - NT)], 3: [(4, u - NZ)], 4: [(5, u - NZ)]}.get(stage, [])
+            if all(v < 0 or (other, v) in self.done for other, v in ahead):
+                best = (t, stage, u)
+        return best
+
+    def step(self, best):
+        t, stage, u = best
+        del self.ready[stage, u]
+        self.plan.now = max(self.plan.now, t) + STAGE
+        if stage > 10:
+            (self.d2, self.d3, self.d4, self.d5, self.d6, self.d7)[stage - 12](u)
+            links, rows = {
+                12: (("x",), 128), 13: (("y",), 64), 14: (("mid", "out", "back"), 96), 15: (("y",), 64),
+                16: (("out", "back"), 128),
+            }.get(stage, (None, 0))
+        else:
+            (self.s1, self.s2, self.s3, self.s4, self.s5, self.s6)[stage - 1](u)
+            links = {1: ("y",), 2: ("out",), 3: ("mid",), 4: ("back",), 5: ("y",)}.get(stage)
+            rows = self.size(u) // 2
+        self.done.add((stage, u))
+        if links:
+            self.ready[stage + 1, u] = self.send(links, rows)
+
+    def poll(self):
+        while best := self.pick(self.plan.now):
+            self.step(best)
+
+    def catch_up(self, stage, u):
+        while (stage, u) not in self.done:
+            self.step(self.pick(float("inf")))
+
     def reserve(self, k):
         if k >= NS:
-            self.plan.now = max(self.plan.now, self.when[2, self.last[k - NS]])
-            self.plan.poll()
+            old = k - NS
+            if old in self.turn:
+                self.catch_up(2, self.last[old])
+            else:
+                self.catch_up(14, self.cross.index(old))
+        if self.turn.get(k, 0) >= NS:
+            self.catch_up(1, self.last[list(self.turn)[self.turn[k] - NS]])
 
     def launch(self, k):
-        if k >= NS:
+        if k not in self.turn:
+            d = self.cross.index(k)
+            self.move(d, 0, self.g.at[k % NS, :, self.rows_of(1 - self.at.inn)], self.zd.at[d], self.at.zn)
+            self.ready[12, d] = self.send(("out", "back"), CHUNK)
+            return
+        a = self.turn[k]
+        if a >= NS:
             pl.semaphore_wait(self.cx, 1)
-        plan = self.plan
         for u in range(self.first[k], self.last[k] + 1):
             _, start, n = self.units[u]
             copy = remote(
-                self.g.at[k % NS, 0, pl.ds(start, n)], self.xr.at[k % NS, pl.ds(start, n)],
+                self.g.at[k % NS, 0, pl.ds(start, n)], self.xr.at[a % NS, pl.ds(start, n)],
                 self.x_send.at[u], self.x_recv.at[u], self.at.xn,
             )
             copy.start()
             self.copies["x", u] = copy
-            part = n / CHUNK
-            self.x_free = max(plan.now, self.x_free) + 11.3 * part
-            t = self.x_free + 1.5
-            for i, lag in enumerate((0, 8 * part + 1.5, *[6 * part + 2] * 3, 11 * part + 2)):
-                t += lag
-                self.when[i + 1, u] = t
-                plan.add(t, (i + 1, u), functools.partial(self.run, i + 1, u))
-        plan.order()
-
-    def run(self, stage, u):
-        if u < 0 or (stage, u) in self.done:
-            return
-        self.done.add((stage, u))
-        if stage > 1:
-            self.run(stage - 1, u)
-        self.run(stage, u - 1)
-        free = {1: ((2, NY),), 2: ((3, NZ), (6, NT)), 3: ((4, NZ),), 4: ((5, NZ),)}
-        for other, slots in free.get(stage, ()):
-            self.run(other, u - slots)
-        (self.s1, self.s2, self.s3, self.s4, self.s5, self.s6)[stage - 1](u)
+            self.ready[1, u] = self.send(("x",), n)
+
+    def rows_of(self, part):
+        return span(part * (CHUNK // 2), CHUNK // 2)
+
+    def move(self, d, hop, src, dst, peer):
+        copy = remote(src, dst, self.d_send.at[hop, d], self.d_recv.at[hop, d], peer)
+        copy.start()
+        self.copies[hop, d] = copy
+
+    def d2(self, d):
+        slot, mine = self.cross[d] % NS, self.rows_of(self.at.inn)
+        self.copies[0, d].wait()
+        for hh in range(2):
+            self.add(self.g.at[slot, hh, mine], self.zd.at[d, hh], CHUNK // 2)
+        self.move(d, 1, self.g.at[slot, 0, mine], self.xd.at[d], self.at.xn)
+
+    def d3(self, d):
+        slot, mine, quarter = self.cross[d] % NS, self.rows_of(self.at.inn), CHUNK // 4
+        self.copies[1, d].wait()
+        self.add(self.g.at[slot, 1, mine], self.xd.at[d], CHUNK // 2)
+        give = span((2 * self.at.inn + 1 - self.at.y) * quarter, quarter)
+        self.move(d, 2, self.g.at[slot, 1, give], self.yd.at[d], self.at.yn)
+
+    def d4(self, d):
+        slot, quarter = self.cross[d] % NS, CHUNK // 4
+        t = self.td.at[d, span(self.at.y * quarter, quarter)]
+        self.copies[2, d].wait()
+        self.add(t, self.yd.at[d], quarter, self.g.at[slot, 1], (2 * self.at.inn + self.at.y) * quarter)
+        self.move(d, 3, t, self.cd.at[d], self.at.mid)
+
+    def d5(self, d):
+        quarter = CHUNK // 4
+        t = self.td.at[d, span(self.at.y * quarter, quarter)]
+        self.copies[3, d].wait()
+        self.add(t, self.cd.at[d], quarter)
+        self.move(d, 4, t, t, self.at.yn)
+
+    def d6(self, d):
+        at = self.at
+        kind, l, i = self.chunks[self.cross[d]]
+        out = self.outs[kind]
+        self.copies[4, d].wait()
+        if kind == "down":
+            dst = out.at[l, span((2 * i + at.inn) * (CHUNK // 2), CHUNK // 2)]
+        else:
+            width = self.td.shape[2]
+            dst = out.at[l, self.rows_of(at.inn), span((2 * (i % 2) + at.c) * width, width)]
+        sent = self.d_out.at[d]
+        pltpu.make_async_copy(self.td.at[d], dst, sent).start()
+        remote(self.td.at[d], dst, sent, self.f_recv.at[KINDS.index(kind)], at.zn).start()
+
+    def d7(self, d):
+        settle(self.zd.at[d], self.d_out.at[d])
 
     def credit(self, sem, u, slots, peer):
         if u + slots < self.count:
@@ -621,10 +720,10 @@
     def s1(self, u):
         at = self.at
         k, start, n = self.units[u]
-        slot = k % NS
+        slot, a = k % NS, self.turn[k]
         self.copies["x", u].wait()
-        self.add(self.g.at[slot, 1, pl.ds(start, n)], self.xr.at[slot, pl.ds(start, n)], n)
-        if u == self.last[k] and k + NS < len(self.chunks):
+        self.add(self.g.at[slot, 1, pl.ds(start, n)], self.xr.at[a % NS, pl.ds(start, n)], n)
+        if u == self.last[k] and a + NS < len(self.turn):
             pl.semaphore_signal(self.cx, inc=1, device_id=at.xn, device_id_type=MESH)
         self.claim(self.cy, u, NY)
         copy = remote(
@@ -737,8 +836,8 @@
             settle(t, self.w_send.at[u % NT])
 
     def finish(self):
-        while self.plan.events:
-            self.plan.fire()
+        while best := self.pick(float("inf")):
+            self.step(best)
         for i, kind in enumerate(KINDS):
             out = self.outs[kind]
             rows = out.shape[1]
@@ -749,8 +848,7 @@
     seq, dm_ref, act_ref, vec_ref, tv_ref, vqkv, vout, vup, vdown, xs, x2s, h1s, qkvs, as_, h2s, zs, gps,
     oqkv, oout, oup, odown, osmall, otok, oact,
     wqkv, wout, wup, wdown, x_ref, x2_ref, h1, qkv, att, h2, z, gp,
-    tok, g_ref, dm, da, dj, dx2, dh, put, got, small, small_put, small_got, ring_g, ring_x, ring_y, ring_z, ring_w, ring_t,
-    s_load, s_core, r_core, s_misc, r_misc, *ring_sems,
+    g_ref, dm, da, dj, dx2, dh, put, got, small, small_put, small_got, s_load, s_core, r_core, s_misc, r_misc, *rest,
 ):
     at = Place()
     layers = vqkv.shape[0]
@@ -761,10 +859,13 @@
     x, c = at.x, at.c
     plan = Plan()
     chunks = chunks_of(layers)
+    rings, ring_sems = rest[:11], rest[11:]
+    ring_g = rings[0]
     ring = Ring(
         at, plan, chunks, dict(qkv=oqkv, out=oout, up=oup, down=odown, small=osmall),
-        (ring_g, ring_x, ring_y, ring_z, ring_w, ring_t), ring_sems,
+        rings, ring_sems,
     )
+    plan.poll = ring.poll
     number = {chunk: u for u, chunk in enumerate(chunks)}
 
     stores = dict(
@@ -994,12 +1095,11 @@
             produce(("qkv", l, i), make, 1.3)
         load("h1", l - 1)
 
-    for i in range(2):
-        for j in range(block // STEP):
-            tok[i, pl.ds(j * STEP, STEP), :] = g_ref[pl.ds(i * block + j * STEP, STEP), :].astype(BF16)
+    for j in range(rows // STEP):
+        put[pl.ds(j * STEP, STEP), :] = g_ref[pl.ds(j * STEP, STEP), :].astype(BF16)
     back = [
-        remote(tok.at[1], otok.at[x], s_misc.at[1], r_misc.at[1], at.xn),
-        pltpu.make_async_copy(tok.at[0], otok.at[x], s_misc.at[2]),
+        remote(put.at[pl.ds(block, block)], otok.at[x], s_misc.at[1], r_misc.at[1], at.xn),
+        pltpu.make_async_copy(put.at[pl.ds(0, block)], otok.at[x], s_misc.at[2]),
     ]
     small_put[...] = small[...].astype(BF16)
     copy = remote(small_put, small_got, s_misc.at[3], r_misc.at[3], at.sib)
@@ -1026,7 +1126,9 @@
     rows = acts[0].shape[1]
     block, both = rows // 2, 2 * rows
     hc, f = hc3 // 3, weights[2].shape[3]
-    units = len(units_of(chunks_of(layers))[0])
+    chunks = chunks_of(layers)
+    units = len(units_of(chunks)[0])
+    crosses = sum(crossed(chunk) for chunk in chunks)
     outs = [(layers, n, 3 * d), (layers, n, d), (layers, n, 2 * f), (layers, f // 2, d), (layers * SMALL, d)]
     outs += [(2, block, d)] * 2
     args = (dm, act, vec, tv, *weights, *acts)
@@ -1037,16 +1139,20 @@
         out_specs=[ANY] * len(outs),
         scratch_shapes=[pltpu.VMEM(w.shape[1:], w.dtype) for w in (*weights, *acts)]
         + [
-            pltpu.VMEM((2, block, d), BF16), pltpu.VMEM((rows, d), F32), pltpu.VMEM((2, both, d), BF16),
+            pltpu.VMEM((rows, d), F32), pltpu.VMEM((2, both, d), BF16),
             pltpu.VMEM((both, hc), BF16), pltpu.VMEM((both, 3 * hc), BF16), pltpu.VMEM((rows, d), F32),
             pltpu.VMEM((rows, d), F32), pltpu.VMEM((rows, d), BF16), pltpu.VMEM((rows, d), BF16),
             pltpu.VMEM((layers * SMALL, d), F32), pltpu.VMEM((layers * SMALL, d), BF16),
             pltpu.VMEM((layers * SMALL, d), BF16),
+            dma(12), dma(3), dma(3), dma(6), dma(6),
             pltpu.VMEM((NS, 2, CHUNK, d), BF16), pltpu.VMEM((NS, CHUNK, d), BF16),
             pltpu.VMEM((NY, CHUNK // 2, d), BF16), pltpu.VMEM((NZ, CHUNK // 2, d), BF16),
             pltpu.VMEM((NZ, CHUNK // 2, d), BF16), pltpu.VMEM((NT, CHUNK // 2, d), BF16),
-            dma(12), dma(3), dma(3), dma(6), dma(6),
+            pltpu.VMEM((crosses, 2, CHUNK // 2, d), BF16), pltpu.VMEM((crosses, CHUNK // 2, d), BF16),
+            pltpu.VMEM((crosses, CHUNK // 4, d), BF16), pltpu.VMEM((crosses, CHUNK // 4, d), BF16),
+            pltpu.VMEM((crosses, CHUNK // 2, d), BF16),
             dma(units), dma(units), dma(units), dma(NY), dma(NT), dma(NZ), dma(NT), dma(NZ), dma(NT), dma(4),
+            dma(5, crosses), dma(5, crosses), dma(crosses),
         ]
         + [pltpu.SemaphoreType.REGULAR] * 5,
         compiler_params=pltpu.CompilerParams(

time: 507 us -> 472 us (0.931)
  Pallas kernels: 488 us -> 453 us
    pallas_call x1, Pallas kernels: 344 us -> 308 us  [run_bwd(): pl.pallas_call(functools.partial(bwd_kernel, seq), out_shape=[jax.ShapeDt...]
where the time goes in v5:
time: 472 us; the launch traced here: 463 us
  Pallas kernels  453 us (96%)
  local copies, waits for them, and re-layouts  9.31 us (2%)
    pallas_call x1, Pallas kernels, run_bwd(): pl.pallas_call(functools.partial(bwd_kernel, seq), out_shape=[jax.ShapeDt...  308 us
    pallas_call x1, Pallas kernels, run_fwd(): pl.pallas_call(functools.partial(fwd_kernel, seq), out_shape=[jax.ShapeDt...  130 us
    pallas_call x1, Pallas kernels, run_finish(): pl.pallas_call(finish_kernel, grid=(layers, steps), out_shape=[jax.ShapeD...  14 us

profile of v5, /device:TPU:0, one launch (start us, length us, event | category | flops | bytes accessed | tf_op | source)
XLA Modules:
  0.0 463.4 jit_solution(3677039549172590826)
XLA Ops:
  0.6 1.2 copy.30
  1.9 0.9 pad.7.tok_ref
  2.8 1.2 copy.31
  4.0 0.9 pad.8.cot_ref
  4.9 130.5 %forward.1 = (bf16[2,4,256,1536]{3,2,1,0:T(8,128)(2,1)}, bf16[2,2,256,1024]{3,2,1,0:T(8,128)(2,1)}, bf16[2,4,256,2048]{3,2,1,0:T(8,128)(2,1)}, bf16[2,2,1024,102...) custom-call(bf16[2,160,1024]{2,1,0:T(8,128)(2,1)} %pad.7.tok_ref, ...), custom_call_target="tpu_custom_call" | custom-call | flops 16999999488 | bytes 80000000 | tf_op jit(solution)/shard_map/forward/pallas_call | solution.py:507
  135.3 308.5 %backward.1 = (bf16[2,256,3072]{2,1,0:T(8,128)(2,1)}, bf16[2,256,1024]{2,1,0:T(8,128)(2,1)}, bf16[2,256,4096]{2,1,0:T(8,128)(2,1)}, bf16[2,1024,1024]{2,1,0:T(8,...) custom-call(bf16[640,1024]{1,0:T(8,128)(2,1)} %get-tuple-element.48.dm_ref, ...), custom_call_target="tpu_custom_call" | custom-call | flops 33999998976 | bytes 120000000 | tf_op jit(solution)/shard_map/backward/pallas_call | solution.py:1135
  443.8 1.1 slice.6
  445.0 1.4 copy.32
  446.4 1.1 slice.7
  447.5 1.4 copy.33
  448.9 14.0 %finish.1 = (f32[2,256,3072]{2,1,0:T(8,128)}, f32[2,256,1024]{2,1,0:T(8,128)}, f32[2,256,4096]{2,1,0:T(8,128)}, f32[2,1024,1024]{2,1,0:T(8,128)}, f32[2,256]{1,0...) custom-call(bf16[2,256,3072]{2,1,0:T(8,128)(2,1)} %get-tuple-element, ...), custom_call_target="tpu_custom_call" | custom-call | tf_op jit(solution)/shard_map/finish/pallas_call | solution.py:1192

commit v6 on v5

--- a/solution.py
+++ b/solution.py
@@ -16,7 +16,8 @@
 STEP = 16
 G1, B1, BOUT, G2, B2, BDOWN, BQV, BUP = 0, 1, 2, 3, 4, 5, 6, 8
 SMALL = 16
-WIDER = ("down",)
+PIECES = dict(qkv=2, out=1, up=2, down=2)
+WIDER = ((0, "down", 0), (0, "down", 1), (1, "down", 0))
 
 
 def nn(a, b):
@@ -150,9 +151,9 @@
 
 
 def fwd_kernel(
-    seq, tok_ref, cot_ref, g1_in, b1_in, bo_in, g2_in, b2_in, bd_in, bqv_in, bup_in, tv_ref, iv_ref, wqkv_in, wout_in, wup_in, wdown_in,
+    seq, tok_in, cot_in, g1_in, b1_in, bo_in, g2_in, b2_in, bd_in, bqv_in, bup_in, tv_ref, iv_ref, wqkv_in, wout_in, wup_in, wdown_in,
     vqkv, vout, vup, vdown, xs, x2s, h1s, qkvs, as_, h2s, zs, gps, dm_out, act_out, vec_out,
-    wqkv, wout, wup, wdown, x_ref, x2_ref, h1, qkv, att, h2, z, gp, put, got, tok, vec, bup, cot, dm, pack_ref,
+    wqkv, wout, wup, wdown, x_ref, x2_ref, h1, qkv, att, h2, z, gp, put, got, tok, vec, bup, cot, dm, pack_ref, tok_ref, cot_ref,
     s_rx, s_ry, s_rz, s_ra, s_rb, s_rs, s_loc, s_send, s_core, r_core, s_save, s_misc, r_misc,
 ):
     at = Place()
@@ -169,10 +170,17 @@
     runs = dict(qkv=(d // 4, 6), up=(f // 2, 2))
     plan = Plan()
     index = {}
+    piece_index = {}
     for l in range(layers):
         for kind in KINDS:
             index[l, kind] = len(index)
-
+            for p in range(PIECES[kind]):
+                piece_index[l, kind, p] = len(piece_index)
+
+    for src, dst in ((tok_in, tok_ref), (cot_in, cot_ref)):
+        for i in range(2):
+            dst[i, seq // STEP * STEP:, :] = jnp.zeros((block - seq // STEP * STEP, d), BF16)
+            dst[i, 0:seq, :] = src[:, i, :]
     at_row = 0
     for ref in (g1_in, b1_in, bo_in, g2_in, b2_in, bd_in, bqv_in, bup_in):
         values = ref[...].astype(F32)
@@ -194,16 +202,20 @@
     for copy in packs:
         copy.start()
 
-    def wider_parts(kind, y=at.y, zlow=at.zlow):
-        q = full[kind].shape[2] // 4
-        return span(y * q, q), span((2 + zlow) * q, q)
-
-    def launch(l, kind):
-        i = index[l, kind]
+    def quarter_rows(kind):
+        return full[kind].shape[2] // PIECES[kind] // 4
+
+    def part_of(kind, p, first, count=4, of=1):
+        q = quarter_rows(kind) // of
+        return span(4 * of * p * q + first * q, q) if count == 1 else pl.ds(4 * p * q, count * q)
+
+    def wider_parts(kind, p, y, zlow):
+        return part_of(kind, p, y, 1), part_of(kind, p, 2 + zlow, 1)
+
+    def launch(l, kind, p):
+        w, i = index[l, kind], piece_index[l, kind, p]
         src, dst = ins[kind].at[l], full[kind].at[l]
-        n = src.shape[0]
-        q = n // 4
-        part = span(quarter * q, q)
+        part = part_of(kind, p, quarter, 1)
         if kind in runs:
             width, count = runs[kind]
             mine = 2 * x + c
@@ -211,18 +223,16 @@
                 to = pl.ds(j * width, width)
                 keep = span((2 * j + c) * width, width)
                 give = span((2 * j + 1 - c) * width, width)
-                remote(src.at[part, keep], dst.at[mine, part, to], s_send.at[i], s_rx.at[i], at.xn).start()
-                remote(src.at[part, give], dst.at[mine, part, to], s_send.at[i], s_rx.at[i], at.xd).start()
-            for j in range(count):
-                to = pl.ds(j * width, width)
-                keep = span((2 * j + c) * width, width)
-                give = span((2 * j + 1 - c) * width, width)
-                remote(src.at[:, give], dst.at[mine, :, to], s_send.at[i], s_rs.at[i], at.sib).start()
-                pltpu.make_async_copy(src.at[:, keep], dst.at[mine, :, to], s_loc.at[i]).start()
+                remote(src.at[part, keep], dst.at[mine, part, to], s_send.at[w], s_rx.at[i], at.xn).start()
+                remote(src.at[part, give], dst.at[mine, part, to], s_send.at[w], s_rx.at[i], at.xd).start()
+                if p == 0:
+                    remote(src.at[:, give], dst.at[mine, :, to], s_send.at[w], s_rs.at[w], at.sib).start()
+                    pltpu.make_async_copy(src.at[:, keep], dst.at[mine, :, to], s_loc.at[w]).start()
         else:
-            for part in wider_parts(kind) if kind in WIDER else (part,):
-                remote(src.at[part], dst.at[x, part], s_send.at[i], s_rx.at[i], at.xn).start()
-            pltpu.make_async_copy(src, dst.at[x], s_loc.at[i]).start()
+            for part in wider_parts(kind, p, at.y, at.zlow) if (l, kind, p) in WIDER else (part,):
+                remote(src.at[part], dst.at[x, part], s_send.at[w], s_rx.at[i], at.xn).start()
+            if p == 0:
+                pltpu.make_async_copy(src, dst.at[x], s_loc.at[w]).start()
 
     def theirs(l, kind, part):
         dst = full[kind].at[l]
@@ -230,71 +240,82 @@
             return dst.at[span(2 * (1 - x), 2), part]
         return dst.at[pl.ds(1 - x, 1), part]
 
-    def part_of(kind, y, zlow, half=None):
-        q = full[kind].shape[2] // 4
-        if half is None:
-            return span((2 * y + zlow) * q, q)
-        return span((4 * y + 2 * zlow + half) * (q // 2), q // 2)
-
-    def relay1(l, kind):
-        i = index[l, kind]
-        if kind in WIDER:
-            settle(theirs(l, kind, pl.ds(0, full[kind].shape[2] // 2)), s_rx.at[i])
-            by_y, by_z = (theirs(l, kind, part) for part in wider_parts(kind))
-            remote(by_y, by_y, s_send.at[i], s_ry.at[i], at.yn).start()
-            remote(by_z, by_z, s_send.at[i], s_rz.at[i], at.zn).start()
-            return
-        piece = theirs(l, kind, part_of(kind, at.y, at.zlow))
-        settle(piece, s_rx.at[i])
-        remote(piece, piece, s_send.at[i], s_ry.at[i], at.yn).start()
-        remote(piece, piece, s_send.at[i], s_rz.at[i], at.zn).start()
-
-    def relay2(l, kind):
-        i = index[l, kind]
-        settle(theirs(l, kind, part_of(kind, 1 - at.y, at.zlow)), s_ry.at[i])
-        piece = theirs(l, kind, part_of(kind, 1 - at.y, at.zlow, 0))
-        remote(piece, piece, s_send.at[i], s_ra.at[i], at.zn).start()
-        settle(theirs(l, kind, part_of(kind, at.y, 1 - at.zlow)), s_rz.at[i])
-        piece = theirs(l, kind, part_of(kind, at.y, 1 - at.zlow, 1))
-        remote(piece, piece, s_send.at[i], s_rb.at[i], at.yn).start()
-
-    def ready(l, kind):
-        i = index[l, kind]
-        if kind in WIDER:
-            by_y, by_z = (theirs(l, kind, part) for part in wider_parts(kind, 1 - at.y, 1 - at.zlow))
+    link = dict(x=4.0, y=0.0, z=0.0)
+
+    def travel(name, us):
+        link[name] = max(plan.now, link[name]) + us
+        return link[name] + 2.5
+
+    def hop(kind):
+        shape = full[kind].shape
+        return 2 * shape[1] * shape[2] * shape[3] / 2**20 / PIECES[kind] / 4 / 0.094 * 1.05
+
+    def relay1(l, kind, p):
+        key = (l, kind, p)
+        w, i = index[l, kind], piece_index[key]
+        if key in WIDER:
+            settle(theirs(l, kind, part_of(kind, p, 0, 2)), s_rx.at[i])
+            to_y, to_z = (theirs(l, kind, part) for part in wider_parts(kind, p, at.y, at.zlow))
+        else:
+            to_y = to_z = theirs(l, kind, part_of(kind, p, quarter, 1))
+            settle(to_y, s_rx.at[i])
+        remote(to_y, to_y, s_send.at[w], s_ry.at[i], at.yn).start()
+        remote(to_z, to_z, s_send.at[w], s_rz.at[i], at.zn).start()
+        t = max(travel("y", hop(kind)), travel("z", hop(kind)))
+        if key in WIDER:
+            plan.add(t, ("ok", *key), functools.partial(arrived, *key))
+        else:
+            plan.add(t, ("r2", *key), functools.partial(relay2, *key))
+        plan.order()
+
+    def relay2(l, kind, p):
+        key = (l, kind, p)
+        w, i = index[l, kind], piece_index[key]
+        from_y, from_z = 2 * (1 - at.y) + at.zlow, 2 * at.y + 1 - at.zlow
+        settle(theirs(l, kind, part_of(kind, p, from_y, 1)), s_ry.at[i])
+        piece = theirs(l, kind, part_of(kind, p, 2 * from_y, 1, 2))
+        remote(piece, piece, s_send.at[w], s_ra.at[i], at.zn).start()
+        settle(theirs(l, kind, part_of(kind, p, from_z, 1)), s_rz.at[i])
+        piece = theirs(l, kind, part_of(kind, p, 2 * from_z + 1, 1, 2))
+        remote(piece, piece, s_send.at[w], s_rb.at[i], at.yn).start()
+        t = max(travel("y", hop(kind) / 2), travel("z", hop(kind) / 2))
+        plan.add(t, ("ok", *key), functools.partial(arrived, *key))
+        plan.order()
+
+    def arrived(l, kind, p):
+        key = (l, kind, p)
+        i = piece_index[key]
+        if key in WIDER:
+            by_y, by_z = (theirs(l, kind, part) for part in wider_parts(kind, p, 1 - at.y, 1 - at.zlow))
             settle(by_y, s_ry.at[i])
             settle(by_z, s_rz.at[i])
         else:
-            settle(theirs(l, kind, part_of(kind, 1 - at.y, 1 - at.zlow, 0)), s_ra.at[i])
-            settle(theirs(l, kind, part_of(kind, 1 - at.y, 1 - at.zlow, 1)), s_rb.at[i])
+            far = 2 * (1 - at.y) + 1 - at.zlow
+            settle(theirs(l, kind, part_of(kind, p, 2 * far, 1, 2)), s_ra.at[i])
+            settle(theirs(l, kind, part_of(kind, p, 2 * far + 1, 1, 2)), s_rb.at[i])
+
+    def have(l, kind):
+        for p in range(PIECES[kind]):
+            plan.need(("ok", l, kind, p))
+        w = index[l, kind]
         if kind in runs:
-            settle(full[kind].at[l, 0], s_rs.at[i])
-        settle(full[kind].at[l, 0], s_loc.at[i])
-        pltpu.make_async_copy(full[kind].at[l], saves[kind].at[l], s_loc.at[i]).start()
-
-    line = list(index)
+            settle(full[kind].at[l, 0], s_rs.at[w])
+        settle(full[kind].at[l, 0], s_loc.at[w])
+        pltpu.make_async_copy(full[kind].at[l], saves[kind].at[l], s_loc.at[w]).start()
+
     tokens = [
         remote(tok_ref.at[1 - x], tok.at[1], s_misc.at[0], r_misc.at[0], at.xn),
         pltpu.make_async_copy(tok_ref.at[x], tok.at[0], s_misc.at[3]),
     ]
-    x_time, yz_time = 4.0, 0.0
-    for n, (l, kind) in enumerate(line):
-        if n == 2:
+    for key in piece_index:
+        if key[:2] == (0, "up") and key[2] == 0:
             for copy in tokens:
                 copy.start()
-            x_time += 7.3
-        launch(l, kind)
-        mb = 2 * full[kind].shape[1] * full[kind].shape[2] * full[kind].shape[3] / 2**20
-        hop = mb / 4 / 0.094 * 1.05
-        x_time += 2 * hop if kind in WIDER else hop
-        plan.add(x_time + 1, ("r1", l, kind), functools.partial(relay1, l, kind))
-        yz_time = max(yz_time, x_time + 1.5)
-        if kind in WIDER:
-            yz_time += hop
-        else:
-            plan.add(yz_time + hop + 1.5, ("r2", l, kind), functools.partial(relay2, l, kind))
-            yz_time += 1.5 * hop
-        plan.add(yz_time + 3, ("ok", l, kind), functools.partial(ready, l, kind))
+            token_time = travel("x", 7.3)
+        launch(*key)
+        t = travel("x", hop(key[1]) * (2 if key in WIDER else 1))
+        plan.add(t, ("r1", *key), functools.partial(relay1, *key))
+    x_time = travel("x", 7.3)
     late = [
         remote(cot_ref.at[1 - x], cot.at[1], s_misc.at[1], r_misc.at[1], at.xn),
         pltpu.make_async_copy(cot_ref.at[x], cot.at[0], s_misc.at[8]),
@@ -325,8 +346,8 @@
         copy.start()
         saved.append(copy)
 
-    plan.add(x_time + 9, "seed", seed)
-    plan.add(x_time + 14, "seeded", seeded)
+    plan.add(x_time, "seed", seed)
+    plan.add(x_time + 5, "seeded", seeded)
     plan.order()
 
     for copy in packs:
@@ -339,7 +360,7 @@
             bup[l:l + 1, pl.ds(j * WIDE, WIDE)] = vec[
                 l * SMALL + BUP + sub:l * SMALL + BUP + sub + 1, span((2 * half + c) * WIDE, WIDE)
             ]
-    plan.now = 18.0
+    plan.now = token_time
     plan.poll()
     for copy in tokens:
         copy.wait()
@@ -373,7 +394,7 @@
         cp.start()
         x_saved = save(x_ref, xs.at[l], 0)
         plan.spend(2)
-        plan.need(("ok", l, "qkv"))
+        have(l, "qkv")
         if l:
             pending["qkv"].wait()
         bq = jnp.where(c == 0, row(BQV), vec[l * SMALL + BQV + 1:l * SMALL + BQV + 2, :])
@@ -430,7 +451,7 @@
             out[...] += got[slot].astype(F32)
             plan.spend(1)
 
-        plan.need(("ok", l, "out"))
+        have(l, "out")
         if l:
             pending["x2"].wait()
         exchange(att, "out", x_ref, BOUT, x2_ref, 0)
@@ -439,7 +460,7 @@
         cp = remote(h2.at[own], h2.at[other], s_core.at[2], r_core.at[2], at.sib)
         cp.start()
         plan.spend(2)
-        plan.need(("ok", l, "up"))
+        have(l, "up")
         if l:
             pending["z"].wait()
             pending["gp"].wait()
@@ -461,7 +482,7 @@
         h2_saved = save(h2, h2s.at[l], 5)
         pending["z"] = save(z, zs.at[l], 6)
         pending["gp"] = save(gp, gps.at[l], 7)
-        plan.need(("ok", l, "down"))
+        have(l, "down")
         for copy in (x_saved, h1_saved, h2_saved):
             copy.wait()
         exchange(z, "down", x2_ref, BDOWN, x_ref, 1)
@@ -494,7 +515,7 @@
     layers, n, d3 = w_qkv.shape
     d = d3 // 3
     hc, f = d // 2, 2 * w_down.shape[1]
-    block = tok.shape[1]
+    block = -(-seq // 32) * 32
     rows, both = 2 * block, 4 * block
     weights = [(4, n, 3 * hc), (2, n, d), (4, n, f), (2, w_down.shape[1], d)]
     acts = [
@@ -503,11 +524,11 @@
     ]
     shapes = [((layers, *s), BF16) for s in weights] + [((layers, *s), t) for s, t in acts]
     shapes += [((both, d), BF16), ((2, block, d), BF16), ((layers * SMALL, d), F32)]
-    count = layers * len(KINDS)
+    count, pieces = layers * len(KINDS), layers * sum(PIECES.values())
     return pl.pallas_call(
         functools.partial(fwd_kernel, seq),
         out_shape=[jax.ShapeDtypeStruct(s, t) for s, t in shapes],
-        in_specs=[ANY, ANY] + [VM] * 10 + [ANY] * 4,
+        in_specs=[VM] * 12 + [ANY] * 4,
         out_specs=[ANY] * len(shapes),
         scratch_shapes=[pltpu.VMEM((layers, *s), BF16) for s in weights]
         + [pltpu.VMEM(s, t) for s, t in acts]
@@ -515,8 +536,10 @@
             pltpu.VMEM((rows, d), BF16), pltpu.VMEM((2, rows, d), BF16),
             pltpu.VMEM((2, block, d), BF16), pltpu.VMEM((layers * SMALL, d), F32), pltpu.VMEM((8, f), F32),
             pltpu.VMEM((2, block, d), BF16), pltpu.VMEM((both, d), BF16), pltpu.VMEM((layers * SMALL, WIDE), F32),
+            pltpu.VMEM((2, block, d), BF16), pltpu.VMEM((2, block, d), BF16),
         ]
-        + [dma(count)] * 8
+        + [dma(pieces)] * 5
+        + [dma(count)] * 3
         + [dma(3), dma(3), dma(8), dma(12), dma(8)],
         compiler_params=pltpu.CompilerParams(
             collective_id=1, has_side_effects=True, vmem_limit_bytes=VMEM_LIMIT
@@ -1163,7 +1186,14 @@
     )(*args)
 
 
-def finish_kernel(gqkv, gout, gup, gdown, small, oqkv, oout, oup, odown, *vectors):
+def finish_kernel(gqkv, gout, gup, gdown, small, act, gtok, oact, ogtok, oqkv, oout, oup, odown, *vectors):
+    seq = oact.shape[0]
+
+    @pl.when(jnp.logical_and(pl.program_id(0) == 0, pl.program_id(1) == 0))
+    def _():
+        for src, dst in ((act, oact), (gtok, ogtok)):
+            dst[...] = jnp.stack([src[0, :seq, :], src[1, :seq, :]], axis=1)
+
     for src, dst in ((gqkv, oqkv), (gout, oout), (gup, oup), (gdown, odown)):
         dst[...] = src[...].astype(F32)
     mine = span(lax.axis_index("grp") * WIDE, WIDE)
@@ -1177,28 +1207,30 @@
             at += 1
 
 
-def run_finish(gqkv, gout, gup, gdown, small, widths):
+def run_finish(gqkv, gout, gup, gdown, small, act, gtok, seq, widths):
     bigs = (gqkv, gout, gup, gdown)
     layers = gqkv.shape[0]
-    steps = 4
+    steps = 2
 
     def big(g):
         return pl.BlockSpec((1, g.shape[1] // steps, g.shape[2]), lambda l, s: (l, s, 0))
 
     def flat(shape):
-        return pl.BlockSpec(shape, lambda l, s: (0, 0))
-
+        return pl.BlockSpec(shape, lambda l, s: (0,) * len(shape))
+
+    rows = [(seq, act.shape[0], act.shape[2])] * 2
     vectors = [(layers, w) for w in widths]
     return pl.pallas_call(
         finish_kernel,
         grid=(layers, steps),
-        out_shape=[jax.ShapeDtypeStruct(g.shape, F32) for g in bigs]
+        out_shape=[jax.ShapeDtypeStruct(r, BF16) for r in rows]
+        + [jax.ShapeDtypeStruct(g.shape, F32) for g in bigs]
         + [jax.ShapeDtypeStruct(v, F32) for v in vectors],
-        in_specs=[big(g) for g in bigs] + [flat(small.shape)],
-        out_specs=[big(g) for g in bigs] + [flat(v) for v in vectors],
+        in_specs=[big(g) for g in bigs] + [flat(small.shape), flat(act.shape), flat(gtok.shape)],
+        out_specs=[flat(r) for r in rows] + [big(g) for g in bigs] + [flat(v) for v in vectors],
         compiler_params=pltpu.CompilerParams(vmem_limit_bytes=VMEM_LIMIT),
         name="finish",
-    )(*bigs, small)
+    )(*bigs, small, act, gtok)
 
 
 def local(
@@ -1206,14 +1238,9 @@
     norm1_gain, norm1_bias, w_qkv, b_qv, w_out, b_out, norm2_gain, norm2_bias, w_up, b_up, w_down, b_down,
 ):
     seq = tokens.shape[1]
-    block = -(-seq // 32) * 32
-
-    def pad(value):
-        return jnp.pad(value, ((0, 0), (0, block - seq), (0, 0)))
-
     smalls = (norm1_gain, norm1_bias, b_out, norm2_gain, norm2_bias, b_down, b_qv, b_up)
     res = run_fwd(
-        pad(tokens), pad(cotangent), smalls, token_valid, image_valid[None, :], w_qkv, w_out, w_up, w_down, seq
+        tokens.transpose(1, 0, 2), cotangent.transpose(1, 0, 2), smalls, token_valid, image_valid[None, :], w_qkv, w_out, w_up, w_down, seq
     )
     weights, acts, (dm, act, vec) = res[:4], res[4:12], res[12:]
     gqkv, gout, gup, gdown, gsmall, gtok, act = run_bwd(dm, act, vec, token_valid, weights, acts, seq)
@@ -1223,10 +1250,13 @@
         gqkv, gout, gup, gdown, gsmall = (
             lax.psum(g, "rep", axis_index_groups=groups) for g in (gqkv, gout, gup, gdown, gsmall)
         )
-    gqkv, gout, gup, gdown, *vectors = run_finish(gqkv, gout, gup, gdown, gsmall, [w.shape[1] for w in smalls])
+    act, gtok, gqkv, gout, gup, gdown, *vectors = run_finish(
+        gqkv, gout, gup, gdown, gsmall, act, gtok, seq, [w.shape[1] for w in smalls]
+    )
+    act, gtok = act.transpose(1, 0, 2), gtok.transpose(1, 0, 2)
     gg1, gb1, gbout, gg2, gb2, gbdown, gbqv, gbup = vectors
     return (
-        act[:, :seq], gtok[:, :seq], gg1, gb1, gqkv, gbqv, gout, gbout, gg2, gb2, gup, gbup, gdown, gbdown,
+        act, gtok, gg1, gb1, gqkv, gbqv, gout, gbout, gg2, gb2, gup, gbup, gdown, gbdown,
     )
 
 

time: 472 us -> 459 us (0.972); the launches traced: 463 us -> 457 us
  local copies, waits for them, and re-layouts: 9.31 us -> 0 us
    unnamed x4 -> x0, local copies, waits for them, and re-layouts: 5.27 us -> none
where the time goes in v6:
time: 459 us; the launch traced here: 457 us
  Pallas kernels  455 us (99%)
    pallas_call x1, Pallas kernels, run_bwd(): pl.pallas_call(functools.partial(bwd_kernel, seq), out_shape=[jax.ShapeDt...  309 us
    pallas_call x1, Pallas kernels, run_fwd(): pl.pallas_call(functools.partial(fwd_kernel, seq), out_shape=[jax.ShapeDt...  132 us
    pallas_call x1, Pallas kernels, run_finish(): pl.pallas_call(finish_kernel, grid=(layers, steps), out_shape=[jax.ShapeD...  15.1 us

profile of v6, /device:TPU:0, one launch (start us, length us, event | category | flops | bytes accessed | tf_op | source)
XLA Modules:
  0.0 456.5 jit_solution(17404365990793965839)
XLA Ops:
  0.7 131.6 %forward.1 = (bf16[2,4,256,1536]{3,2,1,0:T(8,128)(2,1)}, bf16[2,2,256,1024]{3,2,1,0:T(8,128)(2,1)}, bf16[2,4,256,2048]{3,2,1,0:T(8,128)(2,1)}, bf16[2,2,1024,102...) custom-call(bf16[145,2,1024]{2,1,0:T(2,128)(2,1)} %bitcast.5, ...), custom_call_target="tpu_custom_call" | custom-call | flops 16999999488 | bytes 80000000 | tf_op jit(solution)/shard_map/forward/pallas_call | solution.py:528
  132.3 308.7 %backward.1 = (bf16[2,256,3072]{2,1,0:T(8,128)(2,1)}, bf16[2,256,1024]{2,1,0:T(8,128)(2,1)}, bf16[2,256,4096]{2,1,0:T(8,128)(2,1)}, bf16[2,1024,1024]{2,1,0:T(8,...) custom-call(bf16[640,1024]{1,0:T(8,128)(2,1)} %get-tuple-element.50.dm_ref, ...), custom_call_target="tpu_custom_call" | custom-call | flops 33999998976 | bytes 120000000 | tf_op jit(solution)/shard_map/backward/pallas_call | solution.py:1158
  441.0 15.1 %finish.1 = (bf16[145,2,1024]{2,1,0:T(2,128)(2,1)}, bf16[145,2,1024]{2,1,0:T(2,128)(2,1)}, f32[2,256,3072]{2,1,0:T(8,128)}, f32[2,256,1024]{2,1,0:T(8,128)}, f32...) custom-call(bf16[2,256,3072]{2,1,0:T(8,128)(2,1)} %get-tuple-element, ...), custom_call_target="tpu_custom_call" | custom-call | tf_op jit(solution)/shard_map/finish/pallas_call | solution.py:1223

commit v7 on v6

--- a/solution.py
+++ b/solution.py
@@ -177,10 +177,11 @@
             for p in range(PIECES[kind]):
                 piece_index[l, kind, p] = len(piece_index)
 
-    for src, dst in ((tok_in, tok_ref), (cot_in, cot_ref)):
+    def stage(src, dst):
         for i in range(2):
             dst[i, seq // STEP * STEP:, :] = jnp.zeros((block - seq // STEP * STEP, d), BF16)
             dst[i, 0:seq, :] = src[:, i, :]
+
     at_row = 0
     for ref in (g1_in, b1_in, bo_in, g2_in, b2_in, bd_in, bqv_in, bup_in):
         values = ref[...].astype(F32)
@@ -309,6 +310,7 @@
     ]
     for key in piece_index:
         if key[:2] == (0, "up") and key[2] == 0:
+            stage(tok_in, tok_ref)
             for copy in tokens:
                 copy.start()
             token_time = travel("x", 7.3)
@@ -320,6 +322,7 @@
         remote(cot_ref.at[1 - x], cot.at[1], s_misc.at[1], r_misc.at[1], at.xn),
         pltpu.make_async_copy(cot_ref.at[x], cot.at[0], s_misc.at[8]),
     ]
+    stage(cot_in, cot_ref)
     for copy in late:
         copy.start()
     mask = chip_flags(at, tv_ref, rows, seq)

time: 459 us -> 462 us (level); the launches traced: 457 us -> 453 us
  no operation moved by 1% of the time
where the time goes in v7:
time: 462 us; the launch traced here: 453 us
  Pallas kernels  452 us (98%)
    pallas_call x1, Pallas kernels, run_bwd(): pl.pallas_call(functools.partial(bwd_kernel, seq), out_shape=[jax.ShapeDt...  309 us
    pallas_call x1, Pallas kernels, run_fwd(): pl.pallas_call(functools.partial(fwd_kernel, seq), out_shape=[jax.ShapeDt...  128 us
    pallas_call x1, Pallas kernels, run_finish(): pl.pallas_call(finish_kernel, grid=(layers, steps), out_shape=[jax.ShapeD...  15.1 us

profile of v7, /device:TPU:0, one launch (start us, length us, event | category | flops | bytes accessed | tf_op | source)
XLA Modules:
  0.0 453.2 jit_solution(10019596036817836451)
XLA Ops:
  0.7 128.1 %forward.1 = (bf16[2,4,256,1536]{3,2,1,0:T(8,128)(2,1)}, bf16[2,2,256,1024]{3,2,1,0:T(8,128)(2,1)}, bf16[2,4,256,2048]{3,2,1,0:T(8,128)(2,1)}, bf16[2,2,1024,102...) custom-call(bf16[145,2,1024]{2,1,0:T(2,128)(2,1)} %bitcast.5, ...), custom_call_target="tpu_custom_call" | custom-call | flops 16999999488 | bytes 80000000 | tf_op jit(solution)/shard_map/forward/pallas_call | solution.py:531
  128.8 309.1 %backward.1 = (bf16[2,256,3072]{2,1,0:T(8,128)(2,1)}, bf16[2,256,1024]{2,1,0:T(8,128)(2,1)}, bf16[2,256,4096]{2,1,0:T(8,128)(2,1)}, bf16[2,1024,1024]{2,1,0:T(8,...) custom-call(bf16[640,1024]{1,0:T(8,128)(2,1)} %get-tuple-element.50.dm_ref, ...), custom_call_target="tpu_custom_call" | custom-call | flops 33999998976 | bytes 120000000 | tf_op jit(solution)/shard_map/backward/pallas_call | solution.py:1161
  437.9 15.1 %finish.1 = (bf16[145,2,1024]{2,1,0:T(2,128)(2,1)}, bf16[145,2,1024]{2,1,0:T(2,128)(2,1)}, f32[2,256,3072]{2,1,0:T(8,128)}, f32[2,256,1024]{2,1,0:T(8,128)}, f32...) custom-call(bf16[2,256,3072]{2,1,0:T(8,128)(2,1)} %get-tuple-element, ...), custom_call_target="tpu_custom_call" | custom-call | tf_op jit(solution)/shard_map/finish/pallas_call | solution.py:1226
